TPU v7x, 32 devices: a whole 2x2x4 slice. The times are simulated.
32 devices in a mesh: dp: 8 (over y, x, core), type: 4 (over z).
Axes of the slice: x: 2, y: 2, z: 4, core: 2. Of those that a mesh axis runs over, the one named last changes fastest.
Arguments:
- tokens: bfloat16 [4096, 4096], P(('dp', 'type')), may hold values from -6 to 6
- token_types: int32 [4096, 1], P(('dp', 'type')), may hold values from 0 to 3
- tile_mask: int32 [8, 4, 4], P('dp', 'type'), may hold values from 0 to 1, as said below
- queries: bfloat16 [4096, 4096], P(('dp', 'type')), may hold values from -60 to 60
- keys: bfloat16 [4096, 4096], P(('dp', 'type')), may hold values from -4 to 4
- gate_weight: bfloat16 [4, 4096, 7168], P('type', None, 'dp'), may hold values from -0.09375 to 0.09375
- up_weight: bfloat16 [4, 4096, 7168], P('type', None, 'dp'), may hold values from -0.09375 to 0.09375
- down_weight: bfloat16 [4, 7168, 4096], P('type', 'dp'), may hold values from -0.0625 to 0.0625
Outputs:
- expert_out: bfloat16 [4096, 4096], P(('dp', 'type'))
- attended: bfloat16 [4096, 4096], P(('dp', 'type'))
Inputs may be any that keep to these rules, and one draw needn't show every extreme that they name: `tile_mask`: every diagonal entry is 1.
All inputs are finite; a program needn't handle non-finite values.
Results may differ from a plain program's by a relative error of at most 0.02.
Values may be sent and summed in bfloat16 or wider, within the bound.
No kernel may reach another device: no remote copies, remote signals or barrier semaphores. Data moves between devices by JAX's collectives and lax.ppermute only.
A program may use at most 128 MiB of HBM per device.

v0:
```python
import math

import jax
import jax.numpy as jnp
from jax import lax
from jax.sharding import PartitionSpec as P

HEAD = 128
EXP_CAP = 16


def on_device(tokens, token_types, tile_mask, queries, keys, gate_weight, up_weight, down_weight):
    n_type = lax.axis_size("type")
    my_index = lax.axis_index("type")
    tok_rows = tokens.shape[0]
    feat_width = tokens.shape[1]
    type_ids = jnp.arange(n_type, dtype=jnp.int32)
    slot_ids = jnp.arange(EXP_CAP, dtype=jnp.int32)
    own_types = token_types[:, 0]
    event_types = lax.all_gather(own_types, "type", axis=0, tiled=True)
    source_counts = jnp.sum(
        (event_types.reshape(n_type, tok_rows)[:, :, None] == type_ids[None, None, :]).astype(
            jnp.int32
        ),
        axis=1,
    )
    earlier = (type_ids < my_index).astype(jnp.int32)
    before_mine = jnp.sum(source_counts * earlier[:, None], axis=0)
    own_hot = (own_types[:, None] == type_ids[None, :]).astype(jnp.int32)
    own_rank = jnp.sum((jnp.cumsum(own_hot, axis=0) - own_hot) * own_hot, axis=1)
    own_event_rank = own_rank + jnp.sum(own_hot * before_mine[None, :], axis=1)
    kept = own_event_rank < EXP_CAP
    select = (
        (own_types[None, None, :] == type_ids[:, None, None])
        & (own_rank[None, None, :] == slot_ids[None, :, None])
        & kept[None, None, :]
    ).astype(jnp.bfloat16)
    outgoing = jnp.einsum("ejt,td->ejd", select, tokens, preferred_element_type=jnp.float32).astype(
        jnp.bfloat16
    )
    incoming = lax.all_to_all(outgoing, "type", split_axis=0, concat_axis=0, tiled=True)
    mine_flags = (event_types == my_index).astype(jnp.int32).reshape(n_type, tok_rows)
    counts = jnp.sum(mine_flags, axis=1)
    offsets = jnp.cumsum(counts) - counts
    compact = (
        (offsets[None, :, None] + slot_ids[None, None, :] == slot_ids[:, None, None])
        & (slot_ids[None, None, :] < counts[None, :, None])
    ).astype(jnp.bfloat16)
    packed = jnp.einsum(
        "psj,sjd->pd", compact, incoming, preferred_element_type=jnp.float32
    ).astype(jnp.bfloat16)
    gate_local = gate_weight[0]
    up_local = up_weight[0]
    down_local = down_weight[0]
    block_rows = lax.all_gather(packed, "dp", axis=0, tiled=True)
    gate_act = jnp.dot(block_rows, gate_local, preferred_element_type=jnp.float32)
    up_act = jnp.dot(block_rows, up_local, preferred_element_type=jnp.float32)
    hidden = (jax.nn.silu(gate_act) * up_act).astype(jnp.bfloat16)
    partial_terms = jnp.dot(hidden, down_local, preferred_element_type=jnp.float32)
    summed = lax.psum_scatter(
        partial_terms.astype(jnp.bfloat16), "dp", scatter_dimension=0, tiled=True
    )
    back_rows = jnp.einsum(
        "psj,pd->sjd", compact, summed, preferred_element_type=jnp.float32
    ).astype(jnp.bfloat16)
    returned = lax.all_to_all(back_rows, "type", split_axis=0, concat_axis=0, tiled=True)
    expert_out = jnp.einsum(
        "ejt,ejd->td", select, returned, preferred_element_type=jnp.float32
    ).astype(jnp.bfloat16)
    keys_all, values = (
        lax.all_gather(keys, "type", axis=0, tiled=True),
        lax.all_gather(expert_out, "type", axis=0, tiled=True),
    )
    mask_row = tile_mask[0, 0]
    key_tile = jnp.arange(n_type * tok_rows, dtype=jnp.int32) // tok_rows
    allowed = (
        jnp.sum(
            (key_tile[:, None] == type_ids[None, :]).astype(jnp.int32) * mask_row[None, :], axis=1
        )
        == 1
    )
    head_count = feat_width // HEAD
    query_heads = queries.reshape(tok_rows, head_count, HEAD)
    key_heads = keys_all.reshape(-1, head_count, HEAD)
    value_heads = values.reshape(-1, head_count, HEAD)
    scores = jnp.einsum(
        "qhd,khd->hqk", query_heads, key_heads, preferred_element_type=jnp.float32
    ) * (1.0 / math.sqrt(HEAD))
    masked = jnp.where(allowed[None, None, :], scores, -jnp.inf)
    row_max = jnp.max(masked, axis=-1, keepdims=True)
    weights = jnp.where(allowed[None, None, :], jnp.exp(masked - row_max), 0.0).astype(jnp.bfloat16)
    total_weight = jnp.sum(weights.astype(jnp.float32), axis=-1)
    attended = (
        jnp.einsum("hqk,khd->qhd", weights, value_heads, preferred_element_type=jnp.float32)
        / jnp.transpose(total_weight)[:, :, None]
    )
    return (expert_out, attended.reshape(tok_rows, feat_width).astype(jnp.bfloat16))


def solution(mesh):
    return jax.shard_map(
        on_device,
        mesh=mesh,
        in_specs=(
            P(("dp", "type"), None),
            P(("dp", "type"), None),
            P("dp", "type", None),
            P(("dp", "type"), None),
            P(("dp", "type"), None),
            P("type", None, "dp"),
            P("type", None, "dp"),
            P("type", "dp", None),
        ),
        out_specs=(P(("dp", "type"), None), P(("dp", "type"), None)),
        check_vma=False,
    )
```

profile of v0, /device:TPU:0, one launch (start us, length us, event | category | flops | bytes accessed | tf_op | source)
XLA Modules:
  0.0 276.8 jit_solution(3107706197990176891)
XLA Ops:
  8.0 0.0 copy-start
  8.0 12.8 %all-gather = s32[512,1]{0,1:T(1,128)S(1)} all-gather(s32[128,1]{0,1:T(1,128)} %param.9), channel_id=2, replica_groups=mesh['dp'=8,'type'=4] {'type'}, dimensions={0}, use_global_device_ids=true | all-gather | bytes 2560 | tf_op jit(solution)/shard_map/all_gather | solution.py:20
  20.9 0.7 iota_compare_fusion.6
  21.5 0.7 fusion.36
  22.3 0.1 convert_reduce_fusion.1
  22.4 0.1 multiply_reduce_fusion
  22.5 0.2 reduce_window_sum.18
  22.7 0.8 select_reduce_fusion
  23.6 2.3 convolution_convert_fusion.1
  25.9 3.5 %all-to-all-start = ((bf16[4,16,4096]{2,1,0:T(8,128)(2,1)}), bf16[4,16,4096]{2,1,0:T(8,128)(2,1)S(1)}, u32[]{:S(2)}, u32[]{:S(2)}) async-start(bf16[4,16,4096]{2,1,0:T(8,128)(2,1)} %convolution_convert_fusion.1), calls=%async_computation | async-start | bytes 1048576 | tf_op jit(solution)/shard_map/all_to_all | solution.py:41
  29.3 0.0 all-gather.5.cloned.1.call-start
  29.4 0.1 reduce_sum.67
  29.5 0.2 reduce-window.8
  29.7 0.1 iota_compare_fusion.5
  29.8 0.1 iota_add_fusion
  29.9 12.2 %all-to-all-done = bf16[4,16,4096]{2,1,0:T(8,128)(2,1)S(1)} async-done(((bf16[4,16,4096]{2,1,0:T(8,128)(2,1)}), bf16[4,16,4096]{2,1,0:T(8,128)(2,1)S(1)}, u32[]{:S(2)}, u32[]{:S(2)}) %all-to-all-start) | async-done | bytes 524320 | tf_op jit(solution)/shard_map/all_to_all | solution.py:41
  42.1 1.0 fusion.12
  43.0 0.0 all-gather.5.cloned.1.call-update
  43.1 0.0 reduce-scatter.2.cloned.1.call-start
  43.1 22.7 %all-gather.5.cloned.1.call-done = bf16[128,4096]{1,0:T(8,128)(2,1)} async-done(((bf16[16,4096]{1,0:T(8,128)(2,1)}), bf16[128,4096]{1,0:T(8,128)(2,1)}) %all-gather.5.cloned.1.call-update) | async-done | bytes 1048592 | tf_op jit(solution)/shard_map/all_gather | solution.py:55
  65.8 0.0 copy-start.1
  65.8 4.7 %fusion.5 = f32[128,896]{1,0:T(8,128)S(1)} fusion(bf16[128,4096]{1,0:T(8,128)(2,1)} %all-gather.5.cloned.1.call-done, bf16[1,4096,896]{2,1,0:T(8,128)(2,1)} %param.13), kind=kOutput, calls=%fused_computation.8 | convolution fusion | flops 939524096 | bytes 8847360 | tf_op jit(solution)/shard_map/dot_general | solution.py:56
  70.6 0.0 copy-done.1
  70.6 8.6 %fusion.9 = bf16[128,4096]{1,0:T(8,128)(2,1)} fusion(bf16[1,896,4096]{2,1,0:T(8,128)(2,1)} %param.15, bf16[128,4096]{1,0:T(8,128)(2,1)S(1)} %copy-done.1, bf16[1,4096,896]{2,1,0:T(8,128)(2,1)} %param.14, f32[128,896]{1,0:T(8,128)S(1)} %fusion.5), kind=kOutput, calls=%fused_computation.13 | convolution fusion | flops 1880260608 | bytes 17235968 | tf_op jit(solution)/shard_map/dot_general | solution.py:59
  79.2 0.0 copy-start.2
  79.2 0.0 reduce-scatter.2.cloned.1.call-update
  79.2 0.0 all-gather.9.cloned.1.call-start
  79.2 2.3 copy.19
  81.6 0.0 all-gather.9.cloned.1.call-update
  81.6 0.0 all-gather.7.cloned.1.call-start
  81.7 33.7 %reduce-scatter.2.cloned.1.call-done = bf16[16,4096]{1,0:T(8,128)(2,1)} async-done(((bf16[128,4096]{1,0:T(8,128)(2,1)}), bf16[16,4096]{1,0:T(8,128)(2,1)}) %reduce-scatter.2.cloned.1.call-update) | async-done | bytes 131088 | tf_op jit(solution)/shard_map/reduce_scatter | solution.py:60
  115.3 1.2 convolution_convert_fusion
  116.6 28.5 %all_to_all.10 = bf16[4,16,4096]{2,1,0:T(8,128)(2,1)S(1)} all-to-all(bf16[4,16,4096]{2,1,0:T(8,128)(2,1)S(1)} %convolution_convert_fusion), channel_id=1, replica_groups=mesh['dp'=8,'type'=4] {'type'}, dimensions={0} | all-to-all | bytes 1048576 | tf_op jit(solution)/shard_map/all_to_all | solution.py:66
  145.1 1.5 fusion.8
  146.5 0.0 all-gather.7.cloned.1.call-update
  146.6 0.0 copy-done.2
  146.6 0.1 select_reduce_fusion.2
  146.7 27.3 %all-gather.9.cloned.1.call-done = bf16[512,4096]{0,1:T(8,128)(2,1)} async-done(((bf16[128,4096]{0,1:T(8,128)(2,1)}), bf16[512,4096]{0,1:T(8,128)(2,1)}) %all-gather.9.cloned.1.call-update) | async-done | bytes 4194320 | tf_op jit(solution)/shard_map/all_gather | solution.py:71
  174.0 0.0 copy-done
  174.0 3.4 %fusion.23 = f32[32,128,512]{2,1,0:T(8,128)S(1)} fusion(bf16[512,32,128]{0,2,1:T(8,128)(2,1)} %bitcast.60, bf16[128,4096]{1,0:T(8,128)(2,1)S(1)} %copy-done), kind=kOutput, calls=%fused_computation.25 | convolution fusion | flops 536870912 | bytes 13631488 | tf_op jit(solution)/shard_map/qhd,khd->hqk/dot_general | solution.py:86
  177.4 4.3 %convert_reduce_fusion = (f32[32,128]{1,0:T(8,128)S(1)}, bf16[32,128,512]{2,1,0:T(8,128)(2,1)}) fusion(f32[32,128,512]{2,1,0:T(8,128)S(1)} %fusion.23, pred[512]{0:T(512)(128)(4,1)S(1)} %broadcast_compare_fusion), kind=kOutput, calls=%fused_computation.1 | output fusion | flops 18874880 | bytes 12599808 | tf_op jit(solution)/shard_map/sub | solution.py:91
  181.7 75.1 %all-gather.7.cloned.1.call-done = bf16[512,4096]{1,0:T(8,128)(2,1)} async-done(((bf16[128,4096]{1,0:T(8,128)(2,1)}), bf16[512,4096]{1,0:T(8,128)(2,1)}) %all-gather.7.cloned.1.call-update) | async-done | bytes 4194320 | tf_op jit(solution)/shard_map/all_gather | solution.py:72
  256.8 6.5 %copy.26 = bf16[512,4096]{0,1:T(8,128)(2,1)} copy(bf16[512,4096]{1,0:T(8,128)(2,1)} %all-gather.7.cloned.1.call-done) | data formatting | bytes 8388608 | tf_op jit(solution)/shard_map/reshape | solution.py:85
  263.3 4.7 %fusion.16 = bf16[128,32,128]{0,2,1:T(8,128)(2,1)S(1)} fusion(bf16[512,32,128]{0,2,1:T(8,128)(2,1)} %bitcast.61, bf16[32,128,512]{2,1,0:T(8,128)(2,1)} %get-tuple-element.11, f32[128,32]{0,1:T(8,128)S(1)} %bitcast.70), kind=kOutput, calls=%fused_computation.22 | convolution fusion | flops 537919488 | bytes 9453568 | tf_op jit(solution)/shard_map/hqk,khd->qhd/dot_general | solution.py:94
  268.0 1.3 copy.23
  (7 shorter events, 0.0 us)
Async XLA Ops:
  8.0 166.0 %copy-start = (bf16[128,4096]{1,0:T(8,128)(2,1)S(1)}, bf16[128,4096]{1,0:T(8,128)(2,1)}, u32[]{:S(2)}) copy-start(bf16[128,4096]{1,0:T(8,128)(2,1)} %param.11) | copy-start | bytes 3145732
  25.9 16.2 %all-to-all-start = ((bf16[4,16,4096]{2,1,0:T(8,128)(2,1)}), bf16[4,16,4096]{2,1,0:T(8,128)(2,1)S(1)}, u32[]{:S(2)}, u32[]{:S(2)}) async-start(bf16[4,16,4096]{2,1,0:T(8,128)(2,1)} %convolution_convert_fusion.1), calls=%async_computation | async-start | bytes 1048576 | tf_op jit(solution)/shard_map/all_to_all | solution.py:41
  29.3 36.5 %all-gather.5.cloned.1.call-start = ((), (), s32[]{:S(2)}) async-start(), calls=%async_computation.3 | async-start | bytes 1179648 | tf_op jit(solution)/shard_map/all_gather | solution.py:55
  43.1 72.3 %reduce-scatter.2.cloned.1.call-start = ((), (), s32[]{:S(2)}) async-start(), calls=%async_computation.4 | async-start | bytes 1179648 | tf_op jit(solution)/shard_map/reduce_scatter | solution.py:60
  65.8 4.8 %copy-start.1 = (bf16[128,4096]{1,0:T(8,128)(2,1)S(1)}, bf16[128,4096]{1,0:T(8,128)(2,1)}, u32[]{:S(2)}) copy-start(bf16[128,4096]{1,0:T(8,128)(2,1)} %all-gather.5.cloned.1.call-done) | copy-start | bytes 3145732
  79.2 67.4 %copy-start.2 = (s32[1,1,4]{2,1,0:T(1,128)S(1)}, s32[1,1,4]{2,1,0:T(1,128)}, u32[]{:S(2)}) copy-start(s32[1,1,4]{2,1,0:T(1,128)} %param.10) | copy-start | bytes 52
  79.2 94.8 %all-gather.9.cloned.1.call-start = ((), (), s32[]{:S(2)}) async-start(), calls=%async_computation.6 | async-start | bytes 5242880 | tf_op jit(solution)/shard_map/all_gather | solution.py:71
  81.6 175.2 %all-gather.7.cloned.1.call-start = ((), (), s32[]{:S(2)}) async-start(), calls=%async_computation.5 | async-start | bytes 5242880 | tf_op jit(solution)/shard_map/all_gather | solution.py:72
Sparse Core Ops, SparseCore 0:
  43.2 22.5 all-gather.4
  79.3 35.9 reduce-scatter.1
Sparse Core Ops, SparseCore 1:
  81.7 92.2 all-gather.8
  176.0 80.8 all-gather.6
where the time goes:
time: 277 us
  waiting for transfers between devices  171 us (62%)
  blocking collectives  41.3 us (15%)
  matrix products  27.4 us (10%)
  between operations  15.6 us (6%)
  local copies, waits for them, and re-layouts  10.2 us (4%)
  other arithmetic  7.54 us (3%)
  starting transfers between devices  3.64 us (1%)
    all_gather x1, waiting for transfers between devices, on_device(): lax.all_gather(expert_out, 'type', axis=0, tiled=True)  75.1 us
    reduce_scatter x1, waiting for transfers between devices, on_device(): lax.psum_scatter(partial_terms.astype(jnp.bfloat16), 'dp', scatter_dimens...  33.7 us
    all_to_all x1, blocking collectives, on_device(): lax.all_to_all(back_rows, 'type', split_axis=0, concat_axis=0, tiled=True)  28.5 us
    all_gather x1, waiting for transfers between devices, on_device(): lax.all_gather(keys, 'type', axis=0, tiled=True)  27.3 us
    all_gather x1, waiting for transfers between devices, on_device(): block_rows = lax.all_gather(packed, 'dp', axis=0, tiled=True)  22.7 us
    all_gather x1, blocking collectives, on_device(): event_types = lax.all_gather(own_types, 'type', axis=0, tiled=True)  12.8 us
    all_to_all x1, waiting for transfers between devices, on_device(): lax.all_to_all(outgoing, 'type', split_axis=0, concat_axis=0, tiled=True)  12.2 us
    dot_general x1, matrix products, on_device(): jnp.dot(hidden, down_local, preferred_element_type=jnp.float32)  8.57 us
  transfers between devices with their start and end apart: 5, of which 5 were waited for; matrix products, arithmetic and copies ran while one was open for 5% of the time, Pallas kernels for 0%

commit v1 on v0

v1 whole, which is shorter than its diff:
```python
import functools
import math

import jax
import jax.numpy as jnp
from jax import lax
from jax.experimental import pallas as pl
from jax.experimental.pallas import tpu as pltpu
from jax.sharding import PartitionSpec as P

HEAD = 128
EXP_CAP = 16
LANES = 128
MASKED = -1e30
VMEM_BYTES = 56 * 1024 * 1024
VMEM = pl.BlockSpec(memory_space=pltpu.VMEM)


def params(**more):
    return pltpu.CompilerParams(vmem_limit_bytes=VMEM_BYTES, **more)


def cost(flops, bytes_accessed, transcendentals=0):
    return pl.CostEstimate(
        flops=int(flops), bytes_accessed=int(bytes_accessed), transcendentals=int(transcendentals)
    )


def strict_upper(size):
    earlier = lax.broadcasted_iota(jnp.int32, (size, size), 0)
    later = lax.broadcasted_iota(jnp.int32, (size, size), 1)
    return (earlier < later).astype(jnp.bfloat16)


def columns(width):
    for chunk in (1024, 512, 256, 128):
        if width % chunk == 0:
            return chunk, width // chunk
    raise ValueError(width)


def route_kernel(n_type, types_ref, mask_ref, tokens_ref, *out_refs):
    me = lax.axis_index("type")
    rows, width = tokens_ref.shape
    types = types_ref[...]
    type_rows = 2 * 8
    hot = lax.broadcasted_iota(jnp.int32, (type_rows, rows), 0) == types
    before = jnp.dot(
        hot.astype(jnp.bfloat16), strict_upper(rows), preferred_element_type=jnp.float32
    )
    rank = jnp.sum(jnp.where(hot, before, 0.0), axis=0, keepdims=True).astype(jnp.int32)
    place = jnp.where(rank < EXP_CAP, jnp.bitwise_xor(types, me) * EXP_CAP + rank, -1)
    select = (
        lax.broadcasted_iota(jnp.int32, (n_type * EXP_CAP, rows), 0) == place
    ).astype(jnp.bfloat16)
    chunk, count = columns(width)
    for c in range(count):
        span = pl.ds(c * chunk, chunk)
        moved = jnp.dot(select, tokens_ref[:, span], preferred_element_type=jnp.float32).astype(
            jnp.bfloat16
        )
        for s in range(n_type):
            out_refs[s][:, span] = moved[s * EXP_CAP : (s + 1) * EXP_CAP]
    lane = lax.broadcasted_iota(jnp.int32, (EXP_CAP, LANES), 1)
    row = lax.broadcasted_iota(jnp.int32, (EXP_CAP, LANES), 0)
    mask_row = jnp.zeros((EXP_CAP, LANES), jnp.int32)
    for j in range(n_type):
        mask_row = jnp.where(lane == j, mask_ref[0, j], mask_row)
    extra = jnp.where(row == 0, types, jnp.where(row == 1, mask_row, 0))
    extra = extra.astype(jnp.float32).astype(jnp.bfloat16)
    for s in range(n_type):
        out_refs[s][:, pl.ds(width, LANES)] = extra


def route(n_type, types, mask_row, tokens):
    rows, width = tokens.shape
    wide = width + LANES
    return pl.pallas_call(
        functools.partial(route_kernel, n_type),
        out_shape=[jax.ShapeDtypeStruct((EXP_CAP, wide), jnp.bfloat16)] * n_type,
        in_specs=[VMEM, pl.BlockSpec(memory_space=pltpu.SMEM), VMEM],
        out_specs=[VMEM] * n_type,
        compiler_params=params(),
        cost_estimate=cost(2 * n_type * EXP_CAP * rows * width, 2 * rows * width * 2),
    )(types, mask_row, tokens)


def pack_kernel(n_type, *refs):
    in_refs, packed_ref, info_ref = refs[:n_type], refs[n_type], refs[n_type + 1]
    me = lax.axis_index("type")
    width = packed_ref.shape[1]
    tail = pl.ds(width, LANES)
    type_rows = 2 * 8
    row = lax.broadcasted_iota(jnp.int32, (type_rows, LANES), 0)
    upper = strict_upper(LANES)
    extras = [ref[:, tail].astype(jnp.float32) for ref in in_refs]
    types = [e[0:1] for e in extras]
    hots = [row == t.astype(jnp.int32) for t in types]
    befores = [
        jnp.dot(h.astype(jnp.bfloat16), upper, preferred_element_type=jnp.float32) for h in hots
    ]
    counts = [jnp.sum(h.astype(jnp.float32), axis=1, keepdims=True) for h in hots]
    lane16 = lax.broadcasted_iota(jnp.int32, (EXP_CAP, n_type * EXP_CAP), 1)
    slot16 = lax.broadcasted_iota(jnp.int32, (EXP_CAP, n_type * EXP_CAP), 0)
    compact = jnp.zeros((EXP_CAP, n_type * EXP_CAP), jnp.bool_)
    mine = lax.broadcasted_iota(jnp.int32, (type_rows, 1), 0) == me
    info_rows = []
    for s in range(n_type):
        ahead = jnp.zeros((type_rows, 1), jnp.float32)
        for other in range(n_type):
            if other != s:
                first = jnp.bitwise_xor(me, other) < jnp.bitwise_xor(me, s)
                ahead = ahead + jnp.where(first, counts[other], 0.0)
        rank = jnp.sum(jnp.where(hots[s], befores[s] + ahead, 0.0), axis=0, keepdims=True)
        info_rows.append(jnp.where(rank < EXP_CAP, types[s] * EXP_CAP + rank, -1.0))
        offset = jnp.sum(jnp.where(mine, ahead, 0.0)).astype(jnp.int32)
        amount = jnp.sum(jnp.where(mine, counts[s], 0.0)).astype(jnp.int32)
        local = lane16 - s * EXP_CAP
        compact = compact | (
            (local >= 0) & (local < EXP_CAP) & (local < amount) & (local + offset == slot16)
        )
    lane = lax.broadcasted_iota(jnp.int32, (1, LANES), 1)
    for q in range(2):
        for s in range(n_type):
            kept = jnp.sum(
                jnp.where(lane == jnp.bitwise_xor(me, s), extras[q][1:2], 0.0),
                axis=1,
                keepdims=True,
            )
            info_rows.append(jnp.broadcast_to(jnp.where(kept == 1.0, 0.0, MASKED), (1, LANES)))
    for at, info_row in enumerate(info_rows):
        info_ref[at : at + 1, :] = info_row
    compact = compact.astype(jnp.bfloat16)
    chunk, count = columns(width)
    for c in range(count):
        span = pl.ds(c * chunk, chunk)
        rows = jnp.concatenate([ref[:, span] for ref in in_refs], axis=0)
        packed_ref[:, span] = jnp.dot(compact, rows, preferred_element_type=jnp.float32).astype(
            jnp.bfloat16
        )


def pack(n_type, incoming):
    width = incoming[0].shape[1] - LANES
    return pl.pallas_call(
        functools.partial(pack_kernel, n_type),
        out_shape=[
            jax.ShapeDtypeStruct((EXP_CAP, width), jnp.bfloat16),
            jax.ShapeDtypeStruct((3 * n_type, LANES), jnp.float32),
        ],
        in_specs=[VMEM] * n_type,
        out_specs=[VMEM, VMEM],
        compiler_params=params(),
        cost_estimate=cost(2 * n_type * EXP_CAP * EXP_CAP * width, 6 * EXP_CAP * width * 2),
    )(*incoming)


def ffn_kernel(steps, near_ref, far_ref, gate_ref, up_ref, down_ref, own_ref, away_ref, x_ref, gate_acc, up_acc, hidden_ref):
    step = pl.program_id(0)
    half = near_ref.shape[0]
    depth = gate_ref.shape[0]

    @pl.when(step == 0)
    def _():
        x_ref[:half] = near_ref[...]
        x_ref[half:] = far_ref[...]

    @pl.when(step < steps)
    def _():
        x = x_ref[:, pl.ds(pl.multiple_of(step * depth, depth), depth)]
        gate = jnp.dot(x, gate_ref[...], preferred_element_type=jnp.float32)
        up = jnp.dot(x, up_ref[...], preferred_element_type=jnp.float32)

        @pl.when(step == 0)
        def _():
            gate_acc[...] = gate
            up_acc[...] = up

        @pl.when(step > 0)
        def _():
            gate_acc[...] += gate
            up_acc[...] += up

    @pl.when(step == steps - 1)
    def _():
        gate = gate_acc[...]
        hidden_ref[...] = (gate / (1.0 + jnp.exp(-gate)) * up_acc[...]).astype(jnp.bfloat16)

    @pl.when(step >= steps)
    def _():
        out = jnp.dot(hidden_ref[...], down_ref[...], preferred_element_type=jnp.float32)
        own_ref[...] = out[:half]
        away_ref[...] = out[half:].astype(jnp.bfloat16)


def ffn(near, far, gate, up, down):
    half, width = near.shape
    rows = 2 * half
    hidden = gate.shape[1]
    depth, steps = columns(width)
    depth, steps = 512, width // 512
    first = lambda i: (jnp.minimum(i, steps - 1), 0)
    second = lambda i: (0, jnp.maximum(i - steps, 0))
    return pl.pallas_call(
        functools.partial(ffn_kernel, steps),
        grid=(2 * steps,),
        out_shape=[
            jax.ShapeDtypeStruct((half, width), jnp.float32),
            jax.ShapeDtypeStruct((half, width), jnp.bfloat16),
        ],
        in_specs=[
            VMEM,
            VMEM,
            pl.BlockSpec((depth, hidden), first),
            pl.BlockSpec((depth, hidden), first),
            pl.BlockSpec((hidden, depth), second),
        ],
        out_specs=[pl.BlockSpec((half, depth), second), pl.BlockSpec((half, depth), second)],
        scratch_shapes=[
            pltpu.VMEM((rows, width), jnp.bfloat16),
            pltpu.VMEM((rows, hidden), jnp.float32),
            pltpu.VMEM((rows, hidden), jnp.float32),
            pltpu.VMEM((rows, hidden), jnp.bfloat16),
        ],
        compiler_params=params(dimension_semantics=("arbitrary",)),
        cost_estimate=cost(6 * rows * width * hidden, 6 * width * hidden, rows * hidden),
    )(near, far, gate, up, down)


def weigh_kernel(n_type, n_query, info_ref, *refs):
    query_refs = refs[:n_query]
    key_refs = refs[n_query : n_query + n_type]
    out_refs = refs[n_query + n_type : 2 * n_query + n_type]
    select_ref = refs[-1]
    slots = n_type * EXP_CAP
    tile = key_refs[0].shape[0]

    @pl.when(pl.program_id(0) == 0)
    def _():
        row = lax.broadcasted_iota(jnp.int32, (slots + 2 * 8, tile), 0)
        for s in range(n_type):
            slot = info_ref[s : s + 1, :].astype(jnp.int32)
            select_ref[:, s * tile : (s + 1) * tile] = ((row == slot) | (row == slots)).astype(
                jnp.bfloat16
            )

    select = select_ref[...]
    scale = 1.0 / math.sqrt(HEAD)
    bias = []
    for s in range(n_type):
        rows = [info_ref[(1 + q) * n_type + s : (1 + q) * n_type + s + 1, :] for q in range(n_query)]
        bias.append(jnp.concatenate(rows, axis=1) if n_query > 1 else rows[0])
    for h in range(out_refs[0].shape[0]):
        span = pl.ds(h * HEAD, HEAD)
        query = jnp.concatenate([ref[:, span] for ref in query_refs], axis=0)
        scores = [
            lax.dot_general(
                ref[:, span], query, (((1,), (1,)), ((), ())), preferred_element_type=jnp.float32
            )
            * scale
            + bias[s]
            for s, ref in enumerate(key_refs)
        ]
        scores = jnp.concatenate(scores, axis=0)
        top = jnp.max(scores, axis=0, keepdims=True)
        weights = jnp.exp(scores - top).astype(jnp.bfloat16)
        picked = jnp.dot(select, weights, preferred_element_type=jnp.float32)
        normal = (picked[:slots] / picked[slots : slots + 1]).astype(jnp.bfloat16)
        for q in range(n_query):
            out_refs[q][h] = normal[:, q * tile : (q + 1) * tile]


def weigh(n_type, info, queries, keys, per_step=4):
    tile, width = keys[0].shape
    heads = width // HEAD
    n_query = len(queries)
    slots = n_type * EXP_CAP
    block = pl.BlockSpec((tile, per_step * HEAD), lambda i: (0, i))
    out_block = pl.BlockSpec((per_step, slots, tile), lambda i: (i, 0, 0))
    return pl.pallas_call(
        functools.partial(weigh_kernel, n_type, n_query),
        grid=(heads // per_step,),
        out_shape=[jax.ShapeDtypeStruct((heads, slots, tile), jnp.bfloat16)] * n_query,
        in_specs=[VMEM] + [block] * (n_query + n_type),
        out_specs=[out_block] * n_query,
        scratch_shapes=[pltpu.VMEM((slots + 2 * 8, n_type * tile), jnp.bfloat16)],
        compiler_params=params(dimension_semantics=("arbitrary",)),
        cost_estimate=cost(
            4 * n_query * tile * n_type * tile * width,
            2 * (n_query + n_type) * tile * width,
            n_query * tile * n_type * tile * heads,
        ),
    )(info, *queries, *keys)


def finish_kernel(n_type, n_part, info_ref, *refs):
    own_refs, back_refs = refs[:n_part], refs[n_part : 2 * n_part]
    value_refs = refs[2 * n_part : 2 * n_part + n_type]
    out_ref, attended_ref, value_ref = refs[2 * n_part + n_type :]
    me = lax.axis_index("type")
    ends = (me == 0) | (me == n_type - 1)
    tile = out_ref.shape[0]
    width = out_ref.shape[1]
    for s in range(n_type):
        at = pl.multiple_of(jnp.bitwise_xor(me, s) * EXP_CAP, EXP_CAP)
        value_ref[pl.ds(at, EXP_CAP), :] = value_refs[s][...]
    row = lax.broadcasted_iota(jnp.int32, (n_type * EXP_CAP, tile), 0)
    select = (row == info_ref[0:1, :].astype(jnp.int32)).astype(jnp.bfloat16)
    chunk, count = columns(width)
    contract = (((0,), (0,)), ((), ()))
    for c in range(count):
        span = pl.ds(c * chunk, chunk)
        out_ref[:, span] = lax.dot_general(
            select, value_ref[:, span], contract, preferred_element_type=jnp.float32
        ).astype(jnp.bfloat16)
    at = 0
    for part in range(n_part):
        for h in range(own_refs[part].shape[0]):
            span = pl.ds(at * HEAD, HEAD)
            weights = own_refs[part][h]
            if back_refs:
                weights = jnp.where(ends, back_refs[part][h], weights)
            attended_ref[:, span] = lax.dot_general(
                weights, value_ref[:, span], contract, preferred_element_type=jnp.float32
            ).astype(jnp.bfloat16)
            at += 1


def finish(n_type, info, own, back, values, tile):
    width = values[0].shape[1]
    n_part = len(own)
    return pl.pallas_call(
        functools.partial(finish_kernel, n_type, n_part),
        out_shape=[jax.ShapeDtypeStruct((tile, width), jnp.bfloat16)] * 2,
        in_specs=[VMEM] * (1 + 2 * n_part + n_type),
        out_specs=[VMEM] * 2,
        scratch_shapes=[pltpu.VMEM((n_type * EXP_CAP, width), jnp.bfloat16)],
        compiler_params=params(),
        cost_estimate=cost(4 * tile * n_type * EXP_CAP * width, 6 * tile * width),
    )(info, *own, *back, *values)


def swap(x, axis, size, s):
    return lax.ppermute(x, axis, [(i, i ^ s) for i in range(size)])


def on_device(n_dp, n_type, tokens, token_types, tile_mask, queries, keys, gate_weight, up_weight, down_weight):
    tile, width = tokens.shape
    outgoing = route(n_type, token_types.reshape(1, tile), tile_mask.reshape(1, n_type), tokens)
    incoming = [outgoing[0]] + [swap(outgoing[s], "type", n_type, s) for s in range(1, n_type)]
    packed, info = pack(n_type, incoming)

    if n_type == 4:
        packed, info, keys, queries = lax.optimization_barrier((packed, info, keys, queries))
        n_part = 2
        to_middle = [(0, 1), (3, 2)]
        across = [(1, 2), (2, 1)]
        to_end = [(1, 0), (2, 3)]
        wide = width // n_part
        own_weights, back_weights = [], []
        for part in range(n_part):
            span = slice(part * wide, (part + 1) * wide)
            key_part, query_part = keys[:, span], queries[:, span]
            near = lax.ppermute(key_part, "type", to_middle)
            other = lax.ppermute(key_part, "type", across)
            far = lax.ppermute(near, "type", across)
            guest = lax.ppermute(query_part, "type", to_middle)
            own, theirs = weigh(n_type, info, [query_part, guest], [key_part, near, far, other])
            own_weights.append(own)
            back_weights.append(lax.ppermute(theirs, "type", to_end))
    else:
        others = [keys] + [swap(keys, "type", n_type, s) for s in range(1, n_type)]
        own_weights = list(weigh(n_type, info, [queries], others))
        back_weights = own_weights

    n_same = n_dp // 2
    same_core = jnp.concatenate(
        [packed] + [swap(packed, "dp", n_dp, 2 * p) for p in range(1, n_same)], axis=0
    )
    other_core = swap(same_core, "dp", n_dp, 1)
    own_rows, away_rows = ffn(same_core, other_core, gate_weight[0], up_weight[0], down_weight[0])
    from_core = swap(away_rows, "dp", n_dp, 1)
    chip_rows = (own_rows + from_core.astype(jnp.float32)).astype(jnp.bfloat16)
    pieces = [chip_rows[p * EXP_CAP : (p + 1) * EXP_CAP] for p in range(n_same)]
    total = pieces[0].astype(jnp.float32)
    for p in range(1, n_same):
        total = total + swap(pieces[p], "dp", n_dp, 2 * p).astype(jnp.float32)
    expert_rows = total.astype(jnp.bfloat16)
    values = [expert_rows] + [swap(expert_rows, "type", n_type, s) for s in range(1, n_type)]
    expert_out, attended = finish(n_type, info, own_weights, back_weights, values, tile)
    return (expert_out, attended)


def solution(mesh):
    return jax.shard_map(
        functools.partial(on_device, mesh.shape["dp"], mesh.shape["type"]),
        mesh=mesh,
        in_specs=(
            P(("dp", "type"), None),
            P(("dp", "type"), None),
            P("dp", "type", None),
            P(("dp", "type"), None),
            P(("dp", "type"), None),
            P("type", None, "dp"),
            P("type", None, "dp"),
            P("type", "dp", None),
        ),
        out_specs=(P(("dp", "type"), None), P(("dp", "type"), None)),
        check_vma=False,
    )
```

time: 277 us -> 150 us (0.54)
  waiting for transfers between devices: 171 us -> 61.7 us
  blocking collectives: 41.3 us -> 0 us
  Pallas kernels: 0 us -> 40.7 us
  starting transfers between devices: 3.64 us -> 40 us
  matrix products: 27.4 us -> 0 us
  between operations: 15.6 us -> 1.05 us
  other arithmetic: 7.54 us -> 1.39 us
  local copies, waits for them, and re-layouts: 10.2 us -> 4.26 us
    all_gather x3 -> x0, waiting for transfers between devices: 125 us -> none  [the longest x1 75.1 us: on_device(): lax.all_gather(expert_out, 'type', axis=0, tiled=True)]
    ppermute x0 -> x24, waiting for transfers between devices: none -> 61.7 us  [the longest x2 32.5 us: on_device(): guest = lax.ppermute(query_part, 'type', to_middle)]
    pallas_call x0 -> x6, Pallas kernels: none -> 40.7 us  [the longest x1 17.4 us: ffn(): pl.pallas_call(functools.partial(ffn_kernel, steps), grid=(2 * steps,), o...]
    ppermute x0 -> x24, starting transfers between devices: none -> 40 us  [the longest x14 19 us: swap(): return lax.ppermute(x, axis, [(i, i ^ s) for i in range(size)])]
    reduce_scatter x1 -> x0, waiting for transfers between devices: 33.7 us -> none  [on_device(): lax.psum_scatter(partial_terms.astype(jnp.bfloat16), 'dp', scatter_dimens...]
    all_to_all x1 -> x0, blocking collectives: 28.5 us -> none  [on_device(): lax.all_to_all(back_rows, 'type', split_axis=0, concat_axis=0, tiled=True)]
    dot_general x8 -> x0, matrix products: 27.4 us -> none  [the longest x1 8.57 us: on_device(): jnp.dot(hidden, down_local, preferred_element_type=jnp.float32)]
    all_gather x1 -> x0, blocking collectives: 12.8 us -> none  [on_device(): event_types = lax.all_gather(own_types, 'type', axis=0, tiled=True)]
  transfers between devices with their start and end apart: 5 -> 24, of which waited for: 5 -> 10; matrix products, arithmetic and copies ran while one was open for 5% -> 2% of each run, Pallas kernels for 0% -> 10%
where the time goes in v1:
time: 150 us; the launch traced here: 149 us
  waiting for transfers between devices  61.7 us (41%)
  Pallas kernels  40.7 us (27%)
  starting transfers between devices  40 us (27%)
  local copies, waits for them, and re-layouts  4.26 us (3%)
    ppermute x2, waiting for transfers between devices, on_device(): guest = lax.ppermute(query_part, 'type', to_middle)  32.5 us
    ppermute x14, waiting for transfers between devices, swap(): return lax.ppermute(x, axis, [(i, i ^ s) for i in range(size)])  19.7 us
    ppermute x14, starting transfers between devices, swap(): return lax.ppermute(x, axis, [(i, i ^ s) for i in range(size)])  19 us
    pallas_call x1, Pallas kernels, ffn(): pl.pallas_call(functools.partial(ffn_kernel, steps), grid=(2 * steps,), o...  17.4 us
    pallas_call x2, Pallas kernels, weigh(): pl.pallas_call(functools.partial(weigh_kernel, n_type, n_query), grid=(he...  15.5 us
    ppermute x2, waiting for transfers between devices, on_device(): back_weights.append(lax.ppermute(theirs, 'type', to_end))  9.45 us
    ppermute x2, starting transfers between devices, on_device(): near = lax.ppermute(key_part, 'type', to_middle)  8.29 us
    ppermute x2, starting transfers between devices, on_device(): guest = lax.ppermute(query_part, 'type', to_middle)  7.32 us
  transfers between devices with their start and end apart: 24, of which 10 were waited for; matrix products, arithmetic and copies ran while one was open for 2% of the time, Pallas kernels for 10%

profile of v1, /device:TPU:0, one launch (start us, length us, event | category | flops | bytes accessed | tf_op | source)
XLA Modules:
  0.0 149.1 jit_solution(5964433070061406739)
XLA Ops:
  0.6 2.5 %shard_map.95 = (bf16[16,4224]{1,0:T(8,128)(2,1)}, bf16[16,4224]{1,0:T(8,128)(2,1)}, bf16[16,4224]{1,0:T(8,128)(2,1)}, bf16[16,4224]{1,0:T(8,128)(2,1)}) custom-call(s32[1,128]{1,0:T(1,128)} %bitcast.8, s32[1,4]{1,0:T(1,128)} %bitcast.9, bf16[128,4096]{1,0:T(8,128)(2,1)} %tokens_ref.1), custom_call_target="tpu_custom_call" | custom-call | flops 67108864 | bytes 2097152 | tf_op jit(solution)/shard_map/pallas_call | solution.py:78
  3.1 3.0 %collective-permute-start = (bf16[16,4224]{1,0:T(8,128)(2,1)}, bf16[16,4224]{1,0:T(8,128)(2,1)S(1)}, u32[]{:S(2)}, u32[]{:S(2)}) collective-permute-start(bf16[16,4224]{1,0:T(8,128)(2,1)} %get-tuple-element.19), channel_id=1, source_target_pairs={{0,1},{1,0},{2,3},{3,2},{4,5},{5,4},{6,7},{7,6},{8,9},{9,8},{10,11... | collective-permute-start | bytes 405512 | tf_op jit(solution)/shard_map/ppermute | solution.py:344
  6.1 2.6 %collective-permute-start.1 = (bf16[16,4224]{1,0:T(8,128)(2,1)}, bf16[16,4224]{1,0:T(8,128)(2,1)S(1)}, u32[]{:S(2)}, u32[]{:S(2)}) collective-permute-start(bf16[16,4224]{1,0:T(8,128)(2,1)} %get-tuple-element.20), channel_id=1, source_target_pairs={{0,2},{1,3},{2,0},{3,1},{4,6},{5,7},{6,4},{7,5},{8,10},{9,11},{10,... | collective-permute-start | bytes 405512 | tf_op jit(solution)/shard_map/ppermute | solution.py:344
  8.7 2.9 %collective-permute-done.refs_1_ = bf16[16,4224]{1,0:T(8,128)(2,1)S(1)} collective-permute-done((bf16[16,4224]{1,0:T(8,128)(2,1)}, bf16[16,4224]{1,0:T(8,128)(2,1)S(1)}, u32[]{:S(2)}, u32[]{:S(2)}) %collective-permute-start) | collective-permute-done | bytes 135200 | tf_op jit(solution)/shard_map/ppermute | solution.py:344
  11.5 8.0 %collective-permute-done.1.refs_2_ = bf16[16,4224]{1,0:T(8,128)(2,1)S(1)} collective-permute-done((bf16[16,4224]{1,0:T(8,128)(2,1)}, bf16[16,4224]{1,0:T(8,128)(2,1)S(1)}, u32[]{:S(2)}, u32[]{:S(2)}) %collective-permute-start.1) | collective-permute-done | bytes 135200 | tf_op jit(solution)/shard_map/ppermute | solution.py:344
  19.5 0.6 copy-done.12
  20.2 2.2 %shard_map.96 = (bf16[16,4096]{1,0:T(8,128)(2,1)}, f32[12,128]{1,0:T(8,128)}) custom-call(bf16[16,4224]{1,0:T(8,128)(2,1)} %get-tuple-element.18.refs_0_, bf16[16,4224]{1,0:T(8,128)(2,1)} %copy-done.11, bf16[16,4224]{1,0:T(8,128)(2,1)} %copy-done.12, bf16[16,4224]{1,0:T(8,128)(2,1)} %copy-done.13), custom_call_target="tpu_custom_call" | custom-call | flops 8388608 | bytes 786432 | tf_op jit(solution)/shard_map/pallas_call | solution.py:145
  22.4 1.5 collective-permute-start.13
  23.9 0.9 constant_dynamic-update-slice_fusion.3
  24.8 1.6 %collective-permute-start.14 = (bf16[16,4096]{1,0:T(8,128)(2,1)}, bf16[16,4096]{1,0:T(8,128)(2,1)S(1)}, u32[]{:S(2)}, u32[]{:S(2)}) collective-permute-start(bf16[16,4096]{1,0:T(8,128)(2,1)} %get-tuple-element.31), channel_id=1, source_target_pairs={{0,16},{4,20},{8,24},{12,28},{16,0},{20,4},{24,8},{28,12},{1,17},{... | collective-permute-start | bytes 393224 | tf_op jit(solution)/shard_map/ppermute | solution.py:344
  26.4 0.5 collective-permute-start.15
  26.9 1.8 %collective-permute-done.13 = bf16[16,4096]{1,0:T(8,128)(2,1)S(1)} collective-permute-done((bf16[16,4096]{1,0:T(8,128)(2,1)}, bf16[16,4096]{1,0:T(8,128)(2,1)S(1)}, u32[]{:S(2)}, u32[]{:S(2)}) %collective-permute-start.13) | collective-permute-done | bytes 131104 | tf_op jit(solution)/shard_map/ppermute | solution.py:344
  28.7 1.7 %collective-permute-done.14 = bf16[16,4096]{1,0:T(8,128)(2,1)S(1)} collective-permute-done((bf16[16,4096]{1,0:T(8,128)(2,1)}, bf16[16,4096]{1,0:T(8,128)(2,1)S(1)}, u32[]{:S(2)}, u32[]{:S(2)}) %collective-permute-start.14) | collective-permute-done | bytes 131104 | tf_op jit(solution)/shard_map/ppermute | solution.py:344
  30.5 2.0 %collective-permute-done.15 = bf16[16,4096]{1,0:T(8,128)(2,1)S(1)} collective-permute-done((bf16[16,4096]{1,0:T(8,128)(2,1)}, bf16[16,4096]{1,0:T(8,128)(2,1)S(1)}, u32[]{:S(2)}, u32[]{:S(2)}) %collective-permute-start.15) | collective-permute-done | bytes 131104 | tf_op jit(solution)/shard_map/ppermute | solution.py:344
  32.5 0.1 collective-permute-start.16
  32.6 1.9 %collective-permute-done.16.far_ref = bf16[64,4096]{1,0:T(8,128)(2,1)S(1)} collective-permute-done((bf16[64,4096]{1,0:T(8,128)(2,1)S(1)}, bf16[64,4096]{1,0:T(8,128)(2,1)S(1)}, u32[]{:S(2)}, u32[]{:S(2)}) %collective-permute-start.16) | collective-permute-done | bytes 524320 | tf_op jit(solution)/shard_map/ppermute | solution.py:344
  34.5 0.8 copy-done.3
  35.3 17.4 %shard_map.99 = (f32[64,4096]{1,0:T(8,128)}, bf16[64,4096]{1,0:T(8,128)(2,1)}) custom-call(bf16[64,4096]{1,0:T(8,128)(2,1)} %copy-done.2, bf16[64,4096]{1,0:T(8,128)(2,1)} %copy-done.3, bf16[4096,896]{1,0:T(8,128)(2,1)} %bitcast.5, bf16[4096,896]{1,0:T(8,128)(2,1)} %bitcast.6, bf16[896,4096]{1,0:T(8,128)(2,1)} %bitcast.7), custom_call_target="tpu_custom_call" | custom-call | flops 2818572288 | bytes 22020096 | tf_op jit(solution)/shard_map/pallas_call | solution.py:204
  52.8 0.1 collective-permute-start.17
  52.9 0.1 fusion
  53.0 4.2 %collective-permute-start.4 = (bf16[128,2048]{1,0:T(8,128)(2,1)S(1)}, bf16[128,2048]{1,0:T(8,128)(2,1)S(1)}, u32[]{:S(2)}, u32[]{:S(2)}) collective-permute-start(bf16[128,2048]{1,0:T(8,128)(2,1)S(1)} %get-tuple-element.35.refs_2_), channel_id=1, source_target_pairs={{0,1},{3,2},{4,5},{7,6},{8,9},{11,10},{12,13},{15,14},{16,17},{19,... | collective-permute-start | bytes 1572872 | tf_op jit(solution)/shard_map/ppermute | solution.py:364
  57.2 0.7 collective-permute-start.6
  57.9 4.1 %collective-permute-start.8 = (bf16[128,2048]{1,0:T(8,128)(2,1)S(1)}, bf16[128,2048]{1,0:T(8,128)(2,1)S(1)}, u32[]{:S(2)}, u32[]{:S(2)}) collective-permute-start(bf16[128,2048]{1,0:T(8,128)(2,1)S(1)} %get-tuple-element.34.refs_2_), channel_id=1, source_target_pairs={{0,1},{3,2},{4,5},{7,6},{8,9},{11,10},{12,13},{15,14},{16,17},{19,... | collective-permute-start | bytes 1572872 | tf_op jit(solution)/shard_map/ppermute | solution.py:364
  62.0 0.7 collective-permute-start.10
  62.7 0.1 fusion.1
  62.9 2.9 %collective-permute-start.3 = (bf16[128,2048]{1,0:T(8,128)(2,1)S(1)}, bf16[128,2048]{1,0:T(8,128)(2,1)S(1)}, u32[]{:S(2)}, u32[]{:S(2)}) collective-permute-start(bf16[128,2048]{1,0:T(8,128)(2,1)S(1)} %get-tuple-element.37.refs_0_), channel_id=1, source_target_pairs={{0,1},{3,2},{4,5},{7,6},{8,9},{11,10},{12,13},{15,14},{16,17},{19,... | collective-permute-start | bytes 1572872 | tf_op jit(solution)/shard_map/ppermute | solution.py:367
  65.8 1.3 add_convert_fusion
  67.1 24.2 %collective-permute-done.3.refs_1_ = bf16[128,2048]{1,0:T(8,128)(2,1)S(1)} collective-permute-done((bf16[128,2048]{1,0:T(8,128)(2,1)S(1)}, bf16[128,2048]{1,0:T(8,128)(2,1)S(1)}, u32[]{:S(2)}, u32[]{:S(2)}) %collective-permute-start.3) | collective-permute-done | bytes 524320 | tf_op jit(solution)/shard_map/ppermute | solution.py:367
  91.3 4.4 %collective-permute-start.7 = (bf16[128,2048]{1,0:T(8,128)(2,1)S(1)}, bf16[128,2048]{1,0:T(8,128)(2,1)S(1)}, u32[]{:S(2)}, u32[]{:S(2)}) collective-permute-start(bf16[128,2048]{1,0:T(8,128)(2,1)S(1)} %get-tuple-element.36.refs_0_), channel_id=1, source_target_pairs={{0,1},{3,2},{4,5},{7,6},{8,9},{11,10},{12,13},{15,14},{16,17},{19,... | collective-permute-start | bytes 1572872 | tf_op jit(solution)/shard_map/ppermute | solution.py:367
  95.8 0.7 collective-permute-start.5
  96.5 0.7 collective-permute-start.9
  97.2 1.0 collective-permute-start.20
  98.3 8.3 %collective-permute-done.7.refs_1_ = bf16[128,2048]{1,0:T(8,128)(2,1)S(1)} collective-permute-done((bf16[128,2048]{1,0:T(8,128)(2,1)S(1)}, bf16[128,2048]{1,0:T(8,128)(2,1)S(1)}, u32[]{:S(2)}, u32[]{:S(2)}) %collective-permute-start.7) | collective-permute-done | bytes 524320 | tf_op jit(solution)/shard_map/ppermute | solution.py:367
  106.6 0.6 collective-permute-start.19
  107.2 1.0 collective-permute-start.18
  108.2 7.8 %shard_map.97 = (bf16[16,64,128]{2,1,0:T(8,128)(2,1)}, bf16[16,64,128]{2,1,0:T(8,128)(2,1)}) custom-call(f32[12,128]{1,0:T(8,128)} %get-tuple-element.24.info_ref, bf16[128,2048]{1,0:T(8,128)(2,1)} %copy-done.8, bf16[128,2048]{1,0:T(8,128)(2,1)} %copy-done.22, bf16[128,2048]{1,0:T(8,128)(2,1)} %copy-done.7, bf16[128,2048]{1,0:T(8,128)(2,1)} %copy-done.19, ...), custom_call_target="tpu_custom_call" | custom-call | flops 1073741824 | bytes 3145728 | tf_op jit(solution)/shard_map/pallas_call | solution.py:280
  115.9 1.3 collective-permute-start.11
  117.3 0.8 copy-done.23
  118.1 7.7 %shard_map.98 = (bf16[16,64,128]{2,1,0:T(8,128)(2,1)}, bf16[16,64,128]{2,1,0:T(8,128)(2,1)}) custom-call(f32[12,128]{1,0:T(8,128)} %get-tuple-element.24.info_ref, bf16[128,2048]{1,0:T(8,128)(2,1)} %copy-done.6, bf16[128,2048]{1,0:T(8,128)(2,1)} %copy-done.21, bf16[128,2048]{1,0:T(8,128)(2,1)} %copy-done.5, bf16[128,2048]{1,0:T(8,128)(2,1)} %copy-done.17, ...), custom_call_target="tpu_custom_call" | custom-call | flops 1073741824 | bytes 3145728 | tf_op jit(solution)/shard_map/pallas_call | solution.py:280
  125.9 1.3 collective-permute-start.12
  127.2 0.1 add_convert_fusion.1.refs_4_
  127.3 4.6 %collective-permute-start.21 = (bf16[16,4096]{1,0:T(8,128)(2,1)S(1)}, bf16[16,4096]{1,0:T(8,128)(2,1)S(1)}, u32[]{:S(2)}, u32[]{:S(2)}) collective-permute-start(bf16[16,4096]{1,0:T(8,128)(2,1)S(1)} %add_convert_fusion.1.refs_4_), channel_id=1, source_target_pairs={{0,1},{1,0},{2,3},{3,2},{4,5},{5,4},{6,7},{7,6},{8,9},{9,8},{10,11... | collective-permute-start | bytes 393224 | tf_op jit(solution)/shard_map/ppermute | solution.py:344
  131.8 1.1 collective-permute-start.22
  133.0 1.4 collective-permute-start.23
  134.4 9.4 %collective-permute-done.12.refs_3_ = bf16[16,64,128]{2,1,0:T(8,128)(2,1)S(1)} collective-permute-done((bf16[16,64,128]{2,1,0:T(8,128)(2,1)}, bf16[16,64,128]{2,1,0:T(8,128)(2,1)S(1)}, u32[]{:S(2)}, u32[]{:S(2)}) %collective-permute-start.12) | collective-permute-done | bytes 262176 | tf_op jit(solution)/shard_map/ppermute | solution.py:370
  143.8 1.4 collective-permute-done.21.refs_5_
  145.3 0.6 copy-done.14
  146.0 3.1 %shard_map.100 = (bf16[128,4096]{1,0:T(8,128)(2,1)}, bf16[128,4096]{1,0:T(8,128)(2,1)}) custom-call(f32[12,128]{1,0:T(8,128)} %get-tuple-element.24.info_ref, bf16[16,64,128]{2,1,0:T(8,128)(2,1)} %get-tuple-element.27.refs_0_, bf16[16,64,128]{2,1,0:T(8,128)(2,1)} %get-tuple-element.28.refs_1_, bf16[16,64,128]{2,1,0:T(8,128)(2,1)} %copy-done.9, ...), custom_call_target="tpu_custom_call" | custom-call | flops 134217728 | bytes 3145728 | tf_op jit(solution)/shard_map/pallas_call | solution.py:332
  (65 shorter events, 0.3 us)
Async XLA Ops:
  3.1 8.5 %collective-permute-start = (bf16[16,4224]{1,0:T(8,128)(2,1)}, bf16[16,4224]{1,0:T(8,128)(2,1)S(1)}, u32[]{:S(2)}, u32[]{:S(2)}) collective-permute-start(bf16[16,4224]{1,0:T(8,128)(2,1)} %get-tuple-element.19), channel_id=1, source_target_pairs={{0,1},{1,0},{2,3},{3,2},{4,5},{5,4},{6,7},{7,6},{8,9},{9,8},{10,11... | collective-permute-start | bytes 405512 | tf_op jit(solution)/shard_map/ppermute | solution.py:344
  6.1 13.4 %collective-permute-start.1 = (bf16[16,4224]{1,0:T(8,128)(2,1)}, bf16[16,4224]{1,0:T(8,128)(2,1)S(1)}, u32[]{:S(2)}, u32[]{:S(2)}) collective-permute-start(bf16[16,4224]{1,0:T(8,128)(2,1)} %get-tuple-element.20), channel_id=1, source_target_pairs={{0,2},{1,3},{2,0},{3,1},{4,6},{5,7},{6,4},{7,5},{8,10},{9,11},{10,... | collective-permute-start | bytes 405512 | tf_op jit(solution)/shard_map/ppermute | solution.py:344
  8.7 10.8 %collective-permute-start.2 = (bf16[16,4224]{1,0:T(8,128)(2,1)}, bf16[16,4224]{1,0:T(8,128)(2,1)S(1)}, u32[]{:S(2)}, u32[]{:S(2)}) collective-permute-start(bf16[16,4224]{1,0:T(8,128)(2,1)} %get-tuple-element.21), channel_id=1, source_target_pairs={{0,3},{1,2},{2,1},{3,0},{4,7},{5,6},{6,5},{7,4},{8,11},{9,10},{10,... | collective-permute-start | bytes 405512 | tf_op jit(solution)/shard_map/ppermute | solution.py:344
  11.5 8.0 %copy-start.11 = (bf16[16,4224]{1,0:T(8,128)(2,1)}, bf16[16,4224]{1,0:T(8,128)(2,1)S(1)}, u32[]{:S(2)}) copy-start(bf16[16,4224]{1,0:T(8,128)(2,1)S(1)} %collective-permute-done.refs_1_) | copy-start | bytes 405508
  19.5 0.7 copy-start.12
  19.5 0.7 copy-start.13
  22.4 6.3 %collective-permute-start.13 = (bf16[16,4096]{1,0:T(8,128)(2,1)}, bf16[16,4096]{1,0:T(8,128)(2,1)S(1)}, u32[]{:S(2)}, u32[]{:S(2)}) collective-permute-start(bf16[16,4096]{1,0:T(8,128)(2,1)} %get-tuple-element.31), channel_id=1, source_target_pairs={{0,8},{4,12},{8,0},{12,4},{16,24},{20,28},{24,16},{28,20},{1,9},{5... | collective-permute-start | bytes 393224 | tf_op jit(solution)/shard_map/ppermute | solution.py:344
  24.8 5.6 %collective-permute-start.14 = (bf16[16,4096]{1,0:T(8,128)(2,1)}, bf16[16,4096]{1,0:T(8,128)(2,1)S(1)}, u32[]{:S(2)}, u32[]{:S(2)}) collective-permute-start(bf16[16,4096]{1,0:T(8,128)(2,1)} %get-tuple-element.31), channel_id=1, source_target_pairs={{0,16},{4,20},{8,24},{12,28},{16,0},{20,4},{24,8},{28,12},{1,17},{... | collective-permute-start | bytes 393224 | tf_op jit(solution)/shard_map/ppermute | solution.py:344
  26.4 6.1 %collective-permute-start.15 = (bf16[16,4096]{1,0:T(8,128)(2,1)}, bf16[16,4096]{1,0:T(8,128)(2,1)S(1)}, u32[]{:S(2)}, u32[]{:S(2)}) collective-permute-start(bf16[16,4096]{1,0:T(8,128)(2,1)} %get-tuple-element.31), channel_id=1, source_target_pairs={{0,24},{4,28},{8,16},{12,20},{16,8},{20,12},{24,0},{28,4},{1,25},{... | collective-permute-start | bytes 393224 | tf_op jit(solution)/shard_map/ppermute | solution.py:344
  32.5 2.0 %copy-start.2 = (bf16[64,4096]{1,0:T(8,128)(2,1)}, bf16[64,4096]{1,0:T(8,128)(2,1)S(1)}, u32[]{:S(2)}) copy-start(bf16[64,4096]{1,0:T(8,128)(2,1)S(1)} %constant_dynamic-update-slice_fusion.near_ref) | copy-start | bytes 1572868
  32.5 2.0 %collective-permute-start.16 = (bf16[64,4096]{1,0:T(8,128)(2,1)S(1)}, bf16[64,4096]{1,0:T(8,128)(2,1)S(1)}, u32[]{:S(2)}, u32[]{:S(2)}) collective-permute-start(bf16[64,4096]{1,0:T(8,128)(2,1)S(1)} %constant_dynamic-update-slice_fusion.near_ref), channel_id=1, source_target_pairs={{0,4},{4,0},{8,12},{12,8},{16,20},{20,16},{24,28},{28,24},{1,5},{5... | collective-permute-start | bytes 1572872 | tf_op jit(solution)/shard_map/ppermute | solution.py:344
  34.5 0.8 copy-start.3
  35.3 17.6 %copy-start = (bf16[128,4096]{1,0:T(8,128)(2,1)S(1)}, bf16[128,4096]{1,0:T(8,128)(2,1)}, u32[]{:S(2)}) copy-start(bf16[128,4096]{1,0:T(8,128)(2,1)} %param.12) | copy-start | bytes 3145732
  35.3 27.4 %copy-start.1 = (bf16[128,4096]{1,0:T(8,128)(2,1)S(1)}, bf16[128,4096]{1,0:T(8,128)(2,1)}, u32[]{:S(2)}) copy-start(bf16[128,4096]{1,0:T(8,128)(2,1)} %param.11) | copy-start | bytes 3145732
  52.8 10.1 %collective-permute-start.17 = (bf16[64,4096]{1,0:T(8,128)(2,1)}, bf16[64,4096]{1,0:T(8,128)(2,1)S(1)}, u32[]{:S(2)}, u32[]{:S(2)}) collective-permute-start(bf16[64,4096]{1,0:T(8,128)(2,1)} %get-tuple-element.33), channel_id=1, source_target_pairs={{0,4},{4,0},{8,12},{12,8},{16,20},{20,16},{24,28},{28,24},{1,5},{5... | collective-permute-start | bytes 1572872 | tf_op jit(solution)/shard_map/ppermute | solution.py:344
  53.0 55.1 %copy-start.7 = (bf16[128,2048]{1,0:T(8,128)(2,1)}, bf16[128,2048]{1,0:T(8,128)(2,1)S(1)}, u32[]{:S(2)}) copy-start(bf16[128,2048]{1,0:T(8,128)(2,1)S(1)} %get-tuple-element.35.refs_2_) | copy-start | bytes 1572868
  53.0 64.2 %copy-start.5 = (bf16[128,2048]{1,0:T(8,128)(2,1)}, bf16[128,2048]{1,0:T(8,128)(2,1)S(1)}, u32[]{:S(2)}) copy-start(bf16[128,2048]{1,0:T(8,128)(2,1)S(1)} %get-tuple-element.34.refs_2_) | copy-start | bytes 1572868
  53.0 42.7 %collective-permute-start.4 = (bf16[128,2048]{1,0:T(8,128)(2,1)S(1)}, bf16[128,2048]{1,0:T(8,128)(2,1)S(1)}, u32[]{:S(2)}, u32[]{:S(2)}) collective-permute-start(bf16[128,2048]{1,0:T(8,128)(2,1)S(1)} %get-tuple-element.35.refs_2_), channel_id=1, source_target_pairs={{0,1},{3,2},{4,5},{7,6},{8,9},{11,10},{12,13},{15,14},{16,17},{19,... | collective-permute-start | bytes 1572872 | tf_op jit(solution)/shard_map/ppermute | solution.py:364
  57.2 40.0 %collective-permute-start.6 = (bf16[128,2048]{1,0:T(8,128)(2,1)S(1)}, bf16[128,2048]{1,0:T(8,128)(2,1)S(1)}, u32[]{:S(2)}, u32[]{:S(2)}) collective-permute-start(bf16[128,2048]{1,0:T(8,128)(2,1)S(1)} %get-tuple-element.35.refs_2_), channel_id=1, source_target_pairs={{1,2},{2,1},{5,6},{6,5},{9,10},{10,9},{13,14},{14,13},{17,18},{18,... | collective-permute-start | bytes 1572872 | tf_op jit(solution)/shard_map/ppermute | solution.py:365
  57.9 38.6 %collective-permute-start.8 = (bf16[128,2048]{1,0:T(8,128)(2,1)S(1)}, bf16[128,2048]{1,0:T(8,128)(2,1)S(1)}, u32[]{:S(2)}, u32[]{:S(2)}) collective-permute-start(bf16[128,2048]{1,0:T(8,128)(2,1)S(1)} %get-tuple-element.34.refs_2_), channel_id=1, source_target_pairs={{0,1},{3,2},{4,5},{7,6},{8,9},{11,10},{12,13},{15,14},{16,17},{19,... | collective-permute-start | bytes 1572872 | tf_op jit(solution)/shard_map/ppermute | solution.py:364
  62.0 53.9 %collective-permute-start.10 = (bf16[128,2048]{1,0:T(8,128)(2,1)S(1)}, bf16[128,2048]{1,0:T(8,128)(2,1)S(1)}, u32[]{:S(2)}, u32[]{:S(2)}) collective-permute-start(bf16[128,2048]{1,0:T(8,128)(2,1)S(1)} %get-tuple-element.34.refs_2_), channel_id=1, source_target_pairs={{1,2},{2,1},{5,6},{6,5},{9,10},{10,9},{13,14},{14,13},{17,18},{18,... | collective-permute-start | bytes 1572872 | tf_op jit(solution)/shard_map/ppermute | solution.py:365
  62.8 45.3 %copy-start.8 = (bf16[128,2048]{1,0:T(8,128)(2,1)}, bf16[128,2048]{1,0:T(8,128)(2,1)S(1)}, u32[]{:S(2)}) copy-start(bf16[128,2048]{1,0:T(8,128)(2,1)S(1)} %get-tuple-element.37.refs_0_) | copy-start | bytes 1572868
  62.9 54.4 %copy-start.6 = (bf16[128,2048]{1,0:T(8,128)(2,1)}, bf16[128,2048]{1,0:T(8,128)(2,1)S(1)}, u32[]{:S(2)}) copy-start(bf16[128,2048]{1,0:T(8,128)(2,1)S(1)} %get-tuple-element.36.refs_0_) | copy-start | bytes 1572868
  62.9 28.4 %collective-permute-start.3 = (bf16[128,2048]{1,0:T(8,128)(2,1)S(1)}, bf16[128,2048]{1,0:T(8,128)(2,1)S(1)}, u32[]{:S(2)}, u32[]{:S(2)}) collective-permute-start(bf16[128,2048]{1,0:T(8,128)(2,1)S(1)} %get-tuple-element.37.refs_0_), channel_id=1, source_target_pairs={{0,1},{3,2},{4,5},{7,6},{8,9},{11,10},{12,13},{15,14},{16,17},{19,... | collective-permute-start | bytes 1572872 | tf_op jit(solution)/shard_map/ppermute | solution.py:367
  91.3 16.8 %copy-start.22 = (bf16[128,2048]{1,0:T(8,128)(2,1)}, bf16[128,2048]{1,0:T(8,128)(2,1)S(1)}, u32[]{:S(2)}) copy-start(bf16[128,2048]{1,0:T(8,128)(2,1)S(1)} %collective-permute-done.3.refs_1_) | copy-start | bytes 1572868
  91.3 15.3 %collective-permute-start.7 = (bf16[128,2048]{1,0:T(8,128)(2,1)S(1)}, bf16[128,2048]{1,0:T(8,128)(2,1)S(1)}, u32[]{:S(2)}, u32[]{:S(2)}) collective-permute-start(bf16[128,2048]{1,0:T(8,128)(2,1)S(1)} %get-tuple-element.36.refs_0_), channel_id=1, source_target_pairs={{0,1},{3,2},{4,5},{7,6},{8,9},{11,10},{12,13},{15,14},{16,17},{19,... | collective-permute-start | bytes 1572872 | tf_op jit(solution)/shard_map/ppermute | solution.py:367
  95.7 12.4 %copy-start.19 = (bf16[128,2048]{1,0:T(8,128)(2,1)}, bf16[128,2048]{1,0:T(8,128)(2,1)S(1)}, u32[]{:S(2)}) copy-start(bf16[128,2048]{1,0:T(8,128)(2,1)S(1)} %collective-permute-done.4.refs_3_) | copy-start | bytes 1572868
  95.8 11.4 %collective-permute-start.5 = (bf16[128,2048]{1,0:T(8,128)(2,1)S(1)}, bf16[128,2048]{1,0:T(8,128)(2,1)S(1)}, u32[]{:S(2)}, u32[]{:S(2)}) collective-permute-start(bf16[128,2048]{1,0:T(8,128)(2,1)S(1)} %collective-permute-done.4.refs_3_), channel_id=1, source_target_pairs={{1,2},{2,1},{5,6},{6,5},{9,10},{10,9},{13,14},{14,13},{17,18},{18,... | collective-permute-start | bytes 1572872 | tf_op jit(solution)/shard_map/ppermute | solution.py:366
  96.5 20.8 %copy-start.17 = (bf16[128,2048]{1,0:T(8,128)(2,1)}, bf16[128,2048]{1,0:T(8,128)(2,1)S(1)}, u32[]{:S(2)}) copy-start(bf16[128,2048]{1,0:T(8,128)(2,1)S(1)} %collective-permute-done.8.refs_3_) | copy-start | bytes 1572868
  96.5 20.8 %collective-permute-start.9 = (bf16[128,2048]{1,0:T(8,128)(2,1)S(1)}, bf16[128,2048]{1,0:T(8,128)(2,1)S(1)}, u32[]{:S(2)}, u32[]{:S(2)}) collective-permute-start(bf16[128,2048]{1,0:T(8,128)(2,1)S(1)} %collective-permute-done.8.refs_3_), channel_id=1, source_target_pairs={{1,2},{2,1},{5,6},{6,5},{9,10},{10,9},{13,14},{14,13},{17,18},{18,... | collective-permute-start | bytes 1572872 | tf_op jit(solution)/shard_map/ppermute | solution.py:366
  97.2 10.9 %copy-start.20 = (bf16[128,2048]{1,0:T(8,128)(2,1)}, bf16[128,2048]{1,0:T(8,128)(2,1)S(1)}, u32[]{:S(2)}) copy-start(bf16[128,2048]{1,0:T(8,128)(2,1)S(1)} %collective-permute-done.6.refs_5_) | copy-start | bytes 1572868
  97.2 29.9 %collective-permute-start.20 = (bf16[16,4096]{1,0:T(8,128)(2,1)S(1)}, bf16[16,4096]{1,0:T(8,128)(2,1)S(1)}, u32[]{:S(2)}, u32[]{:S(2)}) collective-permute-start(bf16[16,4096]{1,0:T(8,128)(2,1)S(1)} %get-tuple-element.39), channel_id=1, source_target_pairs={{0,24},{4,28},{8,16},{12,20},{16,8},{20,12},{24,0},{28,4},{1,25},{... | collective-permute-start | bytes 393224 | tf_op jit(solution)/shard_map/ppermute | solution.py:344
  106.6 10.7 %copy-start.21 = (bf16[128,2048]{1,0:T(8,128)(2,1)}, bf16[128,2048]{1,0:T(8,128)(2,1)S(1)}, u32[]{:S(2)}) copy-start(bf16[128,2048]{1,0:T(8,128)(2,1)S(1)} %collective-permute-done.7.refs_1_) | copy-start | bytes 1572868
  106.6 20.6 %collective-permute-start.19 = (bf16[16,4096]{1,0:T(8,128)(2,1)S(1)}, bf16[16,4096]{1,0:T(8,128)(2,1)S(1)}, u32[]{:S(2)}, u32[]{:S(2)}) collective-permute-start(bf16[16,4096]{1,0:T(8,128)(2,1)S(1)} %get-tuple-element.40), channel_id=1, source_target_pairs={{0,16},{4,20},{8,24},{12,28},{16,0},{20,4},{24,8},{28,12},{1,17},{... | collective-permute-start | bytes 393224 | tf_op jit(solution)/shard_map/ppermute | solution.py:344
  107.1 1.0 copy-start.24
  107.2 20.0 %collective-permute-start.18 = (bf16[16,4096]{1,0:T(8,128)(2,1)S(1)}, bf16[16,4096]{1,0:T(8,128)(2,1)S(1)}, u32[]{:S(2)}, u32[]{:S(2)}) collective-permute-start(bf16[16,4096]{1,0:T(8,128)(2,1)S(1)} %get-tuple-element.38), channel_id=1, source_target_pairs={{0,8},{4,12},{8,0},{12,4},{16,24},{20,28},{24,16},{28,20},{1,9},{5... | collective-permute-start | bytes 393224 | tf_op jit(solution)/shard_map/ppermute | solution.py:344
  115.9 1.4 copy-start.18
  115.9 18.4 %collective-permute-start.11 = (bf16[16,64,128]{2,1,0:T(8,128)(2,1)}, bf16[16,64,128]{2,1,0:T(8,128)(2,1)S(1)}, u32[]{:S(2)}, u32[]{:S(2)}) collective-permute-start(bf16[16,64,128]{2,1,0:T(8,128)(2,1)} %get-tuple-element.29), channel_id=1, source_target_pairs={{1,0},{2,3},{5,4},{6,7},{9,8},{10,11},{13,12},{14,15},{17,16},{18,... | collective-permute-start | bytes 786440 | tf_op jit(solution)/shard_map/ppermute | solution.py:370
  117.3 0.8 copy-start.23
  125.9 18.0 %collective-permute-start.12 = (bf16[16,64,128]{2,1,0:T(8,128)(2,1)}, bf16[16,64,128]{2,1,0:T(8,128)(2,1)S(1)}, u32[]{:S(2)}, u32[]{:S(2)}) collective-permute-start(bf16[16,64,128]{2,1,0:T(8,128)(2,1)} %get-tuple-element.30), channel_id=1, source_target_pairs={{1,0},{2,3},{5,4},{6,7},{9,8},{10,11},{13,12},{14,15},{17,16},{18,... | collective-permute-start | bytes 786440 | tf_op jit(solution)/shard_map/ppermute | solution.py:370
  127.2 18.0 %copy-start.4 = (bf16[16,4096]{1,0:T(8,128)(2,1)}, bf16[16,4096]{1,0:T(8,128)(2,1)S(1)}, u32[]{:S(2)}) copy-start(bf16[16,4096]{1,0:T(8,128)(2,1)S(1)} %add_convert_fusion.1.refs_4_) | copy-start | bytes 393220
  127.3 18.0 %collective-permute-start.21 = (bf16[16,4096]{1,0:T(8,128)(2,1)S(1)}, bf16[16,4096]{1,0:T(8,128)(2,1)S(1)}, u32[]{:S(2)}, u32[]{:S(2)}) collective-permute-start(bf16[16,4096]{1,0:T(8,128)(2,1)S(1)} %add_convert_fusion.1.refs_4_), channel_id=1, source_target_pairs={{0,1},{1,0},{2,3},{3,2},{4,5},{5,4},{6,7},{7,6},{8,9},{9,8},{10,11... | collective-permute-start | bytes 393224 | tf_op jit(solution)/shard_map/ppermute | solution.py:344
  131.8 13.4 %collective-permute-start.22 = (bf16[16,4096]{1,0:T(8,128)(2,1)S(1)}, bf16[16,4096]{1,0:T(8,128)(2,1)S(1)}, u32[]{:S(2)}, u32[]{:S(2)}) collective-permute-start(bf16[16,4096]{1,0:T(8,128)(2,1)S(1)} %add_convert_fusion.1.refs_4_), channel_id=1, source_target_pairs={{0,2},{1,3},{2,0},{3,1},{4,6},{5,7},{6,4},{7,5},{8,10},{9,11},{10,... | collective-permute-start | bytes 393224 | tf_op jit(solution)/shard_map/ppermute | solution.py:344
  133.0 12.3 %collective-permute-start.23 = (bf16[16,4096]{1,0:T(8,128)(2,1)S(1)}, bf16[16,4096]{1,0:T(8,128)(2,1)S(1)}, u32[]{:S(2)}, u32[]{:S(2)}) collective-permute-start(bf16[16,4096]{1,0:T(8,128)(2,1)S(1)} %add_convert_fusion.1.refs_4_), channel_id=1, source_target_pairs={{0,3},{1,2},{2,1},{3,0},{4,7},{5,6},{6,5},{7,4},{8,11},{9,10},{10,... | collective-permute-start | bytes 393224 | tf_op jit(solution)/shard_map/ppermute | solution.py:344
  134.4 10.9 %copy-start.9 = (bf16[16,64,128]{2,1,0:T(8,128)(2,1)}, bf16[16,64,128]{2,1,0:T(8,128)(2,1)S(1)}, u32[]{:S(2)}) copy-start(bf16[16,64,128]{2,1,0:T(8,128)(2,1)S(1)} %collective-permute-done.11.refs_2_) | copy-start | bytes 786436
  143.8 1.5 copy-start.10
  145.2 0.7 copy-start.15
  145.2 0.7 copy-start.16
  (1 other events, 0.6 us)

commit v2 on v1

v2 whole, which is shorter than its diff:
```python
import functools
import math

import jax
import jax.numpy as jnp
from jax import lax
from jax.experimental import pallas as pl
from jax.experimental.pallas import tpu as pltpu
from jax.sharding import PartitionSpec as P

HEAD = 128
EXP_CAP = 16
LANES = 128
MASKED = -1e30
MIB = 1024 * 1024
VMEM = pl.BlockSpec(memory_space=pltpu.VMEM)


def params(mib, **more):
    return pltpu.CompilerParams(vmem_limit_bytes=mib * MIB, **more)


def held(arrays):
    return [pltpu.with_memory_space_constraint(x, pltpu.VMEM) for x in arrays]


def cost(flops, bytes_accessed, transcendentals=0):
    return pl.CostEstimate(
        flops=int(flops), bytes_accessed=int(bytes_accessed), transcendentals=int(transcendentals)
    )


def strict_upper(size):
    earlier = lax.broadcasted_iota(jnp.int32, (size, size), 0)
    later = lax.broadcasted_iota(jnp.int32, (size, size), 1)
    return (earlier < later).astype(jnp.bfloat16)


def columns(width):
    for chunk in (1024, 512, 256, 128):
        if width % chunk == 0:
            return chunk, width // chunk
    raise ValueError(width)


def route_kernel(n_type, types_ref, mask_ref, tokens_ref, *refs):
    out_refs, select_ref = refs[:n_type], refs[n_type]
    me = lax.axis_index("type")
    step = pl.program_id(0)
    rows, chunk = tokens_ref.shape
    width = out_refs[0].shape[1] - LANES

    @pl.when(step == 0)
    def _():
        types = types_ref[...]
        hot = lax.broadcasted_iota(jnp.int32, (EXP_CAP, rows), 0) == types
        before = jnp.dot(
            hot.astype(jnp.bfloat16), strict_upper(rows), preferred_element_type=jnp.float32
        )
        rank = jnp.sum(jnp.where(hot, before, 0.0), axis=0, keepdims=True).astype(jnp.int32)
        place = jnp.where(rank < EXP_CAP, jnp.bitwise_xor(types, me) * EXP_CAP + rank, -1)
        select_ref[...] = (
            lax.broadcasted_iota(jnp.int32, (n_type * EXP_CAP, rows), 0) == place
        ).astype(jnp.bfloat16)
        lane = lax.broadcasted_iota(jnp.int32, (EXP_CAP, LANES), 1)
        row = lax.broadcasted_iota(jnp.int32, (EXP_CAP, LANES), 0)
        mask_row = jnp.zeros((EXP_CAP, LANES), jnp.int32)
        for j in range(n_type):
            mask_row = jnp.where(lane == j, mask_ref[0, j], mask_row)
        extra = jnp.where(row == 0, types, jnp.where(row == 1, mask_row, 0))
        extra = extra.astype(jnp.float32).astype(jnp.bfloat16)
        for s in range(n_type):
            out_refs[s][:, pl.ds(width, LANES)] = extra

    moved = jnp.dot(select_ref[...], tokens_ref[...], preferred_element_type=jnp.float32).astype(
        jnp.bfloat16
    )
    span = pl.ds(pl.multiple_of(step * chunk, chunk), chunk)
    for s in range(n_type):
        out_refs[s][:, span] = moved[s * EXP_CAP : (s + 1) * EXP_CAP]


def route(n_type, types, mask_row, tokens):
    rows, width = tokens.shape
    wide = width + LANES
    chunk, count = columns(width)
    return pl.pallas_call(
        functools.partial(route_kernel, n_type),
        grid=(count,),
        out_shape=[jax.ShapeDtypeStruct((EXP_CAP, wide), jnp.bfloat16)] * n_type,
        in_specs=[
            VMEM,
            pl.BlockSpec(memory_space=pltpu.SMEM),
            pl.BlockSpec((rows, chunk), lambda i: (0, i)),
        ],
        out_specs=[VMEM] * n_type,
        scratch_shapes=[pltpu.VMEM((n_type * EXP_CAP, rows), jnp.bfloat16)],
        compiler_params=params(8, dimension_semantics=("arbitrary",)),
        cost_estimate=cost(0, 0),
    )(*[pltpu.with_memory_space_constraint(x, pltpu.HBM) for x in (types, mask_row, tokens)])


def fetch_kernel(count, *refs):
    sems = refs[2 * count]
    copies = [pltpu.make_async_copy(refs[i], refs[count + i], sems.at[i]) for i in range(count)]
    for copy in copies:
        copy.start()
    for copy in copies:
        copy.wait()


def fetch(arrays):
    count = len(arrays)
    return pl.pallas_call(
        functools.partial(fetch_kernel, count),
        out_shape=[pltpu.VMEM(x.shape, x.dtype) for x in arrays],
        in_specs=[pl.BlockSpec(memory_space=pl.ANY)] * count,
        out_specs=[VMEM] * count,
        scratch_shapes=[pltpu.SemaphoreType.DMA((count,))],
        compiler_params=params(1),
        cost_estimate=cost(0, 2 * sum(x.size * 2 for x in arrays)),
    )(*[pltpu.with_memory_space_constraint(x, pltpu.HBM) for x in arrays])


def pack_kernel(n_type, *refs):
    in_refs, packed_ref, info_ref = refs[:n_type], refs[n_type], refs[n_type + 1]
    me = lax.axis_index("type")
    width = packed_ref.shape[1]
    tail = pl.ds(width, LANES)
    type_rows = 2 * 8
    row = lax.broadcasted_iota(jnp.int32, (type_rows, LANES), 0)
    upper = strict_upper(LANES)
    extras = [ref[:, tail].astype(jnp.float32) for ref in in_refs]
    types = [e[0:1] for e in extras]
    hots = [row == t.astype(jnp.int32) for t in types]
    befores = [
        jnp.dot(h.astype(jnp.bfloat16), upper, preferred_element_type=jnp.float32) for h in hots
    ]
    counts = [jnp.sum(h.astype(jnp.float32), axis=1, keepdims=True) for h in hots]
    lane16 = lax.broadcasted_iota(jnp.int32, (EXP_CAP, n_type * EXP_CAP), 1)
    slot16 = lax.broadcasted_iota(jnp.int32, (EXP_CAP, n_type * EXP_CAP), 0)
    compact = jnp.zeros((EXP_CAP, n_type * EXP_CAP), jnp.bool_)
    mine = lax.broadcasted_iota(jnp.int32, (type_rows, 1), 0) == me
    info_rows = []
    for s in range(n_type):
        ahead = jnp.zeros((type_rows, 1), jnp.float32)
        for other in range(n_type):
            if other != s:
                first = jnp.bitwise_xor(me, other) < jnp.bitwise_xor(me, s)
                ahead = ahead + jnp.where(first, counts[other], 0.0)
        rank = jnp.sum(jnp.where(hots[s], befores[s] + ahead, 0.0), axis=0, keepdims=True)
        info_rows.append(jnp.where(rank < EXP_CAP, types[s] * EXP_CAP + rank, -1.0))
        offset = jnp.sum(jnp.where(mine, ahead, 0.0)).astype(jnp.int32)
        amount = jnp.sum(jnp.where(mine, counts[s], 0.0)).astype(jnp.int32)
        local = lane16 - s * EXP_CAP
        compact = compact | (
            (local >= 0) & (local < EXP_CAP) & (local < amount) & (local + offset == slot16)
        )
    lane = lax.broadcasted_iota(jnp.int32, (1, LANES), 1)
    for q in range(2):
        for s in range(n_type):
            kept = jnp.sum(
                jnp.where(lane == jnp.bitwise_xor(me, s), extras[q][1:2], 0.0),
                axis=1,
                keepdims=True,
            )
            info_rows.append(jnp.broadcast_to(jnp.where(kept == 1.0, 0.0, MASKED), (1, LANES)))
    for at, info_row in enumerate(info_rows):
        info_ref[at : at + 1, :] = info_row
    compact = compact.astype(jnp.bfloat16)
    chunk, count = columns(width)
    for c in range(count):
        span = pl.ds(c * chunk, chunk)
        rows = jnp.concatenate([ref[:, span] for ref in in_refs], axis=0)
        packed_ref[:, span] = jnp.dot(compact, rows, preferred_element_type=jnp.float32).astype(
            jnp.bfloat16
        )


def pack(n_type, incoming):
    width = incoming[0].shape[1] - LANES
    return pl.pallas_call(
        functools.partial(pack_kernel, n_type),
        out_shape=[
            jax.ShapeDtypeStruct((EXP_CAP, width), jnp.bfloat16),
            jax.ShapeDtypeStruct((3 * n_type, LANES), jnp.float32),
        ],
        in_specs=[VMEM] * n_type,
        out_specs=[VMEM, VMEM],
        compiler_params=params(8),
        cost_estimate=cost(0, 0),
    )(*held(incoming))


def ffn_kernel(near_ref, far_ref, gate_ref, up_ref, down_ref, own_ref, away_ref, x_ref, hidden_ref):
    half = near_ref.shape[0]
    x_ref[:half] = near_ref[...]
    x_ref[half:] = far_ref[...]
    hidden = gate_ref.shape[1]
    for at in range(0, hidden, 256):
        span = pl.ds(at, min(256, hidden - at))
        gate = jnp.dot(x_ref[...], gate_ref[:, span], preferred_element_type=jnp.float32)
        up = jnp.dot(x_ref[...], up_ref[:, span], preferred_element_type=jnp.float32)
        hidden_ref[:, span] = (gate / (1.0 + jnp.exp(-gate)) * up).astype(jnp.bfloat16)
    for at in range(0, down_ref.shape[1], 512):
        span = pl.ds(at, 512)
        out = jnp.dot(hidden_ref[...], down_ref[:, span], preferred_element_type=jnp.float32)
        own_ref[:, span] = out[:half]
        away_ref[:, span] = out[half:].astype(jnp.bfloat16)


def ffn(near, far, gate, up, down):
    half, width = near.shape
    rows = 2 * half
    hidden = gate.shape[1]
    return pl.pallas_call(
        ffn_kernel,
        out_shape=[
            jax.ShapeDtypeStruct((half, width), jnp.float32),
            jax.ShapeDtypeStruct((half, width), jnp.bfloat16),
        ],
        in_specs=[VMEM] * 5,
        out_specs=[VMEM] * 2,
        scratch_shapes=[
            pltpu.VMEM((rows, width), jnp.bfloat16),
            pltpu.VMEM((rows, hidden), jnp.bfloat16),
        ],
        compiler_params=params(16),
        cost_estimate=cost(0, 0),
    )(*held([near, far, gate, up, down]))


def weigh_setup(n_type, tile_ids, query_ids, info_ref, select_ref, mask_ref, pick_ref):
    slots = n_type * EXP_CAP
    tile = select_ref.shape[1] // len(tile_ids)
    row = lax.broadcasted_iota(jnp.int32, (slots + 2 * 8, tile), 0)
    lane = lax.broadcasted_iota(jnp.int32, (tile, HEAD), 1)
    for at, s in enumerate(tile_ids):
        slot = info_ref[s : s + 1, :].astype(jnp.int32)
        select_ref[:, at * tile : (at + 1) * tile] = ((row == slot) | (row == slots)).astype(
            jnp.bfloat16
        )
        mask = jnp.zeros((tile, HEAD), jnp.float32)
        for q in query_ids:
            line = (1 + q) * n_type + s
            mask = jnp.where(lane == q, info_ref[line : line + 1, :], mask)
        mask_ref[at * tile : (at + 1) * tile, :] = mask.astype(jnp.bfloat16)
    for at, q in enumerate(query_ids):
        pick_ref[at * tile : (at + 1) * tile, :] = (lane == q).astype(jnp.bfloat16)


def weigh_scores(keys, queries, mask_ref, pick_ref):
    return lax.dot_general(
        jnp.concatenate([jnp.concatenate(keys, axis=0), mask_ref[...]], axis=1),
        jnp.concatenate([jnp.concatenate(queries, axis=0), pick_ref[...]], axis=1),
        (((1,), (1,)), ((), ())),
        preferred_element_type=jnp.float32,
    )


FACTOR = math.log2(math.e) / math.sqrt(HEAD)


def weigh_begin_kernel(n_type, tile_ids, query_id, info_ref, query_ref, *refs):
    key_refs = refs[: len(tile_ids)]
    state_ref, select_ref, mask_ref, pick_ref = refs[len(tile_ids) :]
    weigh_setup(n_type, tile_ids, [query_id], info_ref, select_ref, mask_ref, pick_ref)
    rows = n_type * EXP_CAP + 8
    tile = query_ref.shape[0]

    def body(h, carry):
        span = pl.ds(pl.multiple_of(h * HEAD, HEAD), HEAD)
        scores = weigh_scores(
            [ref[:, span] for ref in key_refs], [query_ref[:, span]], mask_ref, pick_ref
        )
        top = jnp.max(scores, axis=0, keepdims=True)
        weights = jnp.exp2((scores - top) * FACTOR).astype(jnp.bfloat16)
        picked = jnp.dot(select_ref[...], weights, preferred_element_type=jnp.float32)
        state_ref[h, :rows] = picked[:rows]
        state_ref[h, rows:] = jnp.broadcast_to(top, (8, tile))
        return carry

    lax.fori_loop(0, state_ref.shape[0], body, 0, unroll=4)


def weigh_scratch(n_type, n_tile, n_query, tile):
    return [
        pltpu.VMEM((n_type * EXP_CAP + 2 * 8, n_tile * tile), jnp.bfloat16),
        pltpu.VMEM((n_tile * tile, HEAD), jnp.bfloat16),
        pltpu.VMEM((n_query * tile, HEAD), jnp.bfloat16),
    ]


def weigh_begin(n_type, info, query, query_id, keys, tile_ids):
    tile, width = query.shape
    heads = width // HEAD
    return pl.pallas_call(
        functools.partial(weigh_begin_kernel, n_type, tile_ids, query_id),
        out_shape=jax.ShapeDtypeStruct((heads, n_type * EXP_CAP + 2 * 8, tile), jnp.float32),
        in_specs=[VMEM] * (2 + len(keys)),
        out_specs=VMEM,
        scratch_shapes=weigh_scratch(n_type, len(keys), 1, tile),
        compiler_params=params(8),
        cost_estimate=cost(0, 16 * tile * tile * heads),
    )(*held([info, query, *keys]))


def weigh_end_kernel(n_type, tile_id, first_head, info_ref, key_ref, *refs):
    n_query = (len(refs) - 3) // 3
    query_refs, state_refs = refs[:n_query], refs[n_query : 2 * n_query]
    out_refs = refs[2 * n_query : 3 * n_query]
    select_ref, mask_ref, pick_ref = refs[3 * n_query :]
    weigh_setup(n_type, [tile_id], range(n_query), info_ref, select_ref, mask_ref, pick_ref)
    slots = n_type * EXP_CAP
    rows = slots + 8
    tile = key_ref.shape[0]

    def body(h, carry):
        head = h + first_head
        span = pl.ds(pl.multiple_of(head * HEAD, HEAD), HEAD)
        scores = weigh_scores(
            [key_ref[:, span]], [ref[:, span] for ref in query_refs], mask_ref, pick_ref
        )
        before = jnp.concatenate([ref[head, rows : rows + 1] for ref in state_refs], axis=1)
        top = jnp.maximum(before, jnp.max(scores, axis=0, keepdims=True))
        weights = jnp.exp2((scores - top) * FACTOR).astype(jnp.bfloat16)
        picked = jnp.dot(select_ref[...], weights, preferred_element_type=jnp.float32)[:rows]
        shrink = jnp.exp2((before - top) * FACTOR)
        for q in range(n_query):
            mine = slice(q * tile, (q + 1) * tile)
            total = state_refs[q][head, :rows] * shrink[:, mine] + picked[:, mine]
            out_refs[q][h] = (total[:slots] * (1.0 / total[slots : slots + 1])).astype(jnp.bfloat16)
        return carry

    lax.fori_loop(0, out_refs[0].shape[0], body, 0, unroll=4)


def weigh_end(n_type, info, key, tile_id, queries, states, first_head, heads):
    tile = key.shape[0]
    n_query = len(queries)
    return pl.pallas_call(
        functools.partial(weigh_end_kernel, n_type, tile_id, first_head),
        out_shape=[jax.ShapeDtypeStruct((heads, n_type * EXP_CAP, tile), jnp.bfloat16)] * n_query,
        in_specs=[VMEM] * (2 + 2 * n_query),
        out_specs=[VMEM] * n_query,
        scratch_shapes=weigh_scratch(n_type, 1, n_query, tile),
        compiler_params=params(8),
        cost_estimate=cost(0, 16 * tile * tile * heads),
    )(*held([info, key, *queries, *states]))


def finish_kernel(n_type, n_part, info_ref, *refs):
    own_refs, back_refs = refs[:n_part], refs[n_part : 2 * n_part]
    value_refs = refs[2 * n_part : 2 * n_part + n_type]
    out_ref, attended_ref, value_ref = refs[2 * n_part + n_type :]
    me = lax.axis_index("type")
    ends = (me == 0) | (me == n_type - 1)
    tile = out_ref.shape[0]
    width = out_ref.shape[1]
    for s in range(n_type):
        at = pl.multiple_of(jnp.bitwise_xor(me, s) * EXP_CAP, EXP_CAP)
        value_ref[pl.ds(at, EXP_CAP), :] = value_refs[s][...]
    row = lax.broadcasted_iota(jnp.int32, (n_type * EXP_CAP, tile), 0)
    select = (row == info_ref[0:1, :].astype(jnp.int32)).astype(jnp.bfloat16)
    chunk, count = columns(width)
    contract = (((0,), (0,)), ((), ()))
    for c in range(count):
        span = pl.ds(c * chunk, chunk)
        out_ref[:, span] = lax.dot_general(
            select, value_ref[:, span], contract, preferred_element_type=jnp.float32
        ).astype(jnp.bfloat16)
    at = 0
    for part in range(n_part):
        for h in range(own_refs[part].shape[0]):
            span = pl.ds(at * HEAD, HEAD)
            weights = own_refs[part][h]
            if back_refs:
                weights = jnp.where(ends, back_refs[part][h], weights)
            attended_ref[:, span] = lax.dot_general(
                weights, value_ref[:, span], contract, preferred_element_type=jnp.float32
            ).astype(jnp.bfloat16)
            at += 1


def finish(n_type, info, own, back, values, tile):
    width = values[0].shape[1]
    n_part = len(own)
    return pl.pallas_call(
        functools.partial(finish_kernel, n_type, n_part),
        out_shape=[jax.ShapeDtypeStruct((tile, width), jnp.bfloat16)] * 2,
        in_specs=[VMEM] * (1 + 2 * n_part + n_type),
        out_specs=[VMEM] * 2,
        scratch_shapes=[pltpu.VMEM((n_type * EXP_CAP, width), jnp.bfloat16)],
        compiler_params=params(8),
        cost_estimate=cost(0, 0),
    )(*held([info, *own, *back, *values]))


def swap(x, axis, size, s):
    return lax.ppermute(x, axis, [(i, i ^ s) for i in range(size)])


def as_one_step(fn, *operands):
    shapes = jax.eval_shape(fn, *operands)
    blank = lambda *_: jax.tree.map(lambda x: jnp.zeros(x.shape, x.dtype), shapes)
    return lax.cond(lax.axis_index("type") >= 0, fn, blank, *operands)


def on_device(n_dp, n_type, tokens, token_types, tile_mask, queries, keys, gate_weight, up_weight, down_weight):
    tile, width = tokens.shape
    heads = width // HEAD
    tie = lax.optimization_barrier
    n_same = n_dp // 2
    outgoing = route(n_type, token_types.reshape(1, tile), tile_mask.reshape(1, n_type), tokens)
    incoming = [outgoing[0]] + [swap(outgoing[s], "type", n_type, s) for s in range(1, n_type)]

    def experts(incoming, *weights):
        packed, info = pack(n_type, incoming)
        weights = fetch(weights)
        rows = [packed]
        for p in range(1, n_same):
            low = p & -p
            rows.append(swap(rows[p - low], "dp", n_dp, 2 * low))
        rows, weights = tie((rows, weights))
        same_core = jnp.concatenate(rows, axis=0)
        return info, *ffn(same_core, swap(same_core, "dp", n_dp, 1), *weights)

    def gather_sum(own_rows, away_rows, *beside):
        chip_rows = own_rows + swap(away_rows, "dp", n_dp, 1).astype(jnp.float32)
        chip_rows = chip_rows.astype(jnp.bfloat16)
        pieces = [chip_rows[p * EXP_CAP : (p + 1) * EXP_CAP] for p in range(n_same)]
        pieces = [pieces[0]] + [swap(pieces[p], "dp", n_dp, 2 * p) for p in range(1, n_same)]
        state = None
        if beside:
            info, queries, *tiles = beside
            state = weigh_begin(n_type, info, queries, 0, tiles, [0, 1, 3])
            pieces, state = tie((pieces, state))
        total = pieces[0].astype(jnp.float32)
        for piece in pieces[1:]:
            total = total + piece.astype(jnp.float32)
        return total.astype(jnp.bfloat16), state

    weights = (gate_weight[0], up_weight[0], down_weight[0])
    if n_type == 4:
        to_middle = [(0, 1), (3, 2)]
        across = [(1, 2), (2, 1)]
        to_end = [(1, 0), (2, 3)]
        incoming, keys, queries = tie((incoming, keys, queries))
        near = lax.ppermute(keys, "type", to_middle)
        other = lax.ppermute(keys, "type", across)
        guest = lax.ppermute(queries, "type", to_middle)
        info, own_rows, away_rows = as_one_step(experts, incoming, *weights)
        own_rows, near, other = tie((own_rows, near, other))
        far = lax.ppermute(near, "type", across)
        expert_rows, state = as_one_step(
            gather_sum, own_rows, away_rows, info, queries, keys, near, other
        )
        values = [expert_rows] + [swap(expert_rows, "type", n_type, s) for s in range(1, n_type)]
        expert_rows, guest, far = tie((expert_rows, guest, far))
        guest_state = weigh_begin(n_type, info, guest, 1, [keys, near, other], [0, 1, 3])
        own_weights, back_weights = [], []
        ends = [0, heads // 2, heads - heads // 8, heads]
        for first, last in zip(ends[:-1], ends[1:]):
            own, theirs = weigh_end(
                n_type, info, far, 2, [queries, guest], [state, guest_state], first, last - first
            )
            own_weights.append(own)
            back_weights.append(lax.ppermute(theirs, "type", to_end))
    else:
        info, own_rows, away_rows = experts(incoming, *weights)
        expert_rows, _ = gather_sum(own_rows, away_rows)
        values = [expert_rows] + [swap(expert_rows, "type", n_type, s) for s in range(1, n_type)]
        tiles = [keys] + [swap(keys, "type", n_type, s) for s in range(1, n_type)]
        state = weigh_begin(n_type, info, queries, 0, tiles[:-1], list(range(n_type - 1)))
        own_weights = list(
            weigh_end(n_type, info, tiles[-1], n_type - 1, [queries], [state], 0, heads)
        )
        back_weights = own_weights
    expert_out, attended = finish(n_type, info, own_weights, back_weights, values, tile)
    return (expert_out, attended)


def solution(mesh):
    return jax.shard_map(
        functools.partial(on_device, mesh.shape["dp"], mesh.shape["type"]),
        mesh=mesh,
        in_specs=(
            P(("dp", "type"), None),
            P(("dp", "type"), None),
            P("dp", "type", None),
            P(("dp", "type"), None),
            P(("dp", "type"), None),
            P("type", None, "dp"),
            P("type", None, "dp"),
            P("type", "dp", None),
        ),
        out_specs=(P(("dp", "type"), None), P(("dp", "type"), None)),
        check_vma=False,
    )
```

time: 150 us -> 115 us (0.77)
  waiting for transfers between devices: 61.7 us -> 25.5 us
  Pallas kernels: 40.7 us -> 49.5 us
  starting transfers between devices: 40 us -> 35.7 us
  local copies, waits for them, and re-layouts: 4.26 us -> 2.54 us
    ppermute x6 -> x3, waiting for transfers between devices: 32.5 us -> 2.07 us  [the longest x1 1.66 us: on_device(): near = lax.ppermute(keys, 'type', to_middle)]
    pallas_call x4 -> x8, Pallas kernels: 35.4 us -> 47.3 us  [the longest x2 22.1 us: weigh_begin(): pl.pallas_call(functools.partial(weigh_begin_kernel, n_type, tile_ids, qu...]
    ppermute x2 -> x3, waiting for transfers between devices: 9.45 us -> 0.71 us  [on_device(): back_weights.append(lax.ppermute(theirs, 'type', to_end))]
    ppermute x6 -> x3, starting transfers between devices: 17 us -> 9.76 us  [the longest x1 6.76 us: on_device(): near = lax.ppermute(keys, 'type', to_middle)]
    ppermute x14, waiting for transfers between devices: 19.7 us -> 22.8 us  [swap(): return lax.ppermute(x, axis, [(i, i ^ s) for i in range(size)])]
    unnamed x53 -> x4, local copies, waits for them, and re-layouts: 4.02 us -> 1.23 us
    pallas_call x1, Pallas kernels: 2.17 us -> 0.4 us  [pack(): pl.pallas_call(functools.partial(pack_kernel, n_type), out_shape=[jax.Sha...]
    ppermute x2 -> x3, starting transfers between devices: 2.57 us -> 3.88 us  [on_device(): back_weights.append(lax.ppermute(theirs, 'type', to_end))]
  transfers between devices with their start and end apart: 24 -> 21, of which waited for: 10 -> 10; matrix products, arithmetic and copies ran while one was open for 2% -> 0% of each run, Pallas kernels for 10% -> 25%
where the time goes in v2:
time: 115 us; the launch traced here: 114 us
  Pallas kernels  49.5 us (43%)
  starting transfers between devices  35.7 us (31%)
  waiting for transfers between devices  25.5 us (22%)
  local copies, waits for them, and re-layouts  2.54 us (2%)
    ppermute x14, waiting for transfers between devices, swap(): return lax.ppermute(x, axis, [(i, i ^ s) for i in range(size)])  22.8 us
    pallas_call x2, Pallas kernels, weigh_begin(): pl.pallas_call(functools.partial(weigh_begin_kernel, n_type, tile_ids, qu...  22.1 us
    ppermute x14, starting transfers between devices, swap(): return lax.ppermute(x, axis, [(i, i ^ s) for i in range(size)])  20.4 us
    pallas_call x3, Pallas kernels, weigh_end(): pl.pallas_call(functools.partial(weigh_end_kernel, n_type, tile_id, first...  11.6 us
    pallas_call x1, Pallas kernels, fetch(): pl.pallas_call(functools.partial(fetch_kernel, count), out_shape=[pltpu.V...  7.28 us
    ppermute x1, starting transfers between devices, on_device(): near = lax.ppermute(keys, 'type', to_middle)  6.76 us
    ppermute x3, starting transfers between devices, on_device(): back_weights.append(lax.ppermute(theirs, 'type', to_end))  3.88 us
    pallas_call x1, Pallas kernels, ffn(): pl.pallas_call(ffn_kernel, out_shape=[jax.ShapeDtypeStruct((half, width),...  3.59 us
  transfers between devices with their start and end apart: 21, of which 10 were waited for; matrix products, arithmetic and copies ran while one was open for 0% of the time, Pallas kernels for 25%

profile of v2, /device:TPU:0, one launch (start us, length us, event | category | flops | bytes accessed | tf_op | source)
XLA Modules:
  0.0 114.3 jit_solution(4586273785198721525)
XLA Ops:
  0.6 2.7 %shard_map.98 = (bf16[16,4224]{1,0:T(8,128)(2,1)S(1)}, bf16[16,4224]{1,0:T(8,128)(2,1)S(1)}, bf16[16,4224]{1,0:T(8,128)(2,1)S(1)}, bf16[16,4224]{1,0:T(8,128)(2,1)S(1)}) custom-call(s32[1,128]{1,0:T(1,128)} %bitcast.8, s32[1,4]{1,0:T(1,128)} %bitcast.9, bf16[128,4096]{1,0:T(8,128)(2,1)} %tokens_ref.1), custom_call_target="tpu_custom_call" | custom-call | tf_op jit(solution)/shard_map/pallas_call | solution.py:87
  3.3 3.1 %collective-permute-start.8 = (bf16[16,4224]{1,0:T(8,128)(2,1)S(1)}, bf16[16,4224]{1,0:T(8,128)(2,1)S(1)}, u32[]{:S(2)}, u32[]{:S(2)}) collective-permute-start(bf16[16,4224]{1,0:T(8,128)(2,1)S(1)} %get-tuple-element.93), channel_id=1, source_target_pairs={{0,1},{1,0},{2,3},{3,2},{4,5},{5,4},{6,7},{7,6},{8,9},{9,8},{10,11... | collective-permute-start | bytes 405512 | tf_op jit(solution)/shard_map/ppermute | solution.py:400
  6.4 2.6 %collective-permute-start.9 = (bf16[16,4224]{1,0:T(8,128)(2,1)S(1)}, bf16[16,4224]{1,0:T(8,128)(2,1)S(1)}, u32[]{:S(2)}, u32[]{:S(2)}) collective-permute-start(bf16[16,4224]{1,0:T(8,128)(2,1)S(1)} %get-tuple-element.94), channel_id=1, source_target_pairs={{0,2},{1,3},{2,0},{3,1},{4,6},{5,7},{6,4},{7,5},{8,10},{9,11},{10,... | collective-permute-start | bytes 405512 | tf_op jit(solution)/shard_map/ppermute | solution.py:400
  9.0 0.0 collective-permute-start.10
  9.0 2.6 %collective-permute-done.8 = bf16[16,4224]{1,0:T(8,128)(2,1)S(1)} collective-permute-done((bf16[16,4224]{1,0:T(8,128)(2,1)S(1)}, bf16[16,4224]{1,0:T(8,128)(2,1)S(1)}, u32[]{:S(2)}, u32[]{:S(2)}) %collective-permute-start.8) | collective-permute-done | bytes 135200 | tf_op jit(solution)/shard_map/ppermute | solution.py:400
  11.7 8.0 %collective-permute-done.9 = bf16[16,4224]{1,0:T(8,128)(2,1)S(1)} collective-permute-done((bf16[16,4224]{1,0:T(8,128)(2,1)S(1)}, bf16[16,4224]{1,0:T(8,128)(2,1)S(1)}, u32[]{:S(2)}, u32[]{:S(2)}) %collective-permute-start.9) | collective-permute-done | bytes 135200 | tf_op jit(solution)/shard_map/ppermute | solution.py:400
  19.6 0.0 collective-permute-done.10
  19.6 1.6 %collective-permute-start.12 = (bf16[128,4096]{1,0:T(8,128)(2,1)}, bf16[128,4096]{1,0:T(8,128)(2,1)}, u32[]{:S(2)}, u32[]{:S(2)}) collective-permute-start(bf16[128,4096]{1,0:T(8,128)(2,1)} %refs_0_), channel_id=1, source_target_pairs={{1,2},{2,1},{5,6},{6,5},{9,10},{10,9},{13,14},{14,13},{17,18},{18,... | collective-permute-start | bytes 3145736 | tf_op jit(solution)/shard_map/ppermute | solution.py:450
  21.3 6.8 %collective-permute-start.11 = (bf16[128,4096]{1,0:T(8,128)(2,1)}, bf16[128,4096]{1,0:T(8,128)(2,1)}, u32[]{:S(2)}, u32[]{:S(2)}) collective-permute-start(bf16[128,4096]{1,0:T(8,128)(2,1)} %refs_0_), channel_id=1, source_target_pairs={{0,1},{3,2},{4,5},{7,6},{8,9},{11,10},{12,13},{15,14},{16,17},{19,... | collective-permute-start | bytes 3145736 | tf_op jit(solution)/shard_map/ppermute | solution.py:449
  28.0 1.3 %collective-permute-start.13 = (bf16[128,4096]{1,0:T(8,128)(2,1)}, bf16[128,4096]{1,0:T(8,128)(2,1)S(1)}, u32[]{:S(2)}, u32[]{:S(2)}) collective-permute-start(bf16[128,4096]{1,0:T(8,128)(2,1)} %refs_0_.3), channel_id=1, source_target_pairs={{0,1},{3,2},{4,5},{7,6},{8,9},{11,10},{12,13},{15,14},{16,17},{19,... | collective-permute-start | bytes 3145736 | tf_op jit(solution)/shard_map/ppermute | solution.py:451
  29.4 0.0 copy-start
  29.4 19.9 %conditional.2 = (f32[12,128]{1,0:T(8,128)S(1)}, f32[64,4096]{1,0:T(8,128)S(1)}, bf16[64,4096]{1,0:T(8,128)(2,1)S(1)}) conditional(s32[]{:T(128)} %convert_element_type.25, () %tuple.28, (bf16[16,4224]{1,0:T(8,128)(2,1)S(1)}, bf16[16,4224]{1,0:T(8,128)(2,1)S(1)}, bf16[16,4224]{1,0:T(8,128)(2,1)S(1)}, bf16[16,4224]{1,0:T(8,128)(2,1)S(1)}, ...), branch_computations={%region_0.0_spmd, %region_1.0_spmd} | conditional | bytes 48758968 | solution.py:406
  29.4 0.4 branch_1_fun.4
  29.8 1.6 %collective-permute-start.1 = (bf16[16,4096]{1,0:T(8,128)(2,1)S(1)}, bf16[16,4096]{1,0:T(8,128)(2,1)S(1)}, u32[]{:S(2)}, u32[]{:S(2)}) collective-permute-start(bf16[16,4096]{1,0:T(8,128)(2,1)S(1)} %get-tuple-element.43), channel_id=1, source_target_pairs={{0,16},{4,20},{8,24},{12,28},{16,0},{20,4},{24,8},{28,12},{1,17},{... | collective-permute-start | bytes 393224 | tf_op jit(solution)/shard_map/cond/branch_1_fun/ppermute | solution.py:400
  31.4 1.5 %collective-permute-start = (bf16[16,4096]{1,0:T(8,128)(2,1)S(1)}, bf16[16,4096]{1,0:T(8,128)(2,1)S(1)}, u32[]{:S(2)}, u32[]{:S(2)}) collective-permute-start(bf16[16,4096]{1,0:T(8,128)(2,1)S(1)} %get-tuple-element.43), channel_id=1, source_target_pairs={{0,8},{4,12},{8,0},{12,4},{16,24},{20,28},{24,16},{28,20},{1,9},{5... | collective-permute-start | bytes 393224 | tf_op jit(solution)/shard_map/cond/branch_1_fun/ppermute | solution.py:400
  32.9 2.0 %collective-permute-done.1 = bf16[16,4096]{1,0:T(8,128)(2,1)S(1)} collective-permute-done((bf16[16,4096]{1,0:T(8,128)(2,1)S(1)}, bf16[16,4096]{1,0:T(8,128)(2,1)S(1)}, u32[]{:S(2)}, u32[]{:S(2)}) %collective-permute-start.1) | collective-permute-done | bytes 131104 | tf_op jit(solution)/shard_map/cond/branch_1_fun/ppermute | solution.py:400
  34.9 1.5 %collective-permute-start.2 = (bf16[16,4096]{1,0:T(8,128)(2,1)S(1)}, bf16[16,4096]{1,0:T(8,128)(2,1)S(1)}, u32[]{:S(2)}, u32[]{:S(2)}) collective-permute-start(bf16[16,4096]{1,0:T(8,128)(2,1)S(1)} %collective-permute-done.1), channel_id=1, source_target_pairs={{0,8},{4,12},{8,0},{12,4},{16,24},{20,28},{24,16},{28,20},{1,9},{5... | collective-permute-start | bytes 393224 | tf_op jit(solution)/shard_map/cond/branch_1_fun/ppermute | solution.py:400
  36.4 7.3 %branch_1_fun.5 = (bf16[4096,896]{1,0:T(8,128)(2,1)S(1)}, bf16[4096,896]{1,0:T(8,128)(2,1)S(1)}, bf16[896,4096]{1,0:T(8,128)(2,1)S(1)}) custom-call(bf16[4096,896]{1,0:T(8,128)(2,1)} %bitcast.5, bf16[4096,896]{1,0:T(8,128)(2,1)} %bitcast.6, bf16[896,4096]{1,0:T(8,128)(2,1)} %bitcast.7), custom_call_target="tpu_custom_call" | custom-call | bytes 44040192 | tf_op jit(solution)/shard_map/cond/branch_1_fun/pallas_call | solution.py:114
  43.6 0.0 collective-permute-done
  43.7 0.1 collective-permute-start.3
  43.8 1.9 %collective-permute-done.3.far_ref = bf16[64,4096]{1,0:T(8,128)(2,1)S(1)} collective-permute-done((bf16[64,4096]{1,0:T(8,128)(2,1)S(1)}, bf16[64,4096]{1,0:T(8,128)(2,1)S(1)}, u32[]{:S(2)}, u32[]{:S(2)}) %collective-permute-start.3) | collective-permute-done | bytes 524320 | tf_op jit(solution)/shard_map/cond/branch_1_fun/ppermute | solution.py:400
  45.7 3.6 %branch_1_fun.6 = (f32[64,4096]{1,0:T(8,128)S(1)}, bf16[64,4096]{1,0:T(8,128)(2,1)S(1)}) custom-call(bf16[64,4096]{1,0:T(8,128)(2,1)S(1)} %constant_dynamic-update-slice_fusion.near_ref, bf16[64,4096]{1,0:T(8,128)(2,1)S(1)} %collective-permute-done.3.far_ref, bf16[4096,896]{1,0:T(8,128)(2,1)S(1)} %get-tuple-element.47.gate_ref, ...), custom_call_target="tpu_custom_call" | custom-call | tf_op jit(solution)/shard_map/cond/branch_1_fun/pallas_call | solution.py:216
  49.3 1.7 %collective-permute-done.11.refs_1_ = bf16[128,4096]{1,0:T(8,128)(2,1)} collective-permute-done((bf16[128,4096]{1,0:T(8,128)(2,1)}, bf16[128,4096]{1,0:T(8,128)(2,1)}, u32[]{:S(2)}, u32[]{:S(2)}) %collective-permute-start.11) | collective-permute-done | bytes 1048608 | tf_op jit(solution)/shard_map/ppermute | solution.py:449
  51.0 1.6 %collective-permute-start.14 = (bf16[128,4096]{1,0:T(8,128)(2,1)}, bf16[128,4096]{1,0:T(8,128)(2,1)}, u32[]{:S(2)}, u32[]{:S(2)}) collective-permute-start(bf16[128,4096]{1,0:T(8,128)(2,1)} %collective-permute-done.11.refs_1_), channel_id=1, source_target_pairs={{1,2},{2,1},{5,6},{6,5},{9,10},{10,9},{13,14},{14,13},{17,18},{18,... | collective-permute-start | bytes 3145736 | tf_op jit(solution)/shard_map/ppermute | solution.py:454
  52.6 18.0 %conditional.3 = (bf16[16,4096]{1,0:T(8,128)(2,1)S(1)}, f32[32,80,128]{2,1,0:T(8,128)S(1)}) conditional(s32[]{:T(128)} %convert_element_type.25, () %tuple.31, (bf16[64,4096]{1,0:T(8,128)(2,1)S(1)}, f32[64,4096]{1,0:T(8,128)S(1)}, f32[12,128]{1,0:T(8,128)S(1)}, bf16[128,4096]{1,0:T(8,128)(2,1)S(1)}, bf16[128,4096]{1,0:T(8,128)(2,1)}, ...), branch_computations={%region_2.0_spmd, %region_3.0_spmd} | conditional | flops 1310720 | bytes 20054220 | solution.py:406
  52.6 1.9 %collective-permute-done.4 = bf16[64,4096]{1,0:T(8,128)(2,1)S(1)} collective-permute-done((bf16[64,4096]{1,0:T(8,128)(2,1)S(1)}, bf16[64,4096]{1,0:T(8,128)(2,1)S(1)}, u32[]{:S(2)}, u32[]{:S(2)}) %collective-permute-start.4) | collective-permute-done | bytes 524320 | tf_op jit(solution)/shard_map/cond/branch_1_fun/ppermute | solution.py:400
  54.5 0.1 add_convert_fusion
  54.7 2.5 %collective-permute-start.7 = (bf16[16,4096]{1,0:T(8,128)(2,1)S(1)}, bf16[16,4096]{1,0:T(8,128)(2,1)S(1)}, u32[]{:S(2)}, u32[]{:S(2)}) collective-permute-start(bf16[16,4096]{1,0:T(8,128)(2,1)S(1)} %get-tuple-element.124), channel_id=1, source_target_pairs={{0,24},{4,28},{8,16},{12,20},{16,8},{20,12},{24,0},{28,4},{1,25},{... | collective-permute-start | bytes 393224 | tf_op jit(solution)/shard_map/cond/branch_1_fun/ppermute | solution.py:400
  57.2 0.5 collective-permute-start.6
  57.7 0.5 collective-permute-start.5
  58.2 1.2 %copy-done.2 = bf16[128,4096]{1,0:T(8,128)(2,1)S(1)} copy-done((bf16[128,4096]{1,0:T(8,128)(2,1)S(1)}, bf16[128,4096]{1,0:T(8,128)(2,1)}, u32[]{:S(2)}) %copy-start.2) | copy-done | bytes 1048600 | tf_op jit(solution)/shard_map/cond
  59.4 11.1 %branch_1_fun.7 = f32[32,80,128]{2,1,0:T(8,128)S(1)} custom-call(f32[12,128]{1,0:T(8,128)S(1)} %get-tuple-element.54.info_ref, bf16[128,4096]{1,0:T(8,128)(2,1)S(1)} %get-tuple-element.55.query_ref, bf16[128,4096]{1,0:T(8,128)(2,1)S(1)} %copy-done.2, bf16[128,4096]{1,0:T(8,128)(2,1)} %get-tuple-element.57.refs_1_, bf16[128,4096]{1,0:T(8,128)(2,1)} %get-tuple-element.58.refs_2_), custom_call_target="tpu_custom_call" | custom-call | bytes 8388608 | tf_op jit(solution)/shard_map/cond/branch_1_fun/pallas_call | solution.py:297
  70.5 0.1 add_convert_fusion.1
  70.6 0.4 collective-permute-done.13.query_ref.refs_1_
  71.0 1.2 %copy-done.1 = bf16[128,4096]{1,0:T(8,128)(2,1)S(1)} copy-done((bf16[128,4096]{1,0:T(8,128)(2,1)S(1)}, bf16[128,4096]{1,0:T(8,128)(2,1)}, u32[]{:S(2)}) %copy-start.1) | copy-done | bytes 1048600
  72.2 11.1 %shard_map.99.refs_3_ = f32[32,80,128]{2,1,0:T(8,128)S(1)} custom-call(f32[12,128]{1,0:T(8,128)S(1)} %get-tuple-element.100.info_ref, bf16[128,4096]{1,0:T(8,128)(2,1)S(1)} %collective-permute-done.13.query_ref.refs_1_, bf16[128,4096]{1,0:T(8,128)(2,1)S(1)} %copy-done.1, bf16[128,4096]{1,0:T(8,128)(2,1)} %collective-permute-done.11.refs_1_, ...), custom_call_target="tpu_custom_call" | custom-call | bytes 8388608 | tf_op jit(solution)/shard_map/pallas_call | solution.py:297
  83.3 5.2 %shard_map.100 = (bf16[16,64,128]{2,1,0:T(8,128)(2,1)S(1)}, bf16[16,64,128]{2,1,0:T(8,128)(2,1)S(1)}) custom-call(f32[12,128]{1,0:T(8,128)S(1)} %get-tuple-element.100.info_ref, bf16[128,4096]{1,0:T(8,128)(2,1)} %collective-permute-done.14.key_ref, bf16[128,4096]{1,0:T(8,128)(2,1)S(1)} %copy-done, ...), custom_call_target="tpu_custom_call" | custom-call | bytes 4194304 | tf_op jit(solution)/shard_map/pallas_call | solution.py:341
  88.5 1.3 %collective-permute-start.15 = (bf16[16,64,128]{2,1,0:T(8,128)(2,1)S(1)}, bf16[16,64,128]{2,1,0:T(8,128)(2,1)S(1)}, u32[]{:S(2)}, u32[]{:S(2)}) collective-permute-start(bf16[16,64,128]{2,1,0:T(8,128)(2,1)S(1)} %get-tuple-element.115), channel_id=1, source_target_pairs={{1,0},{2,3},{5,4},{6,7},{9,8},{10,11},{13,12},{14,15},{17,16},{18,... | collective-permute-start | bytes 786440 | tf_op jit(solution)/shard_map/ppermute | solution.py:468
  89.8 1.3 %collective-permute-start.20 = (bf16[16,4096]{1,0:T(8,128)(2,1)S(1)}, bf16[16,4096]{1,0:T(8,128)(2,1)S(1)}, u32[]{:S(2)}, u32[]{:S(2)}) collective-permute-start(bf16[16,4096]{1,0:T(8,128)(2,1)S(1)} %get-tuple-element.108.refs_6_), channel_id=1, source_target_pairs={{0,3},{1,2},{2,1},{3,0},{4,7},{5,6},{6,5},{7,4},{8,11},{9,10},{10,... | collective-permute-start | bytes 393224 | tf_op jit(solution)/shard_map/ppermute | solution.py:400
  91.1 4.2 %shard_map.101 = (bf16[12,64,128]{2,1,0:T(8,128)(2,1)S(1)}, bf16[12,64,128]{2,1,0:T(8,128)(2,1)S(1)}) custom-call(f32[12,128]{1,0:T(8,128)S(1)} %get-tuple-element.100.info_ref, bf16[128,4096]{1,0:T(8,128)(2,1)} %collective-permute-done.14.key_ref, bf16[128,4096]{1,0:T(8,128)(2,1)S(1)} %copy-done, ...), custom_call_target="tpu_custom_call" | custom-call | bytes 3145728 | tf_op jit(solution)/shard_map/pallas_call | solution.py:341
  95.3 1.3 %collective-permute-start.16 = (bf16[12,64,128]{2,1,0:T(8,128)(2,1)S(1)}, bf16[12,64,128]{2,1,0:T(8,128)(2,1)S(1)}, u32[]{:S(2)}, u32[]{:S(2)}) collective-permute-start(bf16[12,64,128]{2,1,0:T(8,128)(2,1)S(1)} %get-tuple-element.116), channel_id=1, source_target_pairs={{1,0},{2,3},{5,4},{6,7},{9,8},{10,11},{13,12},{14,15},{17,16},{18,... | collective-permute-start | bytes 589832 | tf_op jit(solution)/shard_map/ppermute | solution.py:468
  96.6 5.3 %collective-permute-start.19 = (bf16[16,4096]{1,0:T(8,128)(2,1)S(1)}, bf16[16,4096]{1,0:T(8,128)(2,1)S(1)}, u32[]{:S(2)}, u32[]{:S(2)}) collective-permute-start(bf16[16,4096]{1,0:T(8,128)(2,1)S(1)} %get-tuple-element.108.refs_6_), channel_id=1, source_target_pairs={{0,2},{1,3},{2,0},{3,1},{4,6},{5,7},{6,4},{7,5},{8,10},{9,11},{10,... | collective-permute-start | bytes 393224 | tf_op jit(solution)/shard_map/ppermute | solution.py:400
  101.9 2.2 %shard_map.102 = (bf16[4,64,128]{2,1,0:T(8,128)(2,1)S(1)}, bf16[4,64,128]{2,1,0:T(8,128)(2,1)S(1)}) custom-call(f32[12,128]{1,0:T(8,128)S(1)} %get-tuple-element.100.info_ref, bf16[128,4096]{1,0:T(8,128)(2,1)} %collective-permute-done.14.key_ref, bf16[128,4096]{1,0:T(8,128)(2,1)S(1)} %copy-done, ...), custom_call_target="tpu_custom_call" | custom-call | bytes 1048576 | tf_op jit(solution)/shard_map/pallas_call | solution.py:341
  104.1 1.3 %collective-permute-start.17 = (bf16[4,64,128]{2,1,0:T(8,128)(2,1)S(1)}, bf16[4,64,128]{2,1,0:T(8,128)(2,1)S(1)}, u32[]{:S(2)}, u32[]{:S(2)}) collective-permute-start(bf16[4,64,128]{2,1,0:T(8,128)(2,1)S(1)} %get-tuple-element.117), channel_id=1, source_target_pairs={{1,0},{2,3},{5,4},{6,7},{9,8},{10,11},{13,12},{14,15},{17,16},{18,... | collective-permute-start | bytes 196616 | tf_op jit(solution)/shard_map/ppermute | solution.py:468
  105.4 1.0 collective-permute-done.19.refs_8_
  106.4 5.4 %collective-permute-done.18.refs_7_ = bf16[16,4096]{1,0:T(8,128)(2,1)S(1)} collective-permute-done((bf16[16,4096]{1,0:T(8,128)(2,1)S(1)}, bf16[16,4096]{1,0:T(8,128)(2,1)S(1)}, u32[]{:S(2)}, u32[]{:S(2)}) %collective-permute-start.18) | collective-permute-done | bytes 131104 | tf_op jit(solution)/shard_map/ppermute | solution.py:400
  111.8 0.7 collective-permute-done.17.refs_5_
  112.5 1.8 %shard_map.103 = (bf16[128,4096]{1,0:T(8,128)(2,1)}, bf16[128,4096]{1,0:T(8,128)(2,1)}) custom-call(f32[12,128]{1,0:T(8,128)S(1)} %get-tuple-element.100.info_ref, bf16[16,64,128]{2,1,0:T(8,128)(2,1)S(1)} %get-tuple-element.112.refs_0_, bf16[12,64,128]{2,1,0:T(8,128)(2,1)S(1)} %get-tuple-element.113.refs_1_, ...), custom_call_target="tpu_custom_call" | custom-call | tf_op jit(solution)/shard_map/pallas_call | solution.py:388
  (19 shorter events, 0.1 us)
Async XLA Ops:
  3.3 8.3 %collective-permute-start.8 = (bf16[16,4224]{1,0:T(8,128)(2,1)S(1)}, bf16[16,4224]{1,0:T(8,128)(2,1)S(1)}, u32[]{:S(2)}, u32[]{:S(2)}) collective-permute-start(bf16[16,4224]{1,0:T(8,128)(2,1)S(1)} %get-tuple-element.93), channel_id=1, source_target_pairs={{0,1},{1,0},{2,3},{3,2},{4,5},{5,4},{6,7},{7,6},{8,9},{9,8},{10,11... | collective-permute-start | bytes 405512 | tf_op jit(solution)/shard_map/ppermute | solution.py:400
  6.4 13.2 %collective-permute-start.9 = (bf16[16,4224]{1,0:T(8,128)(2,1)S(1)}, bf16[16,4224]{1,0:T(8,128)(2,1)S(1)}, u32[]{:S(2)}, u32[]{:S(2)}) collective-permute-start(bf16[16,4224]{1,0:T(8,128)(2,1)S(1)} %get-tuple-element.94), channel_id=1, source_target_pairs={{0,2},{1,3},{2,0},{3,1},{4,6},{5,7},{6,4},{7,5},{8,10},{9,11},{10,... | collective-permute-start | bytes 405512 | tf_op jit(solution)/shard_map/ppermute | solution.py:400
  9.0 10.6 %collective-permute-start.10 = (bf16[16,4224]{1,0:T(8,128)(2,1)S(1)}, bf16[16,4224]{1,0:T(8,128)(2,1)S(1)}, u32[]{:S(2)}, u32[]{:S(2)}) collective-permute-start(bf16[16,4224]{1,0:T(8,128)(2,1)S(1)} %get-tuple-element.95), channel_id=1, source_target_pairs={{0,3},{1,2},{2,1},{3,0},{4,7},{5,6},{6,5},{7,4},{8,11},{9,10},{10,... | collective-permute-start | bytes 405512 | tf_op jit(solution)/shard_map/ppermute | solution.py:400
  19.6 29.7 %collective-permute-start.12 = (bf16[128,4096]{1,0:T(8,128)(2,1)}, bf16[128,4096]{1,0:T(8,128)(2,1)}, u32[]{:S(2)}, u32[]{:S(2)}) collective-permute-start(bf16[128,4096]{1,0:T(8,128)(2,1)} %refs_0_), channel_id=1, source_target_pairs={{1,2},{2,1},{5,6},{6,5},{9,10},{10,9},{13,14},{14,13},{17,18},{18,... | collective-permute-start | bytes 3145736 | tf_op jit(solution)/shard_map/ppermute | solution.py:450
  21.3 29.7 %collective-permute-start.11 = (bf16[128,4096]{1,0:T(8,128)(2,1)}, bf16[128,4096]{1,0:T(8,128)(2,1)}, u32[]{:S(2)}, u32[]{:S(2)}) collective-permute-start(bf16[128,4096]{1,0:T(8,128)(2,1)} %refs_0_), channel_id=1, source_target_pairs={{0,1},{3,2},{4,5},{7,6},{8,9},{11,10},{12,13},{15,14},{16,17},{19,... | collective-permute-start | bytes 3145736 | tf_op jit(solution)/shard_map/ppermute | solution.py:449
  28.0 43.0 %collective-permute-start.13 = (bf16[128,4096]{1,0:T(8,128)(2,1)}, bf16[128,4096]{1,0:T(8,128)(2,1)S(1)}, u32[]{:S(2)}, u32[]{:S(2)}) collective-permute-start(bf16[128,4096]{1,0:T(8,128)(2,1)} %refs_0_.3), channel_id=1, source_target_pairs={{0,1},{3,2},{4,5},{7,6},{8,9},{11,10},{12,13},{15,14},{16,17},{19,... | collective-permute-start | bytes 3145736 | tf_op jit(solution)/shard_map/ppermute | solution.py:451
  29.4 23.2 %copy-start = (bf16[128,4096]{1,0:T(8,128)(2,1)S(1)}, bf16[128,4096]{1,0:T(8,128)(2,1)}, u32[]{:S(2)}) copy-start(bf16[128,4096]{1,0:T(8,128)(2,1)} %refs_0_.3) | copy-start | bytes 3145732
  29.8 5.0 %collective-permute-start.1 = (bf16[16,4096]{1,0:T(8,128)(2,1)S(1)}, bf16[16,4096]{1,0:T(8,128)(2,1)S(1)}, u32[]{:S(2)}, u32[]{:S(2)}) collective-permute-start(bf16[16,4096]{1,0:T(8,128)(2,1)S(1)} %get-tuple-element.43), channel_id=1, source_target_pairs={{0,16},{4,20},{8,24},{12,28},{16,0},{20,4},{24,8},{28,12},{1,17},{... | collective-permute-start | bytes 393224 | tf_op jit(solution)/shard_map/cond/branch_1_fun/ppermute | solution.py:400
  31.4 12.2 %collective-permute-start = (bf16[16,4096]{1,0:T(8,128)(2,1)S(1)}, bf16[16,4096]{1,0:T(8,128)(2,1)S(1)}, u32[]{:S(2)}, u32[]{:S(2)}) collective-permute-start(bf16[16,4096]{1,0:T(8,128)(2,1)S(1)} %get-tuple-element.43), channel_id=1, source_target_pairs={{0,8},{4,12},{8,0},{12,4},{16,24},{20,28},{24,16},{28,20},{1,9},{5... | collective-permute-start | bytes 393224 | tf_op jit(solution)/shard_map/cond/branch_1_fun/ppermute | solution.py:400
  34.9 8.8 %collective-permute-start.2 = (bf16[16,4096]{1,0:T(8,128)(2,1)S(1)}, bf16[16,4096]{1,0:T(8,128)(2,1)S(1)}, u32[]{:S(2)}, u32[]{:S(2)}) collective-permute-start(bf16[16,4096]{1,0:T(8,128)(2,1)S(1)} %collective-permute-done.1), channel_id=1, source_target_pairs={{0,8},{4,12},{8,0},{12,4},{16,24},{20,28},{24,16},{28,20},{1,9},{5... | collective-permute-start | bytes 393224 | tf_op jit(solution)/shard_map/cond/branch_1_fun/ppermute | solution.py:400
  43.7 2.0 %collective-permute-start.3 = (bf16[64,4096]{1,0:T(8,128)(2,1)S(1)}, bf16[64,4096]{1,0:T(8,128)(2,1)S(1)}, u32[]{:S(2)}, u32[]{:S(2)}) collective-permute-start(bf16[64,4096]{1,0:T(8,128)(2,1)S(1)} %constant_dynamic-update-slice_fusion.near_ref), channel_id=1, source_target_pairs={{0,4},{4,0},{8,12},{12,8},{16,20},{20,16},{24,28},{28,24},{1,5},{5... | collective-permute-start | bytes 1572872 | tf_op jit(solution)/shard_map/cond/branch_1_fun/ppermute | solution.py:400
  51.0 20.0 %collective-permute-start.14 = (bf16[128,4096]{1,0:T(8,128)(2,1)}, bf16[128,4096]{1,0:T(8,128)(2,1)}, u32[]{:S(2)}, u32[]{:S(2)}) collective-permute-start(bf16[128,4096]{1,0:T(8,128)(2,1)} %collective-permute-done.11.refs_1_), channel_id=1, source_target_pairs={{1,2},{2,1},{5,6},{6,5},{9,10},{10,9},{13,14},{14,13},{17,18},{18,... | collective-permute-start | bytes 3145736 | tf_op jit(solution)/shard_map/ppermute | solution.py:454
  52.6 1.9 %collective-permute-start.4 = (bf16[64,4096]{1,0:T(8,128)(2,1)S(1)}, bf16[64,4096]{1,0:T(8,128)(2,1)S(1)}, u32[]{:S(2)}, u32[]{:S(2)}) collective-permute-start(bf16[64,4096]{1,0:T(8,128)(2,1)S(1)} %get-tuple-element.53), channel_id=1, source_target_pairs={{0,4},{4,0},{8,12},{12,8},{16,20},{20,16},{24,28},{28,24},{1,5},{5... | collective-permute-start | bytes 1572872 | tf_op jit(solution)/shard_map/cond/branch_1_fun/ppermute | solution.py:400
  54.7 15.8 %collective-permute-start.7 = (bf16[16,4096]{1,0:T(8,128)(2,1)S(1)}, bf16[16,4096]{1,0:T(8,128)(2,1)S(1)}, u32[]{:S(2)}, u32[]{:S(2)}) collective-permute-start(bf16[16,4096]{1,0:T(8,128)(2,1)S(1)} %get-tuple-element.124), channel_id=1, source_target_pairs={{0,24},{4,28},{8,16},{12,20},{16,8},{20,12},{24,0},{28,4},{1,25},{... | collective-permute-start | bytes 393224 | tf_op jit(solution)/shard_map/cond/branch_1_fun/ppermute | solution.py:400
  57.2 13.3 %collective-permute-start.6 = (bf16[16,4096]{1,0:T(8,128)(2,1)S(1)}, bf16[16,4096]{1,0:T(8,128)(2,1)S(1)}, u32[]{:S(2)}, u32[]{:S(2)}) collective-permute-start(bf16[16,4096]{1,0:T(8,128)(2,1)S(1)} %get-tuple-element.125), channel_id=1, source_target_pairs={{0,16},{4,20},{8,24},{12,28},{16,0},{20,4},{24,8},{28,12},{1,17},{... | collective-permute-start | bytes 393224 | tf_op jit(solution)/shard_map/cond/branch_1_fun/ppermute | solution.py:400
  57.7 12.8 %collective-permute-start.5 = (bf16[16,4096]{1,0:T(8,128)(2,1)S(1)}, bf16[16,4096]{1,0:T(8,128)(2,1)S(1)}, u32[]{:S(2)}, u32[]{:S(2)}) collective-permute-start(bf16[16,4096]{1,0:T(8,128)(2,1)S(1)} %get-tuple-element.126), channel_id=1, source_target_pairs={{0,8},{4,12},{8,0},{12,4},{16,24},{20,28},{24,16},{28,20},{1,9},{5... | collective-permute-start | bytes 393224 | tf_op jit(solution)/shard_map/cond/branch_1_fun/ppermute | solution.py:400
  58.2 1.2 %copy-start.2 = (bf16[128,4096]{1,0:T(8,128)(2,1)S(1)}, bf16[128,4096]{1,0:T(8,128)(2,1)}, u32[]{:S(2)}) copy-start(bf16[128,4096]{1,0:T(8,128)(2,1)} %get-tuple-element.56.refs_0_) | copy-start | bytes 3145732 | tf_op jit(solution)/shard_map/cond
  71.0 1.2 %copy-start.1 = (bf16[128,4096]{1,0:T(8,128)(2,1)S(1)}, bf16[128,4096]{1,0:T(8,128)(2,1)}, u32[]{:S(2)}) copy-start(bf16[128,4096]{1,0:T(8,128)(2,1)} %refs_0_) | copy-start | bytes 3145732
  88.5 24.0 %collective-permute-start.15 = (bf16[16,64,128]{2,1,0:T(8,128)(2,1)S(1)}, bf16[16,64,128]{2,1,0:T(8,128)(2,1)S(1)}, u32[]{:S(2)}, u32[]{:S(2)}) collective-permute-start(bf16[16,64,128]{2,1,0:T(8,128)(2,1)S(1)} %get-tuple-element.115), channel_id=1, source_target_pairs={{1,0},{2,3},{5,4},{6,7},{9,8},{10,11},{13,12},{14,15},{17,16},{18,... | collective-permute-start | bytes 786440 | tf_op jit(solution)/shard_map/ppermute | solution.py:468
  89.8 14.3 %collective-permute-start.20 = (bf16[16,4096]{1,0:T(8,128)(2,1)S(1)}, bf16[16,4096]{1,0:T(8,128)(2,1)S(1)}, u32[]{:S(2)}, u32[]{:S(2)}) collective-permute-start(bf16[16,4096]{1,0:T(8,128)(2,1)S(1)} %get-tuple-element.108.refs_6_), channel_id=1, source_target_pairs={{0,3},{1,2},{2,1},{3,0},{4,7},{5,6},{6,5},{7,4},{8,11},{9,10},{10,... | collective-permute-start | bytes 393224 | tf_op jit(solution)/shard_map/ppermute | solution.py:400
  95.3 17.2 %collective-permute-start.16 = (bf16[12,64,128]{2,1,0:T(8,128)(2,1)S(1)}, bf16[12,64,128]{2,1,0:T(8,128)(2,1)S(1)}, u32[]{:S(2)}, u32[]{:S(2)}) collective-permute-start(bf16[12,64,128]{2,1,0:T(8,128)(2,1)S(1)} %get-tuple-element.116), channel_id=1, source_target_pairs={{1,0},{2,3},{5,4},{6,7},{9,8},{10,11},{13,12},{14,15},{17,16},{18,... | collective-permute-start | bytes 589832 | tf_op jit(solution)/shard_map/ppermute | solution.py:468
  96.6 9.8 %collective-permute-start.19 = (bf16[16,4096]{1,0:T(8,128)(2,1)S(1)}, bf16[16,4096]{1,0:T(8,128)(2,1)S(1)}, u32[]{:S(2)}, u32[]{:S(2)}) collective-permute-start(bf16[16,4096]{1,0:T(8,128)(2,1)S(1)} %get-tuple-element.108.refs_6_), channel_id=1, source_target_pairs={{0,2},{1,3},{2,0},{3,1},{4,6},{5,7},{6,4},{7,5},{8,10},{9,11},{10,... | collective-permute-start | bytes 393224 | tf_op jit(solution)/shard_map/ppermute | solution.py:400
  101.9 9.9 %collective-permute-start.18 = (bf16[16,4096]{1,0:T(8,128)(2,1)S(1)}, bf16[16,4096]{1,0:T(8,128)(2,1)S(1)}, u32[]{:S(2)}, u32[]{:S(2)}) collective-permute-start(bf16[16,4096]{1,0:T(8,128)(2,1)S(1)} %get-tuple-element.108.refs_6_), channel_id=1, source_target_pairs={{0,1},{1,0},{2,3},{3,2},{4,5},{5,4},{6,7},{7,6},{8,9},{9,8},{10,11... | collective-permute-start | bytes 393224 | tf_op jit(solution)/shard_map/ppermute | solution.py:400
  104.1 8.4 %collective-permute-start.17 = (bf16[4,64,128]{2,1,0:T(8,128)(2,1)S(1)}, bf16[4,64,128]{2,1,0:T(8,128)(2,1)S(1)}, u32[]{:S(2)}, u32[]{:S(2)}) collective-permute-start(bf16[4,64,128]{2,1,0:T(8,128)(2,1)S(1)} %get-tuple-element.117), channel_id=1, source_target_pairs={{1,0},{2,3},{5,4},{6,7},{9,8},{10,11},{13,12},{14,15},{17,16},{18,... | collective-permute-start | bytes 196616 | tf_op jit(solution)/shard_map/ppermute | solution.py:468

commit v3 on v2

--- a/solution.py
+++ b/solution.py
@@ -230,136 +230,187 @@
     )(*held([near, far, gate, up, down]))
 
 
-def weigh_setup(n_type, tile_ids, query_ids, info_ref, select_ref, mask_ref, pick_ref):
-    slots = n_type * EXP_CAP
-    tile = select_ref.shape[1] // len(tile_ids)
-    row = lax.broadcasted_iota(jnp.int32, (slots + 2 * 8, tile), 0)
-    lane = lax.broadcasted_iota(jnp.int32, (tile, HEAD), 1)
-    for at, s in enumerate(tile_ids):
-        slot = info_ref[s : s + 1, :].astype(jnp.int32)
-        select_ref[:, at * tile : (at + 1) * tile] = ((row == slot) | (row == slots)).astype(
-            jnp.bfloat16
-        )
-        mask = jnp.zeros((tile, HEAD), jnp.float32)
-        for q in query_ids:
-            line = (1 + q) * n_type + s
-            mask = jnp.where(lane == q, info_ref[line : line + 1, :], mask)
-        mask_ref[at * tile : (at + 1) * tile, :] = mask.astype(jnp.bfloat16)
-    for at, q in enumerate(query_ids):
-        pick_ref[at * tile : (at + 1) * tile, :] = (lane == q).astype(jnp.bfloat16)
-
-
-def weigh_scores(keys, queries, mask_ref, pick_ref):
+FACTOR = math.log2(math.e) / math.sqrt(HEAD)
+
+
+def slots_of(slots, tile, s, info_ref):
+    row = lax.broadcasted_iota(jnp.int32, (slots, tile), 0)
+    return row == info_ref[s : s + 1, :].astype(jnp.int32)
+
+
+def mask_row(n_type, q, s, info_ref):
+    line = (1 + q) * n_type + s
+    return info_ref[line : line + 1, :]
+
+
+def product(rows, queries):
     return lax.dot_general(
-        jnp.concatenate([jnp.concatenate(keys, axis=0), mask_ref[...]], axis=1),
-        jnp.concatenate([jnp.concatenate(queries, axis=0), pick_ref[...]], axis=1),
-        (((1,), (1,)), ((), ())),
+        rows, queries, (((1,), (1,)), ((), ())), preferred_element_type=jnp.float32
+    )
+
+
+def pair_of(query):
+    lane = lax.broadcasted_iota(jnp.int32, query.shape, 1)
+    zero = jnp.zeros_like(query)
+    return jnp.concatenate(
+        [jnp.where(lane < HEAD, query, zero), jnp.where(lane >= HEAD, query, zero)], axis=0
+    )
+
+
+def pair_scores(n_type, q, tile_ids, info_ref, key_refs, query_ref, span):
+    tile = query_ref.shape[0]
+    scores = product(
+        jnp.concatenate([ref[:, span] for ref in key_refs], axis=0), pair_of(query_ref[:, span])
+    )
+    scores = [scores[i * tile : (i + 1) * tile] for i in range(len(tile_ids))]
+    masks = [mask_row(n_type, q, s, info_ref) for s in tile_ids]
+    return [x + jnp.concatenate([m, m], axis=1) for x, m in zip(scores, masks)]
+
+
+def top_of(scores):
+    return functools.reduce(jnp.maximum, [jnp.max(x, axis=0, keepdims=True) for x in scores])
+
+
+def total_of(scores, top):
+    return sum(jnp.sum(jnp.exp2((x - top) * FACTOR), axis=0, keepdims=True) for x in scores)
+
+
+def weigh_begin_kernel(n_type, tile_ids, info_ref, query_ref, *refs):
+    key_refs = refs[: len(tile_ids)]
+    state_ref, kept_ref = refs[len(tile_ids) :]
+    slots, width = kept_ref.shape
+    tile = query_ref.shape[0]
+    select = [slots_of(slots, tile, s, info_ref).astype(jnp.bfloat16) for s in tile_ids]
+    kept_ref[...] = jnp.dot(
+        jnp.concatenate(select, axis=1),
+        jnp.concatenate([ref[...] for ref in key_refs], axis=0),
         preferred_element_type=jnp.float32,
-    )
-
-
-FACTOR = math.log2(math.e) / math.sqrt(HEAD)
-
-
-def weigh_begin_kernel(n_type, tile_ids, query_id, info_ref, query_ref, *refs):
-    key_refs = refs[: len(tile_ids)]
-    state_ref, select_ref, mask_ref, pick_ref = refs[len(tile_ids) :]
-    weigh_setup(n_type, tile_ids, [query_id], info_ref, select_ref, mask_ref, pick_ref)
-    rows = n_type * EXP_CAP + 8
-    tile = query_ref.shape[0]
-
-    def body(h, carry):
-        span = pl.ds(pl.multiple_of(h * HEAD, HEAD), HEAD)
-        scores = weigh_scores(
-            [ref[:, span] for ref in key_refs], [query_ref[:, span]], mask_ref, pick_ref
-        )
-        top = jnp.max(scores, axis=0, keepdims=True)
-        weights = jnp.exp2((scores - top) * FACTOR).astype(jnp.bfloat16)
-        picked = jnp.dot(select_ref[...], weights, preferred_element_type=jnp.float32)
-        state_ref[h, :rows] = picked[:rows]
-        state_ref[h, rows:] = jnp.broadcast_to(top, (8, tile))
-        return carry
-
-    lax.fori_loop(0, state_ref.shape[0], body, 0, unroll=4)
-
-
-def weigh_scratch(n_type, n_tile, n_query, tile):
-    return [
-        pltpu.VMEM((n_type * EXP_CAP + 2 * 8, n_tile * tile), jnp.bfloat16),
-        pltpu.VMEM((n_tile * tile, HEAD), jnp.bfloat16),
-        pltpu.VMEM((n_query * tile, HEAD), jnp.bfloat16),
-    ]
-
-
-def weigh_begin(n_type, info, query, query_id, keys, tile_ids):
+    ).astype(jnp.bfloat16)
+    for at in range(0, width, 2 * HEAD):
+        span = pl.ds(at, 2 * HEAD)
+        scores = pair_scores(n_type, 0, tile_ids, info_ref, key_refs, query_ref, span)
+        top = top_of(scores)
+        total = total_of(scores, top)
+        for i in range(2):
+            mine = slice(i * tile, (i + 1) * tile)
+            head = at // HEAD + i
+            state_ref[head, :8] = jnp.broadcast_to(total[:, mine], (8, tile))
+            state_ref[head, 8:] = jnp.broadcast_to(top[:, mine], (8, tile))
+
+
+PER_STEP = 4
+
+
+def weigh_begin(n_type, info, query, keys, tile_ids):
     tile, width = query.shape
     heads = width // HEAD
-    return pl.pallas_call(
-        functools.partial(weigh_begin_kernel, n_type, tile_ids, query_id),
-        out_shape=jax.ShapeDtypeStruct((heads, n_type * EXP_CAP + 2 * 8, tile), jnp.float32),
-        in_specs=[VMEM] * (2 + len(keys)),
-        out_specs=VMEM,
-        scratch_shapes=weigh_scratch(n_type, len(keys), 1, tile),
-        compiler_params=params(8),
+    slots = n_type * EXP_CAP
+    block = pl.BlockSpec((tile, PER_STEP * HEAD), lambda i: (0, i))
+    return pl.pallas_call(
+        functools.partial(weigh_begin_kernel, n_type, tile_ids),
+        grid=(heads // PER_STEP,),
+        out_shape=[
+            jax.ShapeDtypeStruct((heads, 2 * 8, tile), jnp.float32),
+            jax.ShapeDtypeStruct((slots, width), jnp.bfloat16),
+        ],
+        in_specs=[VMEM] + [block] * (1 + len(keys)),
+        out_specs=[
+            pl.BlockSpec((PER_STEP, 2 * 8, tile), lambda i: (i, 0, 0)),
+            pl.BlockSpec((slots, PER_STEP * HEAD), lambda i: (0, i)),
+        ],
+        compiler_params=params(16, dimension_semantics=("arbitrary",)),
+        cost_estimate=cost(0, 0),
+    )(info, query, *keys)
+
+
+def weigh_end_kernel(n_type, n_query, tile_ids, info_ref, kept_ref, state_ref, last_ref, *refs):
+    query_refs, refs = refs[:n_query], refs[n_query:]
+    n_key = len(refs) - n_query - 1
+    key_refs, refs = refs[:n_key], refs[n_key:]
+    out_refs, bias_ref = refs[:n_query], refs[n_query]
+    slots, width = kept_ref.shape
+    tile = last_ref.shape[0]
+
+    @pl.when(pl.program_id(0) == 0)
+    def _():
+        bias = [jnp.full((slots, tile), MASKED, jnp.float32) for _ in range(n_query)]
+        for s in tile_ids:
+            chosen = slots_of(slots, tile, s, info_ref).astype(jnp.float32)
+            filled = jnp.max(chosen, axis=1, keepdims=True)
+            for q in range(n_query):
+                bias[q] = jnp.where(filled > 0.0, mask_row(n_type, q, s, info_ref), bias[q])
+        for q in range(n_query):
+            bias_ref[:, q * tile : (q + 1) * tile] = bias[q]
+
+    select = slots_of(slots, tile, tile_ids[-1], info_ref).astype(jnp.bfloat16)
+    found = jnp.dot(select, last_ref[...], preferred_element_type=jnp.float32)
+    kept = (kept_ref[...].astype(jnp.float32) + found).astype(jnp.bfloat16)
+    last_mask = jnp.concatenate(
+        [mask_row(n_type, q, tile_ids[-1], info_ref) for q in range(n_query)], axis=1
+    )
+    for at in range(0, width, 2 * HEAD):
+        if n_query > 1:
+            rest = pair_scores(
+                n_type, 1, tile_ids[:-1], info_ref, key_refs, query_refs[1], pl.ds(at, 2 * HEAD)
+            )
+            rest_top = top_of(rest)
+        for i in range(2):
+            mine = slice(i * tile, (i + 1) * tile)
+            head = at // HEAD + i
+            span = slice(head * HEAD, (head + 1) * HEAD)
+            scores = product(
+                jnp.concatenate([last_ref[:, span], kept[:, span]], axis=0),
+                jnp.concatenate([ref[:, span] for ref in query_refs], axis=0),
+            )
+            last = scores[:tile] + last_mask
+            state_top = state_ref[head, 8:9]
+            tops = [state_top] + ([rest_top[:, mine]] if n_query > 1 else [])
+            top = jnp.maximum(jnp.concatenate(tops, axis=1), jnp.max(last, axis=0, keepdims=True))
+            own_top = top[:, :tile]
+            before = [state_ref[head, 0:1] * jnp.exp2((state_top - own_top) * FACTOR)]
+            if n_query > 1:
+                before.append(total_of([x[:, mine] for x in rest], top[:, tile:]))
+            total = total_of([last], top) + jnp.concatenate(before, axis=1)
+            weights = jnp.exp2((scores[tile:] + bias_ref[...] - top) * FACTOR) * (1.0 / total)
+            for q in range(n_query):
+                out_refs[q][head] = weights[:, q * tile : (q + 1) * tile].astype(jnp.bfloat16)
+
+
+def weigh_end(n_type, info, begun, last_key, queries, keys, tile_ids, first_head, heads):
+    state, kept = begun
+    tile = last_key.shape[0]
+    n_query = len(queries)
+    slots = n_type * EXP_CAP
+    first = first_head // PER_STEP
+    block = pl.BlockSpec((tile, PER_STEP * HEAD), lambda i: (0, i + first))
+    out_block = pl.BlockSpec((PER_STEP, slots, tile), lambda i: (i, 0, 0))
+    return pl.pallas_call(
+        functools.partial(weigh_end_kernel, n_type, n_query, tile_ids),
+        grid=(heads // PER_STEP,),
+        out_shape=[jax.ShapeDtypeStruct((heads, slots, tile), jnp.bfloat16)] * n_query,
+        in_specs=[
+            VMEM,
+            pl.BlockSpec((slots, PER_STEP * HEAD), lambda i: (0, i + first)),
+            pl.BlockSpec((PER_STEP, 2 * 8, tile), lambda i: (i + first, 0, 0)),
+        ]
+        + [block] * (1 + n_query + len(keys)),
+        out_specs=[out_block] * n_query,
+        scratch_shapes=[pltpu.VMEM((slots, n_query * tile), jnp.float32)],
+        compiler_params=params(16, dimension_semantics=("arbitrary",)),
         cost_estimate=cost(0, 16 * tile * tile * heads),
-    )(*held([info, query, *keys]))
-
-
-def weigh_end_kernel(n_type, tile_id, first_head, info_ref, key_ref, *refs):
-    n_query = (len(refs) - 3) // 3
-    query_refs, state_refs = refs[:n_query], refs[n_query : 2 * n_query]
-    out_refs = refs[2 * n_query : 3 * n_query]
-    select_ref, mask_ref, pick_ref = refs[3 * n_query :]
-    weigh_setup(n_type, [tile_id], range(n_query), info_ref, select_ref, mask_ref, pick_ref)
-    slots = n_type * EXP_CAP
-    rows = slots + 8
-    tile = key_ref.shape[0]
-
-    def body(h, carry):
-        head = h + first_head
-        span = pl.ds(pl.multiple_of(head * HEAD, HEAD), HEAD)
-        scores = weigh_scores(
-            [key_ref[:, span]], [ref[:, span] for ref in query_refs], mask_ref, pick_ref
-        )
-        before = jnp.concatenate([ref[head, rows : rows + 1] for ref in state_refs], axis=1)
-        top = jnp.maximum(before, jnp.max(scores, axis=0, keepdims=True))
-        weights = jnp.exp2((scores - top) * FACTOR).astype(jnp.bfloat16)
-        picked = jnp.dot(select_ref[...], weights, preferred_element_type=jnp.float32)[:rows]
-        shrink = jnp.exp2((before - top) * FACTOR)
-        for q in range(n_query):
-            mine = slice(q * tile, (q + 1) * tile)
-            total = state_refs[q][head, :rows] * shrink[:, mine] + picked[:, mine]
-            out_refs[q][h] = (total[:slots] * (1.0 / total[slots : slots + 1])).astype(jnp.bfloat16)
-        return carry
-
-    lax.fori_loop(0, out_refs[0].shape[0], body, 0, unroll=4)
-
-
-def weigh_end(n_type, info, key, tile_id, queries, states, first_head, heads):
-    tile = key.shape[0]
-    n_query = len(queries)
-    return pl.pallas_call(
-        functools.partial(weigh_end_kernel, n_type, tile_id, first_head),
-        out_shape=[jax.ShapeDtypeStruct((heads, n_type * EXP_CAP, tile), jnp.bfloat16)] * n_query,
-        in_specs=[VMEM] * (2 + 2 * n_query),
-        out_specs=[VMEM] * n_query,
-        scratch_shapes=weigh_scratch(n_type, 1, n_query, tile),
-        compiler_params=params(8),
-        cost_estimate=cost(0, 16 * tile * tile * heads),
-    )(*held([info, key, *queries, *states]))
+    )(info, kept, state, last_key, *queries, *keys)
 
 
 def finish_kernel(n_type, n_part, info_ref, *refs):
     own_refs, back_refs = refs[:n_part], refs[n_part : 2 * n_part]
-    value_refs = refs[2 * n_part : 2 * n_part + n_type]
-    out_ref, attended_ref, value_ref = refs[2 * n_part + n_type :]
+    values_ref, out_ref, attended_ref, value_ref = refs[2 * n_part :]
     me = lax.axis_index("type")
     ends = (me == 0) | (me == n_type - 1)
     tile = out_ref.shape[0]
     width = out_ref.shape[1]
     for s in range(n_type):
         at = pl.multiple_of(jnp.bitwise_xor(me, s) * EXP_CAP, EXP_CAP)
-        value_ref[pl.ds(at, EXP_CAP), :] = value_refs[s][...]
+        value_ref[pl.ds(at, EXP_CAP), :] = values_ref[s * EXP_CAP : (s + 1) * EXP_CAP]
     row = lax.broadcasted_iota(jnp.int32, (n_type * EXP_CAP, tile), 0)
     select = (row == info_ref[0:1, :].astype(jnp.int32)).astype(jnp.bfloat16)
     chunk, count = columns(width)
@@ -383,17 +434,17 @@
 
 
 def finish(n_type, info, own, back, values, tile):
-    width = values[0].shape[1]
+    width = values.shape[1]
     n_part = len(own)
     return pl.pallas_call(
         functools.partial(finish_kernel, n_type, n_part),
         out_shape=[jax.ShapeDtypeStruct((tile, width), jnp.bfloat16)] * 2,
-        in_specs=[VMEM] * (1 + 2 * n_part + n_type),
+        in_specs=[VMEM] * (2 + 2 * n_part),
         out_specs=[VMEM] * 2,
         scratch_shapes=[pltpu.VMEM((n_type * EXP_CAP, width), jnp.bfloat16)],
         compiler_params=params(8),
         cost_estimate=cost(0, 0),
-    )(*held([info, *own, *back, *values]))
+    )(*held([info, *own, *back, values]))
 
 
 def swap(x, axis, size, s):
@@ -430,15 +481,22 @@
         chip_rows = chip_rows.astype(jnp.bfloat16)
         pieces = [chip_rows[p * EXP_CAP : (p + 1) * EXP_CAP] for p in range(n_same)]
         pieces = [pieces[0]] + [swap(pieces[p], "dp", n_dp, 2 * p) for p in range(1, n_same)]
-        state = None
+        begun = None
         if beside:
-            info, queries, *tiles = beside
-            state = weigh_begin(n_type, info, queries, 0, tiles, [0, 1, 3])
-            pieces, state = tie((pieces, state))
+            begun = weigh_begin(n_type, *beside, [0, 1, 3])
+            pieces, begun = tie((pieces, begun))
         total = pieces[0].astype(jnp.float32)
         for piece in pieces[1:]:
             total = total + piece.astype(jnp.float32)
-        return total.astype(jnp.bfloat16), state
+        expert_rows = total.astype(jnp.bfloat16)
+        return jnp.concatenate([expert_rows, swap(expert_rows, "type", n_type, 1)], axis=0), begun
+
+    def spread(rows):
+        step = 2
+        while step < n_type:
+            rows = jnp.concatenate([rows, swap(rows, "type", n_type, step)], axis=0)
+            step *= 2
+        return rows
 
     weights = (gate_weight[0], up_weight[0], down_weight[0])
     if n_type == 4:
@@ -450,30 +508,38 @@
         other = lax.ppermute(keys, "type", across)
         guest = lax.ppermute(queries, "type", to_middle)
         info, own_rows, away_rows = as_one_step(experts, incoming, *weights)
-        own_rows, near, other = tie((own_rows, near, other))
+        own_rows, near = tie((own_rows, near))
         far = lax.ppermute(near, "type", across)
-        expert_rows, state = as_one_step(
-            gather_sum, own_rows, away_rows, info, queries, keys, near, other
+        expert_rows, begun = as_one_step(
+            gather_sum, own_rows, away_rows, info, queries, [keys, near, other]
         )
-        values = [expert_rows] + [swap(expert_rows, "type", n_type, s) for s in range(1, n_type)]
-        expert_rows, guest, far = tie((expert_rows, guest, far))
-        guest_state = weigh_begin(n_type, info, guest, 1, [keys, near, other], [0, 1, 3])
+        values = spread(expert_rows)
+        expert_rows, begun, guest, far = tie((expert_rows, begun, guest, far))
         own_weights, back_weights = [], []
-        ends = [0, heads // 2, heads - heads // 8, heads]
+        ends = [0, heads // 2 + PER_STEP, heads]
         for first, last in zip(ends[:-1], ends[1:]):
             own, theirs = weigh_end(
-                n_type, info, far, 2, [queries, guest], [state, guest_state], first, last - first
+                n_type,
+                info,
+                begun,
+                far,
+                [queries, guest],
+                [keys, near, other],
+                [0, 1, 3, 2],
+                first,
+                last - first,
             )
             own_weights.append(own)
             back_weights.append(lax.ppermute(theirs, "type", to_end))
     else:
         info, own_rows, away_rows = experts(incoming, *weights)
         expert_rows, _ = gather_sum(own_rows, away_rows)
-        values = [expert_rows] + [swap(expert_rows, "type", n_type, s) for s in range(1, n_type)]
+        values = spread(expert_rows)
         tiles = [keys] + [swap(keys, "type", n_type, s) for s in range(1, n_type)]
-        state = weigh_begin(n_type, info, queries, 0, tiles[:-1], list(range(n_type - 1)))
+        ids = list(range(n_type))
+        begun = weigh_begin(n_type, info, queries, tiles[:-1], ids[:-1])
         own_weights = list(
-            weigh_end(n_type, info, tiles[-1], n_type - 1, [queries], [state], 0, heads)
+            weigh_end(n_type, info, begun, tiles[-1], [queries], [], ids, 0, heads)
         )
         back_weights = own_weights
     expert_out, attended = finish(n_type, info, own_weights, back_weights, values, tile)

time: 115 us -> 98.8 us (0.86)
  Pallas kernels: 49.5 us -> 31.7 us
  waiting for transfers between devices: 25.5 us -> 29.4 us
  local copies, waits for them, and re-layouts: 2.54 us -> 0.09 us
  other arithmetic: 0.16 us -> 1.9 us
  starting transfers between devices: 35.7 us -> 34.3 us
    pallas_call x5 -> x3, Pallas kernels: 33.7 us -> 15.9 us  [the longest x2 8.73 us: weigh_end(): pl.pallas_call(functools.partial(weigh_end_kernel, n_type, n_query, tile_...]
    ppermute x3 -> x2, waiting for transfers between devices: 0.71 us -> 9.29 us  [on_device(): back_weights.append(lax.ppermute(theirs, 'type', to_end))]
    ppermute x14 -> x13, waiting for transfers between devices: 22.8 us -> 20.1 us  [swap(): return lax.ppermute(x, axis, [(i, i ^ s) for i in range(size)])]
    ppermute x1, starting transfers between devices: 6.76 us -> 4.92 us  [on_device(): near = lax.ppermute(keys, 'type', to_middle)]
    concatenate x0 -> x2, other arithmetic: none -> 1.74 us  [the longest x1 1.02 us: spread(): rows = jnp.concatenate([rows, swap(rows, 'type', n_type, step)], axis=0)]
    ppermute x14 -> x13, starting transfers between devices: 20.4 us -> 22.2 us  [swap(): return lax.ppermute(x, axis, [(i, i ^ s) for i in range(size)])]
    ppermute x1, waiting for transfers between devices: 1.66 us -> 0.01 us  [on_device(): near = lax.ppermute(keys, 'type', to_middle)]
    ppermute x3 -> x2, starting transfers between devices: 3.88 us -> 2.58 us  [on_device(): back_weights.append(lax.ppermute(theirs, 'type', to_end))]
  transfers between devices with their start and end apart: 21 -> 19, of which waited for: 10 -> 8; matrix products, arithmetic and copies ran while one was open for 0% -> 2% of each run, Pallas kernels for 25% -> 28%
where the time goes in v3:
time: 98.8 us; the launch traced here: 98.2 us
  starting transfers between devices  34.3 us (35%)
  Pallas kernels  31.7 us (32%)
  waiting for transfers between devices  29.4 us (30%)
  other arithmetic  1.9 us (2%)
    ppermute x13, starting transfers between devices, swap(): return lax.ppermute(x, axis, [(i, i ^ s) for i in range(size)])  22.2 us
    ppermute x13, waiting for transfers between devices, swap(): return lax.ppermute(x, axis, [(i, i ^ s) for i in range(size)])  20.1 us
    ppermute x2, waiting for transfers between devices, on_device(): back_weights.append(lax.ppermute(theirs, 'type', to_end))  9.29 us
    pallas_call x2, Pallas kernels, weigh_end(): pl.pallas_call(functools.partial(weigh_end_kernel, n_type, n_query, tile_...  8.73 us
    pallas_call x1, Pallas kernels, fetch(): pl.pallas_call(functools.partial(fetch_kernel, count), out_shape=[pltpu.V...  7.28 us
    pallas_call x1, Pallas kernels, weigh_begin(): pl.pallas_call(functools.partial(weigh_begin_kernel, n_type, tile_ids), g...  7.2 us
    ppermute x1, starting transfers between devices, on_device(): near = lax.ppermute(keys, 'type', to_middle)  4.92 us
    pallas_call x1, Pallas kernels, ffn(): pl.pallas_call(ffn_kernel, out_shape=[jax.ShapeDtypeStruct((half, width),...  3.58 us
  transfers between devices with their start and end apart: 19, of which 8 were waited for; matrix products, arithmetic and copies ran while one was open for 2% of the time, Pallas kernels for 28%

profile of v3, /device:TPU:0, one launch (start us, length us, event | category | flops | bytes accessed | tf_op | source)
XLA Modules:
  0.0 98.2 jit_solution(3276412500749788818)
XLA Ops:
  0.6 2.7 %shard_map.98 = (bf16[16,4224]{1,0:T(8,128)(2,1)S(1)}, bf16[16,4224]{1,0:T(8,128)(2,1)S(1)}, bf16[16,4224]{1,0:T(8,128)(2,1)S(1)}, bf16[16,4224]{1,0:T(8,128)(2,1)S(1)}) custom-call(s32[1,128]{1,0:T(1,128)} %bitcast.8, s32[1,4]{1,0:T(1,128)} %bitcast.9, bf16[128,4096]{1,0:T(8,128)(2,1)} %tokens_ref.1), custom_call_target="tpu_custom_call" | custom-call | tf_op jit(solution)/shard_map/pallas_call | solution.py:87
  3.3 3.1 %collective-permute-start.9 = (bf16[16,4224]{1,0:T(8,128)(2,1)S(1)}, bf16[16,4224]{1,0:T(8,128)(2,1)S(1)}, u32[]{:S(2)}, u32[]{:S(2)}) collective-permute-start(bf16[16,4224]{1,0:T(8,128)(2,1)S(1)} %get-tuple-element.96), channel_id=1, source_target_pairs={{0,1},{1,0},{2,3},{3,2},{4,5},{5,4},{6,7},{7,6},{8,9},{9,8},{10,11... | collective-permute-start | bytes 405512 | tf_op jit(solution)/shard_map/ppermute | solution.py:451
  6.4 2.6 %collective-permute-start.10 = (bf16[16,4224]{1,0:T(8,128)(2,1)S(1)}, bf16[16,4224]{1,0:T(8,128)(2,1)S(1)}, u32[]{:S(2)}, u32[]{:S(2)}) collective-permute-start(bf16[16,4224]{1,0:T(8,128)(2,1)S(1)} %get-tuple-element.97), channel_id=1, source_target_pairs={{0,2},{1,3},{2,0},{3,1},{4,6},{5,7},{6,4},{7,5},{8,10},{9,11},{10,... | collective-permute-start | bytes 405512 | tf_op jit(solution)/shard_map/ppermute | solution.py:451
  9.0 0.0 collective-permute-start.11
  9.0 2.6 %collective-permute-done.9 = bf16[16,4224]{1,0:T(8,128)(2,1)S(1)} collective-permute-done((bf16[16,4224]{1,0:T(8,128)(2,1)S(1)}, bf16[16,4224]{1,0:T(8,128)(2,1)S(1)}, u32[]{:S(2)}, u32[]{:S(2)}) %collective-permute-start.9) | collective-permute-done | bytes 135200 | tf_op jit(solution)/shard_map/ppermute | solution.py:451
  11.7 8.0 %collective-permute-done.10 = bf16[16,4224]{1,0:T(8,128)(2,1)S(1)} collective-permute-done((bf16[16,4224]{1,0:T(8,128)(2,1)S(1)}, bf16[16,4224]{1,0:T(8,128)(2,1)S(1)}, u32[]{:S(2)}, u32[]{:S(2)}) %collective-permute-start.10) | collective-permute-done | bytes 135200 | tf_op jit(solution)/shard_map/ppermute | solution.py:451
  19.6 0.0 collective-permute-done.11
  19.6 4.9 %collective-permute-start.12 = (bf16[128,4096]{1,0:T(8,128)(2,1)}, bf16[128,4096]{1,0:T(8,128)(2,1)}, u32[]{:S(2)}, u32[]{:S(2)}) collective-permute-start(bf16[128,4096]{1,0:T(8,128)(2,1)} %refs_2_.1), channel_id=1, source_target_pairs={{0,1},{3,2},{4,5},{7,6},{8,9},{11,10},{12,13},{15,14},{16,17},{19,... | collective-permute-start | bytes 3145736 | tf_op jit(solution)/shard_map/ppermute | solution.py:507
  24.6 1.6 %collective-permute-start.13 = (bf16[128,4096]{1,0:T(8,128)(2,1)}, bf16[128,4096]{1,0:T(8,128)(2,1)}, u32[]{:S(2)}, u32[]{:S(2)}) collective-permute-start(bf16[128,4096]{1,0:T(8,128)(2,1)} %refs_2_.1), channel_id=1, source_target_pairs={{1,2},{2,1},{5,6},{6,5},{9,10},{10,9},{13,14},{14,13},{17,18},{18,... | collective-permute-start | bytes 3145736 | tf_op jit(solution)/shard_map/ppermute | solution.py:508
  26.2 2.2 %collective-permute-start.14 = (bf16[128,4096]{1,0:T(8,128)(2,1)}, bf16[128,4096]{1,0:T(8,128)(2,1)S(1)}, u32[]{:S(2)}, u32[]{:S(2)}) collective-permute-start(bf16[128,4096]{1,0:T(8,128)(2,1)} %refs_0_.1), channel_id=1, source_target_pairs={{0,1},{3,2},{4,5},{7,6},{8,9},{11,10},{12,13},{15,14},{16,17},{19,... | collective-permute-start | bytes 3145736 | tf_op jit(solution)/shard_map/ppermute | solution.py:509
  28.4 0.0 copy-start
  28.4 19.9 %conditional.2 = (f32[12,128]{1,0:T(8,128)S(1)}, f32[64,4096]{1,0:T(8,128)S(1)}, bf16[64,4096]{1,0:T(8,128)(2,1)S(1)}) conditional(s32[]{:T(128)} %convert_element_type.25, () %tuple.28, (bf16[16,4224]{1,0:T(8,128)(2,1)S(1)}, bf16[16,4224]{1,0:T(8,128)(2,1)S(1)}, bf16[16,4224]{1,0:T(8,128)(2,1)S(1)}, bf16[16,4224]{1,0:T(8,128)(2,1)S(1)}, ...), branch_computations={%region_0.0_spmd, %region_1.0_spmd} | conditional | bytes 48758968 | solution.py:457
  28.5 0.4 branch_1_fun.4
  28.9 1.6 %collective-permute-start.1 = (bf16[16,4096]{1,0:T(8,128)(2,1)S(1)}, bf16[16,4096]{1,0:T(8,128)(2,1)S(1)}, u32[]{:S(2)}, u32[]{:S(2)}) collective-permute-start(bf16[16,4096]{1,0:T(8,128)(2,1)S(1)} %get-tuple-element.43), channel_id=1, source_target_pairs={{0,16},{4,20},{8,24},{12,28},{16,0},{20,4},{24,8},{28,12},{1,17},{... | collective-permute-start | bytes 393224 | tf_op jit(solution)/shard_map/cond/branch_1_fun/ppermute | solution.py:451
  30.4 1.5 %collective-permute-start = (bf16[16,4096]{1,0:T(8,128)(2,1)S(1)}, bf16[16,4096]{1,0:T(8,128)(2,1)S(1)}, u32[]{:S(2)}, u32[]{:S(2)}) collective-permute-start(bf16[16,4096]{1,0:T(8,128)(2,1)S(1)} %get-tuple-element.43), channel_id=1, source_target_pairs={{0,8},{4,12},{8,0},{12,4},{16,24},{20,28},{24,16},{28,20},{1,9},{5... | collective-permute-start | bytes 393224 | tf_op jit(solution)/shard_map/cond/branch_1_fun/ppermute | solution.py:451
  31.9 2.0 %collective-permute-done.1 = bf16[16,4096]{1,0:T(8,128)(2,1)S(1)} collective-permute-done((bf16[16,4096]{1,0:T(8,128)(2,1)S(1)}, bf16[16,4096]{1,0:T(8,128)(2,1)S(1)}, u32[]{:S(2)}, u32[]{:S(2)}) %collective-permute-start.1) | collective-permute-done | bytes 131104 | tf_op jit(solution)/shard_map/cond/branch_1_fun/ppermute | solution.py:451
  33.9 1.5 %collective-permute-start.2 = (bf16[16,4096]{1,0:T(8,128)(2,1)S(1)}, bf16[16,4096]{1,0:T(8,128)(2,1)S(1)}, u32[]{:S(2)}, u32[]{:S(2)}) collective-permute-start(bf16[16,4096]{1,0:T(8,128)(2,1)S(1)} %collective-permute-done.1), channel_id=1, source_target_pairs={{0,8},{4,12},{8,0},{12,4},{16,24},{20,28},{24,16},{28,20},{1,9},{5... | collective-permute-start | bytes 393224 | tf_op jit(solution)/shard_map/cond/branch_1_fun/ppermute | solution.py:451
  35.4 7.3 %branch_1_fun.5 = (bf16[4096,896]{1,0:T(8,128)(2,1)S(1)}, bf16[4096,896]{1,0:T(8,128)(2,1)S(1)}, bf16[896,4096]{1,0:T(8,128)(2,1)S(1)}) custom-call(bf16[4096,896]{1,0:T(8,128)(2,1)} %bitcast.5, bf16[4096,896]{1,0:T(8,128)(2,1)} %bitcast.6, bf16[896,4096]{1,0:T(8,128)(2,1)} %bitcast.7), custom_call_target="tpu_custom_call" | custom-call | bytes 44040192 | tf_op jit(solution)/shard_map/cond/branch_1_fun/pallas_call | solution.py:114
  42.7 0.0 collective-permute-done
  42.7 0.0 collective-permute-done.2
  42.8 0.1 collective-permute-start.3
  42.9 1.9 %collective-permute-done.3.far_ref = bf16[64,4096]{1,0:T(8,128)(2,1)S(1)} collective-permute-done((bf16[64,4096]{1,0:T(8,128)(2,1)S(1)}, bf16[64,4096]{1,0:T(8,128)(2,1)S(1)}, u32[]{:S(2)}, u32[]{:S(2)}) %collective-permute-start.3) | collective-permute-done | bytes 524320 | tf_op jit(solution)/shard_map/cond/branch_1_fun/ppermute | solution.py:451
  44.7 3.6 %branch_1_fun.6 = (f32[64,4096]{1,0:T(8,128)S(1)}, bf16[64,4096]{1,0:T(8,128)(2,1)S(1)}) custom-call(bf16[64,4096]{1,0:T(8,128)(2,1)S(1)} %constant_dynamic-update-slice_fusion.near_ref, bf16[64,4096]{1,0:T(8,128)(2,1)S(1)} %collective-permute-done.3.far_ref, bf16[4096,896]{1,0:T(8,128)(2,1)S(1)} %get-tuple-element.47.gate_ref, ...), custom_call_target="tpu_custom_call" | custom-call | tf_op jit(solution)/shard_map/cond/branch_1_fun/pallas_call | solution.py:216
  48.4 0.7 collective-permute-start.15
  49.1 21.9 %conditional.3 = (bf16[32,4096]{1,0:T(8,128)(2,1)}, f32[32,16,128]{2,1,0:T(8,128)S(1)}, bf16[64,4096]{1,0:T(8,128)(2,1)}) conditional(s32[]{:T(128)} %convert_element_type.25, () %tuple.31, (bf16[64,4096]{1,0:T(8,128)(2,1)S(1)}, f32[64,4096]{1,0:T(8,128)S(1)}, f32[12,128]{1,0:T(8,128)S(1)}, bf16[128,4096]{1,0:T(8,128)(2,1)S(1)}, ...), branch_computations={%region_2.0_spmd, %region_3.0_spmd} | conditional | flops 1835008 | bytes 8519904 | solution.py:457
  49.1 0.2 collective-permute-start.4
  49.3 1.8 %collective-permute-done.4 = bf16[64,4096]{1,0:T(8,128)(2,1)S(1)} collective-permute-done((bf16[64,4096]{1,0:T(8,128)(2,1)S(1)}, bf16[64,4096]{1,0:T(8,128)(2,1)S(1)}, u32[]{:S(2)}, u32[]{:S(2)}) %collective-permute-start.4) | collective-permute-done | bytes 524320 | tf_op jit(solution)/shard_map/cond/branch_1_fun/ppermute | solution.py:451
  51.1 0.1 add_convert_fusion
  51.2 1.6 %collective-permute-start.7 = (bf16[16,4096]{1,0:T(8,128)(2,1)S(1)}, bf16[16,4096]{1,0:T(8,128)(2,1)S(1)}, u32[]{:S(2)}, u32[]{:S(2)}) collective-permute-start(bf16[16,4096]{1,0:T(8,128)(2,1)S(1)} %get-tuple-element.127), channel_id=1, source_target_pairs={{0,24},{4,28},{8,16},{12,20},{16,8},{20,12},{24,0},{28,4},{1,25},{... | collective-permute-start | bytes 393224 | tf_op jit(solution)/shard_map/cond/branch_1_fun/ppermute | solution.py:451
  52.9 0.5 collective-permute-start.6
  53.4 1.4 %collective-permute-start.5 = (bf16[16,4096]{1,0:T(8,128)(2,1)S(1)}, bf16[16,4096]{1,0:T(8,128)(2,1)S(1)}, u32[]{:S(2)}, u32[]{:S(2)}) collective-permute-start(bf16[16,4096]{1,0:T(8,128)(2,1)S(1)} %get-tuple-element.129), channel_id=1, source_target_pairs={{0,8},{4,12},{8,0},{12,4},{16,24},{20,28},{24,16},{28,20},{1,9},{5... | collective-permute-start | bytes 393224 | tf_op jit(solution)/shard_map/cond/branch_1_fun/ppermute | solution.py:451
  54.8 7.2 %branch_1_fun.7 = (f32[32,16,128]{2,1,0:T(8,128)S(1)}, bf16[64,4096]{1,0:T(8,128)(2,1)}) custom-call(f32[12,128]{1,0:T(8,128)S(1)} %get-tuple-element.54.info_ref, bf16[128,4096]{1,0:T(8,128)(2,1)S(1)} %get-tuple-element.55.query_ref, bf16[128,4096]{1,0:T(8,128)(2,1)} %get-tuple-element.56.refs_0_, bf16[128,4096]{1,0:T(8,128)(2,1)} %get-tuple-element.57.refs_1_, ...), custom_call_target="tpu_custom_call" | custom-call | tf_op jit(solution)/shard_map/cond/branch_1_fun/pallas_call | solution.py:309
  62.0 0.0 collective-permute-done.7
  62.0 0.0 collective-permute-done.5
  62.0 0.1 add_convert_fusion.1
  62.1 4.4 %collective-permute-start.8 = (bf16[16,4096]{1,0:T(8,128)(2,1)S(1)}, bf16[16,4096]{1,0:T(8,128)(2,1)S(1)}, u32[]{:S(2)}, u32[]{:S(2)}) collective-permute-start(bf16[16,4096]{1,0:T(8,128)(2,1)S(1)} %add_convert_fusion.1), channel_id=1, source_target_pairs={{0,1},{1,0},{2,3},{3,2},{4,5},{5,4},{6,7},{7,6},{8,9},{9,8},{10,11... | collective-permute-start | bytes 393224 | tf_op jit(solution)/shard_map/cond/branch_1_fun/ppermute | solution.py:451
  66.5 3.8 %collective-permute-done.8 = bf16[16,4096]{1,0:T(8,128)(2,1)S(1)} collective-permute-done((bf16[16,4096]{1,0:T(8,128)(2,1)S(1)}, bf16[16,4096]{1,0:T(8,128)(2,1)S(1)}, u32[]{:S(2)}, u32[]{:S(2)}) %collective-permute-start.8) | collective-permute-done | bytes 131104 | tf_op jit(solution)/shard_map/cond/branch_1_fun/ppermute | solution.py:451
  70.3 0.7 pad_maximum_fusion
  71.0 3.7 %collective-permute-start.18 = (bf16[32,4096]{1,0:T(8,128)(2,1)}, bf16[32,4096]{1,0:T(8,128)(2,1)S(1)}, u32[]{:S(2)}, u32[]{:S(2)}) collective-permute-start(bf16[32,4096]{1,0:T(8,128)(2,1)} %get-tuple-element.110), channel_id=1, source_target_pairs={{0,2},{1,3},{2,0},{3,1},{4,6},{5,7},{6,4},{7,5},{8,10},{9,11},{10,... | collective-permute-start | bytes 786440 | tf_op jit(solution)/shard_map/ppermute | solution.py:451
  74.7 0.0 collective-permute-done.14.refs_1_
  74.7 3.6 %shard_map.100 = (bf16[12,64,128]{2,1,0:T(8,128)(2,1)S(1)}, bf16[12,64,128]{2,1,0:T(8,128)(2,1)S(1)}) custom-call(f32[12,128]{1,0:T(8,128)S(1)} %get-tuple-element.103.info_ref, bf16[64,4096]{1,0:T(8,128)(2,1)} %get-tuple-element.113.kept_ref, f32[32,16,128]{2,1,0:T(8,128)S(1)} %get-tuple-element.114.state_ref, ...), custom_call_target="tpu_custom_call" | custom-call | bytes 3145728 | tf_op jit(solution)/shard_map/pallas_call | solution.py:387
  78.3 1.3 %collective-permute-start.17 = (bf16[12,64,128]{2,1,0:T(8,128)(2,1)S(1)}, bf16[12,64,128]{2,1,0:T(8,128)(2,1)S(1)}, u32[]{:S(2)}, u32[]{:S(2)}) collective-permute-start(bf16[12,64,128]{2,1,0:T(8,128)(2,1)S(1)} %get-tuple-element.120), channel_id=1, source_target_pairs={{1,0},{2,3},{5,4},{6,7},{9,8},{10,11},{13,12},{14,15},{17,16},{18,... | collective-permute-start | bytes 589832 | tf_op jit(solution)/shard_map/ppermute | solution.py:533
  79.6 5.1 %shard_map.99 = (bf16[20,64,128]{2,1,0:T(8,128)(2,1)S(1)}, bf16[20,64,128]{2,1,0:T(8,128)(2,1)S(1)}) custom-call(f32[12,128]{1,0:T(8,128)S(1)} %get-tuple-element.103.info_ref, bf16[64,4096]{1,0:T(8,128)(2,1)} %get-tuple-element.113.kept_ref, f32[32,16,128]{2,1,0:T(8,128)S(1)} %get-tuple-element.114.state_ref, ...), custom_call_target="tpu_custom_call" | custom-call | bytes 5242880 | tf_op jit(solution)/shard_map/pallas_call | solution.py:387
  84.8 1.3 %collective-permute-start.16 = (bf16[20,64,128]{2,1,0:T(8,128)(2,1)S(1)}, bf16[20,64,128]{2,1,0:T(8,128)(2,1)S(1)}, u32[]{:S(2)}, u32[]{:S(2)}) collective-permute-start(bf16[20,64,128]{2,1,0:T(8,128)(2,1)S(1)} %get-tuple-element.119), channel_id=1, source_target_pairs={{1,0},{2,3},{5,4},{6,7},{9,8},{10,11},{13,12},{14,15},{17,16},{18,... | collective-permute-start | bytes 983048 | tf_op jit(solution)/shard_map/ppermute | solution.py:533
  86.1 1.0 %pad_maximum_fusion.1.refs_4_ = bf16[64,4096]{1,0:T(8,128)(2,1)S(1)} fusion(bf16[32,4096]{1,0:T(8,128)(2,1)S(1)} %collective-permute-done.18, bf16[32,4096]{1,0:T(8,128)(2,1)} %get-tuple-element.110), kind=kLoop, calls=%fused_computation.7 | loop fusion | flops 1048576 | bytes 1048576 | tf_op jit(solution)/shard_map/concatenate | solution.py:497
  87.1 2.9 %collective-permute-done.17.refs_3_ = bf16[12,64,128]{2,1,0:T(8,128)(2,1)S(1)} collective-permute-done((bf16[12,64,128]{2,1,0:T(8,128)(2,1)S(1)}, bf16[12,64,128]{2,1,0:T(8,128)(2,1)S(1)}, u32[]{:S(2)}, u32[]{:S(2)}) %collective-permute-start.17) | collective-permute-done | bytes 196640 | tf_op jit(solution)/shard_map/ppermute | solution.py:533
  90.0 6.4 %collective-permute-done.16.refs_2_ = bf16[20,64,128]{2,1,0:T(8,128)(2,1)S(1)} collective-permute-done((bf16[20,64,128]{2,1,0:T(8,128)(2,1)S(1)}, bf16[20,64,128]{2,1,0:T(8,128)(2,1)S(1)}, u32[]{:S(2)}, u32[]{:S(2)}) %collective-permute-start.16) | collective-permute-done | bytes 327712 | tf_op jit(solution)/shard_map/ppermute | solution.py:533
  96.4 1.8 %shard_map.101 = (bf16[128,4096]{1,0:T(8,128)(2,1)}, bf16[128,4096]{1,0:T(8,128)(2,1)}) custom-call(f32[12,128]{1,0:T(8,128)S(1)} %get-tuple-element.103.info_ref, bf16[20,64,128]{2,1,0:T(8,128)(2,1)S(1)} %get-tuple-element.117.refs_0_, bf16[12,64,128]{2,1,0:T(8,128)(2,1)S(1)} %get-tuple-element.118.refs_1_, ...), custom_call_target="tpu_custom_call" | custom-call | tf_op jit(solution)/shard_map/pallas_call | solution.py:439
  (13 shorter events, 0.1 us)
Async XLA Ops:
  3.3 8.3 %collective-permute-start.9 = (bf16[16,4224]{1,0:T(8,128)(2,1)S(1)}, bf16[16,4224]{1,0:T(8,128)(2,1)S(1)}, u32[]{:S(2)}, u32[]{:S(2)}) collective-permute-start(bf16[16,4224]{1,0:T(8,128)(2,1)S(1)} %get-tuple-element.96), channel_id=1, source_target_pairs={{0,1},{1,0},{2,3},{3,2},{4,5},{5,4},{6,7},{7,6},{8,9},{9,8},{10,11... | collective-permute-start | bytes 405512 | tf_op jit(solution)/shard_map/ppermute | solution.py:451
  6.4 13.2 %collective-permute-start.10 = (bf16[16,4224]{1,0:T(8,128)(2,1)S(1)}, bf16[16,4224]{1,0:T(8,128)(2,1)S(1)}, u32[]{:S(2)}, u32[]{:S(2)}) collective-permute-start(bf16[16,4224]{1,0:T(8,128)(2,1)S(1)} %get-tuple-element.97), channel_id=1, source_target_pairs={{0,2},{1,3},{2,0},{3,1},{4,6},{5,7},{6,4},{7,5},{8,10},{9,11},{10,... | collective-permute-start | bytes 405512 | tf_op jit(solution)/shard_map/ppermute | solution.py:451
  9.0 10.6 %collective-permute-start.11 = (bf16[16,4224]{1,0:T(8,128)(2,1)S(1)}, bf16[16,4224]{1,0:T(8,128)(2,1)S(1)}, u32[]{:S(2)}, u32[]{:S(2)}) collective-permute-start(bf16[16,4224]{1,0:T(8,128)(2,1)S(1)} %get-tuple-element.98), channel_id=1, source_target_pairs={{0,3},{1,2},{2,1},{3,0},{4,7},{5,6},{6,5},{7,4},{8,11},{9,10},{10,... | collective-permute-start | bytes 405512 | tf_op jit(solution)/shard_map/ppermute | solution.py:451
  19.6 28.7 %collective-permute-start.12 = (bf16[128,4096]{1,0:T(8,128)(2,1)}, bf16[128,4096]{1,0:T(8,128)(2,1)}, u32[]{:S(2)}, u32[]{:S(2)}) collective-permute-start(bf16[128,4096]{1,0:T(8,128)(2,1)} %refs_2_.1), channel_id=1, source_target_pairs={{0,1},{3,2},{4,5},{7,6},{8,9},{11,10},{12,13},{15,14},{16,17},{19,... | collective-permute-start | bytes 3145736 | tf_op jit(solution)/shard_map/ppermute | solution.py:507
  24.6 24.5 %collective-permute-start.13 = (bf16[128,4096]{1,0:T(8,128)(2,1)}, bf16[128,4096]{1,0:T(8,128)(2,1)}, u32[]{:S(2)}, u32[]{:S(2)}) collective-permute-start(bf16[128,4096]{1,0:T(8,128)(2,1)} %refs_2_.1), channel_id=1, source_target_pairs={{1,2},{2,1},{5,6},{6,5},{9,10},{10,9},{13,14},{14,13},{17,18},{18,... | collective-permute-start | bytes 3145736 | tf_op jit(solution)/shard_map/ppermute | solution.py:508
  26.2 48.5 %collective-permute-start.14 = (bf16[128,4096]{1,0:T(8,128)(2,1)}, bf16[128,4096]{1,0:T(8,128)(2,1)S(1)}, u32[]{:S(2)}, u32[]{:S(2)}) collective-permute-start(bf16[128,4096]{1,0:T(8,128)(2,1)} %refs_0_.1), channel_id=1, source_target_pairs={{0,1},{3,2},{4,5},{7,6},{8,9},{11,10},{12,13},{15,14},{16,17},{19,... | collective-permute-start | bytes 3145736 | tf_op jit(solution)/shard_map/ppermute | solution.py:509
  28.4 20.7 %copy-start = (bf16[128,4096]{1,0:T(8,128)(2,1)S(1)}, bf16[128,4096]{1,0:T(8,128)(2,1)}, u32[]{:S(2)}) copy-start(bf16[128,4096]{1,0:T(8,128)(2,1)} %refs_0_.1) | copy-start | bytes 3145732
  28.9 5.0 %collective-permute-start.1 = (bf16[16,4096]{1,0:T(8,128)(2,1)S(1)}, bf16[16,4096]{1,0:T(8,128)(2,1)S(1)}, u32[]{:S(2)}, u32[]{:S(2)}) collective-permute-start(bf16[16,4096]{1,0:T(8,128)(2,1)S(1)} %get-tuple-element.43), channel_id=1, source_target_pairs={{0,16},{4,20},{8,24},{12,28},{16,0},{20,4},{24,8},{28,12},{1,17},{... | collective-permute-start | bytes 393224 | tf_op jit(solution)/shard_map/cond/branch_1_fun/ppermute | solution.py:451
  30.4 12.2 %collective-permute-start = (bf16[16,4096]{1,0:T(8,128)(2,1)S(1)}, bf16[16,4096]{1,0:T(8,128)(2,1)S(1)}, u32[]{:S(2)}, u32[]{:S(2)}) collective-permute-start(bf16[16,4096]{1,0:T(8,128)(2,1)S(1)} %get-tuple-element.43), channel_id=1, source_target_pairs={{0,8},{4,12},{8,0},{12,4},{16,24},{20,28},{24,16},{28,20},{1,9},{5... | collective-permute-start | bytes 393224 | tf_op jit(solution)/shard_map/cond/branch_1_fun/ppermute | solution.py:451
  33.9 8.8 %collective-permute-start.2 = (bf16[16,4096]{1,0:T(8,128)(2,1)S(1)}, bf16[16,4096]{1,0:T(8,128)(2,1)S(1)}, u32[]{:S(2)}, u32[]{:S(2)}) collective-permute-start(bf16[16,4096]{1,0:T(8,128)(2,1)S(1)} %collective-permute-done.1), channel_id=1, source_target_pairs={{0,8},{4,12},{8,0},{12,4},{16,24},{20,28},{24,16},{28,20},{1,9},{5... | collective-permute-start | bytes 393224 | tf_op jit(solution)/shard_map/cond/branch_1_fun/ppermute | solution.py:451
  42.8 2.0 %collective-permute-start.3 = (bf16[64,4096]{1,0:T(8,128)(2,1)S(1)}, bf16[64,4096]{1,0:T(8,128)(2,1)S(1)}, u32[]{:S(2)}, u32[]{:S(2)}) collective-permute-start(bf16[64,4096]{1,0:T(8,128)(2,1)S(1)} %constant_dynamic-update-slice_fusion.near_ref), channel_id=1, source_target_pairs={{0,4},{4,0},{8,12},{12,8},{16,20},{20,16},{24,28},{28,24},{1,5},{5... | collective-permute-start | bytes 1572872 | tf_op jit(solution)/shard_map/cond/branch_1_fun/ppermute | solution.py:451
  48.4 26.4 %collective-permute-start.15 = (bf16[128,4096]{1,0:T(8,128)(2,1)}, bf16[128,4096]{1,0:T(8,128)(2,1)S(1)}, u32[]{:S(2)}, u32[]{:S(2)}) collective-permute-start(bf16[128,4096]{1,0:T(8,128)(2,1)} %collective-permute-done.12.refs_3_), channel_id=1, source_target_pairs={{1,2},{2,1},{5,6},{6,5},{9,10},{10,9},{13,14},{14,13},{17,18},{18,... | collective-permute-start | bytes 3145736 | tf_op jit(solution)/shard_map/ppermute | solution.py:512
  49.1 2.0 %collective-permute-start.4 = (bf16[64,4096]{1,0:T(8,128)(2,1)S(1)}, bf16[64,4096]{1,0:T(8,128)(2,1)S(1)}, u32[]{:S(2)}, u32[]{:S(2)}) collective-permute-start(bf16[64,4096]{1,0:T(8,128)(2,1)S(1)} %get-tuple-element.53), channel_id=1, source_target_pairs={{0,4},{4,0},{8,12},{12,8},{16,20},{20,16},{24,28},{28,24},{1,5},{5... | collective-permute-start | bytes 1572872 | tf_op jit(solution)/shard_map/cond/branch_1_fun/ppermute | solution.py:451
  51.2 10.8 %collective-permute-start.7 = (bf16[16,4096]{1,0:T(8,128)(2,1)S(1)}, bf16[16,4096]{1,0:T(8,128)(2,1)S(1)}, u32[]{:S(2)}, u32[]{:S(2)}) collective-permute-start(bf16[16,4096]{1,0:T(8,128)(2,1)S(1)} %get-tuple-element.127), channel_id=1, source_target_pairs={{0,24},{4,28},{8,16},{12,20},{16,8},{20,12},{24,0},{28,4},{1,25},{... | collective-permute-start | bytes 393224 | tf_op jit(solution)/shard_map/cond/branch_1_fun/ppermute | solution.py:451
  52.9 9.1 %collective-permute-start.6 = (bf16[16,4096]{1,0:T(8,128)(2,1)S(1)}, bf16[16,4096]{1,0:T(8,128)(2,1)S(1)}, u32[]{:S(2)}, u32[]{:S(2)}) collective-permute-start(bf16[16,4096]{1,0:T(8,128)(2,1)S(1)} %get-tuple-element.128), channel_id=1, source_target_pairs={{0,16},{4,20},{8,24},{12,28},{16,0},{20,4},{24,8},{28,12},{1,17},{... | collective-permute-start | bytes 393224 | tf_op jit(solution)/shard_map/cond/branch_1_fun/ppermute | solution.py:451
  53.4 8.6 %collective-permute-start.5 = (bf16[16,4096]{1,0:T(8,128)(2,1)S(1)}, bf16[16,4096]{1,0:T(8,128)(2,1)S(1)}, u32[]{:S(2)}, u32[]{:S(2)}) collective-permute-start(bf16[16,4096]{1,0:T(8,128)(2,1)S(1)} %get-tuple-element.129), channel_id=1, source_target_pairs={{0,8},{4,12},{8,0},{12,4},{16,24},{20,28},{24,16},{28,20},{1,9},{5... | collective-permute-start | bytes 393224 | tf_op jit(solution)/shard_map/cond/branch_1_fun/ppermute | solution.py:451
  62.1 8.2 %collective-permute-start.8 = (bf16[16,4096]{1,0:T(8,128)(2,1)S(1)}, bf16[16,4096]{1,0:T(8,128)(2,1)S(1)}, u32[]{:S(2)}, u32[]{:S(2)}) collective-permute-start(bf16[16,4096]{1,0:T(8,128)(2,1)S(1)} %add_convert_fusion.1), channel_id=1, source_target_pairs={{0,1},{1,0},{2,3},{3,2},{4,5},{5,4},{6,7},{7,6},{8,9},{9,8},{10,11... | collective-permute-start | bytes 393224 | tf_op jit(solution)/shard_map/cond/branch_1_fun/ppermute | solution.py:451
  71.0 8.6 %copy-start.1 = (bf16[128,4096]{1,0:T(8,128)(2,1)S(1)}, bf16[128,4096]{1,0:T(8,128)(2,1)}, u32[]{:S(2)}) copy-start(bf16[128,4096]{1,0:T(8,128)(2,1)} %refs_2_.1) | copy-start | bytes 3145732
  71.0 15.0 %collective-permute-start.18 = (bf16[32,4096]{1,0:T(8,128)(2,1)}, bf16[32,4096]{1,0:T(8,128)(2,1)S(1)}, u32[]{:S(2)}, u32[]{:S(2)}) collective-permute-start(bf16[32,4096]{1,0:T(8,128)(2,1)} %get-tuple-element.110), channel_id=1, source_target_pairs={{0,2},{1,3},{2,0},{3,1},{4,6},{5,7},{6,4},{7,5},{8,10},{9,11},{10,... | collective-permute-start | bytes 786440 | tf_op jit(solution)/shard_map/ppermute | solution.py:451
  78.3 11.7 %collective-permute-start.17 = (bf16[12,64,128]{2,1,0:T(8,128)(2,1)S(1)}, bf16[12,64,128]{2,1,0:T(8,128)(2,1)S(1)}, u32[]{:S(2)}, u32[]{:S(2)}) collective-permute-start(bf16[12,64,128]{2,1,0:T(8,128)(2,1)S(1)} %get-tuple-element.120), channel_id=1, source_target_pairs={{1,0},{2,3},{5,4},{6,7},{9,8},{10,11},{13,12},{14,15},{17,16},{18,... | collective-permute-start | bytes 589832 | tf_op jit(solution)/shard_map/ppermute | solution.py:533
  84.8 11.6 %collective-permute-start.16 = (bf16[20,64,128]{2,1,0:T(8,128)(2,1)S(1)}, bf16[20,64,128]{2,1,0:T(8,128)(2,1)S(1)}, u32[]{:S(2)}, u32[]{:S(2)}) collective-permute-start(bf16[20,64,128]{2,1,0:T(8,128)(2,1)S(1)} %get-tuple-element.119), channel_id=1, source_target_pairs={{1,0},{2,3},{5,4},{6,7},{9,8},{10,11},{13,12},{14,15},{17,16},{18,... | collective-permute-start | bytes 983048 | tf_op jit(solution)/shard_map/ppermute | solution.py:533

commit v4 on v3

--- a/solution.py
+++ b/solution.py
@@ -275,20 +275,33 @@
     return sum(jnp.sum(jnp.exp2((x - top) * FACTOR), axis=0, keepdims=True) for x in scores)
 
 
-def weigh_begin_kernel(n_type, tile_ids, info_ref, query_ref, *refs):
+def in_middle(body, n_type, *args):
+    me = lax.axis_index("type")
+    step = pl.program_id(0)
+    if n_type != 4:
+        body(step, n_type, *args)
+    else:
+
+        @pl.when((me > 0) & (me < n_type - 1))
+        def _():
+            body(step, n_type, *args)
+
+
+def weigh_begin_body(step, n_type, tile_ids, query_id, info_ref, query_ref, *refs):
     key_refs = refs[: len(tile_ids)]
-    state_ref, kept_ref = refs[len(tile_ids) :]
-    slots, width = kept_ref.shape
-    tile = query_ref.shape[0]
-    select = [slots_of(slots, tile, s, info_ref).astype(jnp.bfloat16) for s in tile_ids]
-    kept_ref[...] = jnp.dot(
-        jnp.concatenate(select, axis=1),
-        jnp.concatenate([ref[...] for ref in key_refs], axis=0),
-        preferred_element_type=jnp.float32,
-    ).astype(jnp.bfloat16)
+    state_ref, *kept_refs = refs[len(tile_ids) :]
+    tile, width = query_ref.shape
+    for kept_ref in kept_refs:
+        slots = kept_ref.shape[0]
+        select = [slots_of(slots, tile, s, info_ref).astype(jnp.bfloat16) for s in tile_ids]
+        kept_ref[...] = jnp.dot(
+            jnp.concatenate(select, axis=1),
+            jnp.concatenate([ref[...] for ref in key_refs], axis=0),
+            preferred_element_type=jnp.float32,
+        ).astype(jnp.bfloat16)
     for at in range(0, width, 2 * HEAD):
         span = pl.ds(at, 2 * HEAD)
-        scores = pair_scores(n_type, 0, tile_ids, info_ref, key_refs, query_ref, span)
+        scores = pair_scores(n_type, query_id, tile_ids, info_ref, key_refs, query_ref, span)
         top = top_of(scores)
         total = total_of(scores, top)
         for i in range(2):
@@ -298,40 +311,39 @@
             state_ref[head, 8:] = jnp.broadcast_to(top[:, mine], (8, tile))
 
 
-PER_STEP = 4
-
-
-def weigh_begin(n_type, info, query, keys, tile_ids):
+PER_STEP = 8
+
+
+def weigh_begin(n_type, info, query, query_id, keys, tile_ids):
     tile, width = query.shape
     heads = width // HEAD
     slots = n_type * EXP_CAP
     block = pl.BlockSpec((tile, PER_STEP * HEAD), lambda i: (0, i))
     return pl.pallas_call(
-        functools.partial(weigh_begin_kernel, n_type, tile_ids),
+        functools.partial(in_middle, weigh_begin_body, n_type, tile_ids, query_id),
         grid=(heads // PER_STEP,),
         out_shape=[
             jax.ShapeDtypeStruct((heads, 2 * 8, tile), jnp.float32),
             jax.ShapeDtypeStruct((slots, width), jnp.bfloat16),
-        ],
+        ][: 2 - query_id],
         in_specs=[VMEM] + [block] * (1 + len(keys)),
         out_specs=[
             pl.BlockSpec((PER_STEP, 2 * 8, tile), lambda i: (i, 0, 0)),
             pl.BlockSpec((slots, PER_STEP * HEAD), lambda i: (0, i)),
-        ],
+        ][: 2 - query_id],
         compiler_params=params(16, dimension_semantics=("arbitrary",)),
-        cost_estimate=cost(0, 0),
+        cost_estimate=cost(0, 16 * tile * tile * heads),
     )(info, query, *keys)
 
 
-def weigh_end_kernel(n_type, n_query, tile_ids, info_ref, kept_ref, state_ref, last_ref, *refs):
-    query_refs, refs = refs[:n_query], refs[n_query:]
-    n_key = len(refs) - n_query - 1
-    key_refs, refs = refs[:n_key], refs[n_key:]
-    out_refs, bias_ref = refs[:n_query], refs[n_query]
+def weigh_end_body(step, n_type, tile_ids, info_ref, kept_ref, last_ref, *refs):
+    n_query = (len(refs) - 1) // 3
+    query_refs, state_refs = refs[:n_query], refs[n_query : 2 * n_query]
+    out_refs, bias_ref = refs[2 * n_query : 3 * n_query], refs[3 * n_query]
     slots, width = kept_ref.shape
     tile = last_ref.shape[0]
 
-    @pl.when(pl.program_id(0) == 0)
+    @pl.when(step == 0)
     def _():
         bias = [jnp.full((slots, tile), MASKED, jnp.float32) for _ in range(n_query)]
         for s in tile_ids:
@@ -348,57 +360,42 @@
     last_mask = jnp.concatenate(
         [mask_row(n_type, q, tile_ids[-1], info_ref) for q in range(n_query)], axis=1
     )
-    for at in range(0, width, 2 * HEAD):
-        if n_query > 1:
-            rest = pair_scores(
-                n_type, 1, tile_ids[:-1], info_ref, key_refs, query_refs[1], pl.ds(at, 2 * HEAD)
-            )
-            rest_top = top_of(rest)
-        for i in range(2):
-            mine = slice(i * tile, (i + 1) * tile)
-            head = at // HEAD + i
-            span = slice(head * HEAD, (head + 1) * HEAD)
-            scores = product(
-                jnp.concatenate([last_ref[:, span], kept[:, span]], axis=0),
-                jnp.concatenate([ref[:, span] for ref in query_refs], axis=0),
-            )
-            last = scores[:tile] + last_mask
-            state_top = state_ref[head, 8:9]
-            tops = [state_top] + ([rest_top[:, mine]] if n_query > 1 else [])
-            top = jnp.maximum(jnp.concatenate(tops, axis=1), jnp.max(last, axis=0, keepdims=True))
-            own_top = top[:, :tile]
-            before = [state_ref[head, 0:1] * jnp.exp2((state_top - own_top) * FACTOR)]
-            if n_query > 1:
-                before.append(total_of([x[:, mine] for x in rest], top[:, tile:]))
-            total = total_of([last], top) + jnp.concatenate(before, axis=1)
-            weights = jnp.exp2((scores[tile:] + bias_ref[...] - top) * FACTOR) * (1.0 / total)
-            for q in range(n_query):
-                out_refs[q][head] = weights[:, q * tile : (q + 1) * tile].astype(jnp.bfloat16)
-
-
-def weigh_end(n_type, info, begun, last_key, queries, keys, tile_ids, first_head, heads):
-    state, kept = begun
+    for head in range(width // HEAD):
+        span = slice(head * HEAD, (head + 1) * HEAD)
+        scores = product(
+            jnp.concatenate([last_ref[:, span], kept[:, span]], axis=0),
+            jnp.concatenate([ref[:, span] for ref in query_refs], axis=0),
+        )
+        last = scores[:tile] + last_mask
+        before = jnp.concatenate([ref[head, 8:9] for ref in state_refs], axis=1)
+        begun = jnp.concatenate([ref[head, 0:1] for ref in state_refs], axis=1)
+        top = jnp.maximum(before, jnp.max(last, axis=0, keepdims=True))
+        total = total_of([last], top) + begun * jnp.exp2((before - top) * FACTOR)
+        weights = jnp.exp2((scores[tile:] + bias_ref[...] - top) * FACTOR) * (1.0 / total)
+        for q in range(n_query):
+            out_refs[q][head] = weights[:, q * tile : (q + 1) * tile].astype(jnp.bfloat16)
+
+
+def weigh_end(n_type, info, kept, last_key, queries, states, tile_ids, first_head, heads):
     tile = last_key.shape[0]
     n_query = len(queries)
     slots = n_type * EXP_CAP
     first = first_head // PER_STEP
     block = pl.BlockSpec((tile, PER_STEP * HEAD), lambda i: (0, i + first))
+    state_block = pl.BlockSpec((PER_STEP, 2 * 8, tile), lambda i: (i + first, 0, 0))
     out_block = pl.BlockSpec((PER_STEP, slots, tile), lambda i: (i, 0, 0))
     return pl.pallas_call(
-        functools.partial(weigh_end_kernel, n_type, n_query, tile_ids),
+        functools.partial(in_middle, weigh_end_body, n_type, tile_ids),
         grid=(heads // PER_STEP,),
         out_shape=[jax.ShapeDtypeStruct((heads, slots, tile), jnp.bfloat16)] * n_query,
-        in_specs=[
-            VMEM,
-            pl.BlockSpec((slots, PER_STEP * HEAD), lambda i: (0, i + first)),
-            pl.BlockSpec((PER_STEP, 2 * 8, tile), lambda i: (i + first, 0, 0)),
-        ]
-        + [block] * (1 + n_query + len(keys)),
+        in_specs=[VMEM, pl.BlockSpec((slots, PER_STEP * HEAD), lambda i: (0, i + first))]
+        + [block] * (1 + n_query)
+        + [state_block] * n_query,
         out_specs=[out_block] * n_query,
         scratch_shapes=[pltpu.VMEM((slots, n_query * tile), jnp.float32)],
         compiler_params=params(16, dimension_semantics=("arbitrary",)),
-        cost_estimate=cost(0, 16 * tile * tile * heads),
-    )(info, kept, state, last_key, *queries, *keys)
+        cost_estimate=cost(0, 0),
+    )(info, kept, last_key, *queries, *states)
 
 
 def finish_kernel(n_type, n_part, info_ref, *refs):
@@ -483,16 +480,15 @@
         pieces = [pieces[0]] + [swap(pieces[p], "dp", n_dp, 2 * p) for p in range(1, n_same)]
         begun = None
         if beside:
-            begun = weigh_begin(n_type, *beside, [0, 1, 3])
+            info, queries, tiles = beside
+            begun = weigh_begin(n_type, info, queries, 0, tiles, [0, 1, 3])
             pieces, begun = tie((pieces, begun))
         total = pieces[0].astype(jnp.float32)
         for piece in pieces[1:]:
             total = total + piece.astype(jnp.float32)
-        expert_rows = total.astype(jnp.bfloat16)
-        return jnp.concatenate([expert_rows, swap(expert_rows, "type", n_type, 1)], axis=0), begun
-
-    def spread(rows):
-        step = 2
+        return total.astype(jnp.bfloat16), begun
+
+    def spread(rows, step=1):
         while step < n_type:
             rows = jnp.concatenate([rows, swap(rows, "type", n_type, step)], axis=0)
             step *= 2
@@ -510,21 +506,25 @@
         info, own_rows, away_rows = as_one_step(experts, incoming, *weights)
         own_rows, near = tie((own_rows, near))
         far = lax.ppermute(near, "type", across)
-        expert_rows, begun = as_one_step(
-            gather_sum, own_rows, away_rows, info, queries, [keys, near, other]
+        tiles = [keys, near, other]
+        expert_rows, (state, kept) = as_one_step(
+            gather_sum, own_rows, away_rows, info, queries, tiles
         )
-        values = spread(expert_rows)
-        expert_rows, begun, guest, far = tie((expert_rows, begun, guest, far))
+        twin = swap(expert_rows, "type", n_type, 1)
+        expert_rows, guest = tie((expert_rows, guest))
+        (guest_state,) = weigh_begin(n_type, info, guest, 1, tiles, [0, 1, 3])
+        twin, guest_state, far = tie((twin, guest_state, far))
+        values = spread(jnp.concatenate([expert_rows, twin], axis=0), 2)
         own_weights, back_weights = [], []
-        ends = [0, heads // 2 + PER_STEP, heads]
+        ends = [0, heads // 2, heads - 8, heads]
         for first, last in zip(ends[:-1], ends[1:]):
             own, theirs = weigh_end(
                 n_type,
                 info,
-                begun,
+                kept,
                 far,
                 [queries, guest],
-                [keys, near, other],
+                [state, guest_state],
                 [0, 1, 3, 2],
                 first,
                 last - first,
@@ -537,9 +537,9 @@
         values = spread(expert_rows)
         tiles = [keys] + [swap(keys, "type", n_type, s) for s in range(1, n_type)]
         ids = list(range(n_type))
-        begun = weigh_begin(n_type, info, queries, tiles[:-1], ids[:-1])
+        state, kept = weigh_begin(n_type, info, queries, 0, tiles[:-1], ids[:-1])
         own_weights = list(
-            weigh_end(n_type, info, begun, tiles[-1], [queries], [], ids, 0, heads)
+            weigh_end(n_type, info, kept, tiles[-1], [queries], [state], ids, 0, heads)
         )
         back_weights = own_weights
     expert_out, attended = finish(n_type, info, own_weights, back_weights, values, tile)

time: 98.8 us -> 96.5 us (0.977)
  Pallas kernels: 31.7 us -> 23 us
  waiting for transfers between devices: 29.4 us -> 34.5 us
  starting transfers between devices: 34.3 us -> 37.4 us
  other arithmetic: 1.9 us -> 0.21 us
    pallas_call x3 -> x5, Pallas kernels: 15.9 us -> 7.29 us  [the longest x2 5.17 us: weigh_begin(): pl.pallas_call(functools.partial(in_middle, weigh_begin_body, n_type, til...]
    ppermute x1, waiting for transfers between devices: 0.01 us -> 3.89 us  [on_device(): guest = lax.ppermute(queries, 'type', to_middle)]
    ppermute x13, waiting for transfers between devices: 20.1 us -> 22.2 us  [swap(): return lax.ppermute(x, axis, [(i, i ^ s) for i in range(size)])]
    ppermute x13, starting transfers between devices: 22.2 us -> 24.1 us  [swap(): return lax.ppermute(x, axis, [(i, i ^ s) for i in range(size)])]
    ppermute x2 -> x3, starting transfers between devices: 2.58 us -> 3.88 us  [on_device(): back_weights.append(lax.ppermute(theirs, 'type', to_end))]
    ppermute x2 -> x3, waiting for transfers between devices: 9.29 us -> 8.38 us  [on_device(): back_weights.append(lax.ppermute(theirs, 'type', to_end))]
  transfers between devices with their start and end apart: 19 -> 20, of which waited for: 8 -> 13; matrix products, arithmetic and copies ran while one was open for 2% -> 0% of each run, Pallas kernels for 28% -> 19%
where the time goes in v4:
time: 96.5 us; the launch traced here: 96.1 us
  starting transfers between devices  37.4 us (39%)
  waiting for transfers between devices  34.5 us (36%)
  Pallas kernels  23 us (24%)
    ppermute x13, starting transfers between devices, swap(): return lax.ppermute(x, axis, [(i, i ^ s) for i in range(size)])  24.1 us
    ppermute x13, waiting for transfers between devices, swap(): return lax.ppermute(x, axis, [(i, i ^ s) for i in range(size)])  22.2 us
    ppermute x3, waiting for transfers between devices, on_device(): back_weights.append(lax.ppermute(theirs, 'type', to_end))  8.38 us
    pallas_call x1, Pallas kernels, fetch(): pl.pallas_call(functools.partial(fetch_kernel, count), out_shape=[pltpu.V...  7.28 us
    pallas_call x2, Pallas kernels, weigh_begin(): pl.pallas_call(functools.partial(in_middle, weigh_begin_body, n_type, til...  5.17 us
    ppermute x1, starting transfers between devices, on_device(): near = lax.ppermute(keys, 'type', to_middle)  4.92 us
    ppermute x1, waiting for transfers between devices, on_device(): guest = lax.ppermute(queries, 'type', to_middle)  3.89 us
    ppermute x3, starting transfers between devices, on_device(): back_weights.append(lax.ppermute(theirs, 'type', to_end))  3.88 us
  transfers between devices with their start and end apart: 20, of which 13 were waited for; matrix products, arithmetic and copies ran while one was open for 0% of the time, Pallas kernels for 19%

profile of v4, /device:TPU:0, one launch (start us, length us, event | category | flops | bytes accessed | tf_op | source)
XLA Modules:
  0.0 96.1 jit_solution(10667518265892333274)
XLA Ops:
  0.6 2.7 %shard_map.98 = (bf16[16,4224]{1,0:T(8,128)(2,1)S(1)}, bf16[16,4224]{1,0:T(8,128)(2,1)S(1)}, bf16[16,4224]{1,0:T(8,128)(2,1)S(1)}, bf16[16,4224]{1,0:T(8,128)(2,1)S(1)}) custom-call(s32[1,128]{1,0:T(1,128)} %bitcast.8, s32[1,4]{1,0:T(1,128)} %bitcast.9, bf16[128,4096]{1,0:T(8,128)(2,1)} %tokens_ref.1), custom_call_target="tpu_custom_call" | custom-call | tf_op jit(solution)/shard_map/pallas_call | solution.py:87
  3.3 3.1 %collective-permute-start.8 = (bf16[16,4224]{1,0:T(8,128)(2,1)S(1)}, bf16[16,4224]{1,0:T(8,128)(2,1)S(1)}, u32[]{:S(2)}, u32[]{:S(2)}) collective-permute-start(bf16[16,4224]{1,0:T(8,128)(2,1)S(1)} %get-tuple-element.99), channel_id=1, source_target_pairs={{0,1},{1,0},{2,3},{3,2},{4,5},{5,4},{6,7},{7,6},{8,9},{9,8},{10,11... | collective-permute-start | bytes 405512 | tf_op jit(solution)/shard_map/ppermute | solution.py:448
  6.4 2.6 %collective-permute-start.9 = (bf16[16,4224]{1,0:T(8,128)(2,1)S(1)}, bf16[16,4224]{1,0:T(8,128)(2,1)S(1)}, u32[]{:S(2)}, u32[]{:S(2)}) collective-permute-start(bf16[16,4224]{1,0:T(8,128)(2,1)S(1)} %get-tuple-element.100), channel_id=1, source_target_pairs={{0,2},{1,3},{2,0},{3,1},{4,6},{5,7},{6,4},{7,5},{8,10},{9,11},{10,... | collective-permute-start | bytes 405512 | tf_op jit(solution)/shard_map/ppermute | solution.py:448
  9.0 2.6 %collective-permute-done.8 = bf16[16,4224]{1,0:T(8,128)(2,1)S(1)} collective-permute-done((bf16[16,4224]{1,0:T(8,128)(2,1)S(1)}, bf16[16,4224]{1,0:T(8,128)(2,1)S(1)}, u32[]{:S(2)}, u32[]{:S(2)}) %collective-permute-start.8) | collective-permute-done | bytes 135200 | tf_op jit(solution)/shard_map/ppermute | solution.py:448
  11.7 8.0 %collective-permute-done.9 = bf16[16,4224]{1,0:T(8,128)(2,1)S(1)} collective-permute-done((bf16[16,4224]{1,0:T(8,128)(2,1)S(1)}, bf16[16,4224]{1,0:T(8,128)(2,1)S(1)}, u32[]{:S(2)}, u32[]{:S(2)}) %collective-permute-start.9) | collective-permute-done | bytes 135200 | tf_op jit(solution)/shard_map/ppermute | solution.py:448
  19.6 4.9 %collective-permute-start.11 = (bf16[128,4096]{1,0:T(8,128)(2,1)}, bf16[128,4096]{1,0:T(8,128)(2,1)}, u32[]{:S(2)}, u32[]{:S(2)}) collective-permute-start(bf16[128,4096]{1,0:T(8,128)(2,1)} %args_2_), channel_id=1, source_target_pairs={{0,1},{3,2},{4,5},{7,6},{8,9},{11,10},{12,13},{15,14},{16,17},{19,... | collective-permute-start | bytes 3145736 | tf_op jit(solution)/shard_map/ppermute | solution.py:503
  24.6 1.6 %collective-permute-start.12 = (bf16[128,4096]{1,0:T(8,128)(2,1)}, bf16[128,4096]{1,0:T(8,128)(2,1)}, u32[]{:S(2)}, u32[]{:S(2)}) collective-permute-start(bf16[128,4096]{1,0:T(8,128)(2,1)} %args_2_), channel_id=1, source_target_pairs={{1,2},{2,1},{5,6},{6,5},{9,10},{10,9},{13,14},{14,13},{17,18},{18,... | collective-permute-start | bytes 3145736 | tf_op jit(solution)/shard_map/ppermute | solution.py:504
  26.2 2.2 %collective-permute-start.14 = (bf16[128,4096]{1,0:T(8,128)(2,1)}, bf16[128,4096]{1,0:T(8,128)(2,1)S(1)}, u32[]{:S(2)}, u32[]{:S(2)}) collective-permute-start(bf16[128,4096]{1,0:T(8,128)(2,1)} %args_3_.5), channel_id=1, source_target_pairs={{0,1},{3,2},{4,5},{7,6},{8,9},{11,10},{12,13},{15,14},{16,17},{19,... | collective-permute-start | bytes 3145736 | tf_op jit(solution)/shard_map/ppermute | solution.py:505
  28.4 0.0 copy-start
  28.4 19.8 %conditional.2 = (f32[12,128]{1,0:T(8,128)S(1)}, f32[64,4096]{1,0:T(8,128)S(1)}, bf16[64,4096]{1,0:T(8,128)(2,1)S(1)}) conditional(s32[]{:T(128)} %convert_element_type.25, () %tuple.29, (bf16[16,4224]{1,0:T(8,128)(2,1)S(1)}, bf16[16,4224]{1,0:T(8,128)(2,1)S(1)}, bf16[16,4224]{1,0:T(8,128)(2,1)S(1)}, bf16[16,4224]{1,0:T(8,128)(2,1)S(1)}, ...), branch_computations={%region_0.0_spmd, %region_1.0_spmd} | conditional | bytes 48758968 | solution.py:454
  28.5 0.4 branch_1_fun.4
  28.9 1.6 %collective-permute-start.1 = (bf16[16,4096]{1,0:T(8,128)(2,1)S(1)}, bf16[16,4096]{1,0:T(8,128)(2,1)S(1)}, u32[]{:S(2)}, u32[]{:S(2)}) collective-permute-start(bf16[16,4096]{1,0:T(8,128)(2,1)S(1)} %get-tuple-element.43), channel_id=1, source_target_pairs={{0,16},{4,20},{8,24},{12,28},{16,0},{20,4},{24,8},{28,12},{1,17},{... | collective-permute-start | bytes 393224 | tf_op jit(solution)/shard_map/cond/branch_1_fun/ppermute | solution.py:448
  30.4 1.5 %collective-permute-start = (bf16[16,4096]{1,0:T(8,128)(2,1)S(1)}, bf16[16,4096]{1,0:T(8,128)(2,1)S(1)}, u32[]{:S(2)}, u32[]{:S(2)}) collective-permute-start(bf16[16,4096]{1,0:T(8,128)(2,1)S(1)} %get-tuple-element.43), channel_id=1, source_target_pairs={{0,8},{4,12},{8,0},{12,4},{16,24},{20,28},{24,16},{28,20},{1,9},{5... | collective-permute-start | bytes 393224 | tf_op jit(solution)/shard_map/cond/branch_1_fun/ppermute | solution.py:448
  31.9 2.0 %collective-permute-done.1 = bf16[16,4096]{1,0:T(8,128)(2,1)S(1)} collective-permute-done((bf16[16,4096]{1,0:T(8,128)(2,1)S(1)}, bf16[16,4096]{1,0:T(8,128)(2,1)S(1)}, u32[]{:S(2)}, u32[]{:S(2)}) %collective-permute-start.1) | collective-permute-done | bytes 131104 | tf_op jit(solution)/shard_map/cond/branch_1_fun/ppermute | solution.py:448
  33.9 1.5 %collective-permute-start.2 = (bf16[16,4096]{1,0:T(8,128)(2,1)S(1)}, bf16[16,4096]{1,0:T(8,128)(2,1)S(1)}, u32[]{:S(2)}, u32[]{:S(2)}) collective-permute-start(bf16[16,4096]{1,0:T(8,128)(2,1)S(1)} %collective-permute-done.1), channel_id=1, source_target_pairs={{0,8},{4,12},{8,0},{12,4},{16,24},{20,28},{24,16},{28,20},{1,9},{5... | collective-permute-start | bytes 393224 | tf_op jit(solution)/shard_map/cond/branch_1_fun/ppermute | solution.py:448
  35.4 7.3 %branch_1_fun.5 = (bf16[4096,896]{1,0:T(8,128)(2,1)S(1)}, bf16[4096,896]{1,0:T(8,128)(2,1)S(1)}, bf16[896,4096]{1,0:T(8,128)(2,1)S(1)}) custom-call(bf16[4096,896]{1,0:T(8,128)(2,1)} %bitcast.5, bf16[4096,896]{1,0:T(8,128)(2,1)} %bitcast.6, bf16[896,4096]{1,0:T(8,128)(2,1)} %bitcast.7), custom_call_target="tpu_custom_call" | custom-call | bytes 44040192 | tf_op jit(solution)/shard_map/cond/branch_1_fun/pallas_call | solution.py:114
  42.8 0.1 collective-permute-start.3
  42.9 1.9 %collective-permute-done.3.far_ref = bf16[64,4096]{1,0:T(8,128)(2,1)S(1)} collective-permute-done((bf16[64,4096]{1,0:T(8,128)(2,1)S(1)}, bf16[64,4096]{1,0:T(8,128)(2,1)S(1)}, u32[]{:S(2)}, u32[]{:S(2)}) %collective-permute-start.3) | collective-permute-done | bytes 524320 | tf_op jit(solution)/shard_map/cond/branch_1_fun/ppermute | solution.py:448
  44.7 3.4 %branch_1_fun.6 = (f32[64,4096]{1,0:T(8,128)S(1)}, bf16[64,4096]{1,0:T(8,128)(2,1)S(1)}) custom-call(bf16[64,4096]{1,0:T(8,128)(2,1)S(1)} %constant_dynamic-update-slice_fusion.near_ref, bf16[64,4096]{1,0:T(8,128)(2,1)S(1)} %collective-permute-done.3.far_ref, bf16[4096,896]{1,0:T(8,128)(2,1)S(1)} %get-tuple-element.47.gate_ref, ...), custom_call_target="tpu_custom_call" | custom-call | tf_op jit(solution)/shard_map/cond/branch_1_fun/pallas_call | solution.py:216
  48.2 0.7 collective-permute-start.15
  49.0 11.6 %conditional.3 = (bf16[16,4096]{1,0:T(8,128)(2,1)S(1)}, f32[32,16,128]{2,1,0:T(8,128)S(1)}, bf16[64,4096]{1,0:T(8,128)(2,1)S(1)}) conditional(s32[]{:T(128)} %convert_element_type.25, () %tuple.32, (bf16[64,4096]{1,0:T(8,128)(2,1)S(1)}, f32[64,4096]{1,0:T(8,128)S(1)}, f32[12,128]{1,0:T(8,128)S(1)}, bf16[128,4096]{1,0:T(8,128)(2,1)S(1)}, ...), branch_computations={%region_2.0_spmd, %region_3.0_spmd} | conditional | flops 1310720 | bytes 15859896 | solution.py:454
  49.0 0.2 collective-permute-start.4
  49.2 1.8 %collective-permute-done.4 = bf16[64,4096]{1,0:T(8,128)(2,1)S(1)} collective-permute-done((bf16[64,4096]{1,0:T(8,128)(2,1)S(1)}, bf16[64,4096]{1,0:T(8,128)(2,1)S(1)}, u32[]{:S(2)}, u32[]{:S(2)}) %collective-permute-start.4) | collective-permute-done | bytes 524320 | tf_op jit(solution)/shard_map/cond/branch_1_fun/ppermute | solution.py:448
  51.0 0.1 add_convert_fusion
  51.1 1.8 %collective-permute-start.7 = (bf16[16,4096]{1,0:T(8,128)(2,1)S(1)}, bf16[16,4096]{1,0:T(8,128)(2,1)S(1)}, u32[]{:S(2)}, u32[]{:S(2)}) collective-permute-start(bf16[16,4096]{1,0:T(8,128)(2,1)S(1)} %get-tuple-element.133), channel_id=1, source_target_pairs={{0,24},{4,28},{8,16},{12,20},{16,8},{20,12},{24,0},{28,4},{1,25},{... | collective-permute-start | bytes 393224 | tf_op jit(solution)/shard_map/cond/branch_1_fun/ppermute | solution.py:448
  52.9 0.5 collective-permute-start.6
  53.4 1.3 %collective-permute-start.5 = (bf16[16,4096]{1,0:T(8,128)(2,1)S(1)}, bf16[16,4096]{1,0:T(8,128)(2,1)S(1)}, u32[]{:S(2)}, u32[]{:S(2)}) collective-permute-start(bf16[16,4096]{1,0:T(8,128)(2,1)S(1)} %get-tuple-element.135), channel_id=1, source_target_pairs={{0,8},{4,12},{8,0},{12,4},{16,24},{20,28},{24,16},{28,20},{1,9},{5... | collective-permute-start | bytes 393224 | tf_op jit(solution)/shard_map/cond/branch_1_fun/ppermute | solution.py:448
  54.6 2.6 %branch_1_fun.7 = (f32[32,16,128]{2,1,0:T(8,128)S(1)}, bf16[64,4096]{1,0:T(8,128)(2,1)S(1)}) custom-call(f32[12,128]{1,0:T(8,128)S(1)} %get-tuple-element.54.args_0_, bf16[128,4096]{1,0:T(8,128)(2,1)S(1)} %get-tuple-element.55.args_1_, bf16[128,4096]{1,0:T(8,128)(2,1)} %get-tuple-element.56.args_2_, bf16[128,4096]{1,0:T(8,128)(2,1)} %get-tuple-element.57.args_3_, ...), custom_call_target="tpu_custom_call" | custom-call | bytes 8388608 | tf_op jit(solution)/shard_map/cond/branch_1_fun/pallas_call | solution.py:322
  57.3 1.1 %collective-permute-done.7 = bf16[16,4096]{1,0:T(8,128)(2,1)S(1)} collective-permute-done((bf16[16,4096]{1,0:T(8,128)(2,1)S(1)}, bf16[16,4096]{1,0:T(8,128)(2,1)S(1)}, u32[]{:S(2)}, u32[]{:S(2)}) %collective-permute-start.7) | collective-permute-done | bytes 131104 | tf_op jit(solution)/shard_map/cond/branch_1_fun/ppermute | solution.py:448
  58.4 2.0 %collective-permute-done.6 = bf16[16,4096]{1,0:T(8,128)(2,1)S(1)} collective-permute-done((bf16[16,4096]{1,0:T(8,128)(2,1)S(1)}, bf16[16,4096]{1,0:T(8,128)(2,1)S(1)}, u32[]{:S(2)}, u32[]{:S(2)}) %collective-permute-start.6) | collective-permute-done | bytes 131104 | tf_op jit(solution)/shard_map/cond/branch_1_fun/ppermute | solution.py:448
  60.4 0.1 collective-permute-done.5
  60.5 0.1 add_convert_fusion.1
  60.6 0.0 copy-start.1
  60.6 4.5 %collective-permute-start.13 = (bf16[16,4096]{1,0:T(8,128)(2,1)S(1)}, bf16[16,4096]{1,0:T(8,128)(2,1)S(1)}, u32[]{:S(2)}, u32[]{:S(2)}) collective-permute-start(bf16[16,4096]{1,0:T(8,128)(2,1)S(1)} %get-tuple-element.125), channel_id=1, source_target_pairs={{0,1},{1,0},{2,3},{3,2},{4,5},{5,4},{6,7},{7,6},{8,9},{9,8},{10,11... | collective-permute-start | bytes 393224 | tf_op jit(solution)/shard_map/ppermute | solution.py:448
  65.1 3.9 %collective-permute-done.14.args_1_.args_4_ = bf16[128,4096]{1,0:T(8,128)(2,1)S(1)} collective-permute-done((bf16[128,4096]{1,0:T(8,128)(2,1)}, bf16[128,4096]{1,0:T(8,128)(2,1)S(1)}, u32[]{:S(2)}, u32[]{:S(2)}) %collective-permute-start.14) | collective-permute-done | bytes 1048608 | tf_op jit(solution)/shard_map/ppermute | solution.py:505
  69.0 2.6 %shard_map.99.args_6_ = f32[32,16,128]{2,1,0:T(8,128)S(1)} custom-call(f32[12,128]{1,0:T(8,128)S(1)} %get-tuple-element.106.args_0_.info_ref, bf16[128,4096]{1,0:T(8,128)(2,1)S(1)} %collective-permute-done.14.args_1_.args_4_, bf16[128,4096]{1,0:T(8,128)(2,1)} %args_2_, bf16[128,4096]{1,0:T(8,128)(2,1)} %collective-permute-done.11.args_3_, ...), custom_call_target="tpu_custom_call" | custom-call | bytes 8388608 | tf_op jit(solution)/shard_map/pallas_call | solution.py:322
  71.6 5.4 %collective-permute-start.19 = (bf16[32,4096]{1,0:T(8,128)(2,1)S(1)}, bf16[32,4096]{1,0:T(8,128)(2,1)S(1)}, u32[]{:S(2)}, u32[]{:S(2)}) collective-permute-start(bf16[32,4096]{1,0:T(8,128)(2,1)S(1)} %pad_maximum_fusion.1), channel_id=1, source_target_pairs={{0,2},{1,3},{2,0},{3,1},{4,6},{5,7},{6,4},{7,5},{8,10},{9,11},{10,... | collective-permute-start | bytes 786440 | tf_op jit(solution)/shard_map/ppermute | solution.py:448
  77.0 1.0 %shard_map.102 = (bf16[8,64,128]{2,1,0:T(8,128)(2,1)S(1)}, bf16[8,64,128]{2,1,0:T(8,128)(2,1)S(1)}) custom-call(f32[12,128]{1,0:T(8,128)S(1)} %get-tuple-element.106.args_0_.info_ref, bf16[64,4096]{1,0:T(8,128)(2,1)} %copy-done.1, bf16[128,4096]{1,0:T(8,128)(2,1)S(1)} %collective-permute-done.15.args_2_, bf16[128,4096]{1,0:T(8,128)(2,1)S(1)} %copy-done, ...), custom_call_target="tpu_custom_call" | custom-call | tf_op jit(solution)/shard_map/pallas_call | solution.py:387
  78.0 0.9 shard_map.101
  78.9 0.2 shard_map.100
  79.2 1.3 %collective-permute-start.18 = (bf16[8,64,128]{2,1,0:T(8,128)(2,1)S(1)}, bf16[8,64,128]{2,1,0:T(8,128)(2,1)S(1)}, u32[]{:S(2)}, u32[]{:S(2)}) collective-permute-start(bf16[8,64,128]{2,1,0:T(8,128)(2,1)S(1)} %get-tuple-element.124), channel_id=1, source_target_pairs={{1,0},{2,3},{5,4},{6,7},{9,8},{10,11},{13,12},{14,15},{17,16},{18,... | collective-permute-start | bytes 393224 | tf_op jit(solution)/shard_map/ppermute | solution.py:533
  80.5 1.3 %collective-permute-start.17 = (bf16[8,64,128]{2,1,0:T(8,128)(2,1)S(1)}, bf16[8,64,128]{2,1,0:T(8,128)(2,1)S(1)}, u32[]{:S(2)}, u32[]{:S(2)}) collective-permute-start(bf16[8,64,128]{2,1,0:T(8,128)(2,1)S(1)} %get-tuple-element.123), channel_id=1, source_target_pairs={{1,0},{2,3},{5,4},{6,7},{9,8},{10,11},{13,12},{14,15},{17,16},{18,... | collective-permute-start | bytes 393224 | tf_op jit(solution)/shard_map/ppermute | solution.py:533
  81.8 1.3 %collective-permute-start.16 = (bf16[16,64,128]{2,1,0:T(8,128)(2,1)S(1)}, bf16[16,64,128]{2,1,0:T(8,128)(2,1)S(1)}, u32[]{:S(2)}, u32[]{:S(2)}) collective-permute-start(bf16[16,64,128]{2,1,0:T(8,128)(2,1)S(1)} %get-tuple-element.122), channel_id=1, source_target_pairs={{1,0},{2,3},{5,4},{6,7},{9,8},{10,11},{13,12},{14,15},{17,16},{18,... | collective-permute-start | bytes 786440 | tf_op jit(solution)/shard_map/ppermute | solution.py:533
  83.1 2.7 %collective-permute-done.19 = bf16[32,4096]{1,0:T(8,128)(2,1)S(1)} collective-permute-done((bf16[32,4096]{1,0:T(8,128)(2,1)S(1)}, bf16[32,4096]{1,0:T(8,128)(2,1)S(1)}, u32[]{:S(2)}, u32[]{:S(2)}) %collective-permute-start.19) | collective-permute-done | bytes 262176 | tf_op jit(solution)/shard_map/ppermute | solution.py:448
  85.8 2.8 %collective-permute-done.18.refs_5_ = bf16[8,64,128]{2,1,0:T(8,128)(2,1)S(1)} collective-permute-done((bf16[8,64,128]{2,1,0:T(8,128)(2,1)S(1)}, bf16[8,64,128]{2,1,0:T(8,128)(2,1)S(1)}, u32[]{:S(2)}, u32[]{:S(2)}) %collective-permute-start.18) | collective-permute-done | bytes 131104 | tf_op jit(solution)/shard_map/ppermute | solution.py:533
  88.7 2.7 %collective-permute-done.17.refs_4_ = bf16[8,64,128]{2,1,0:T(8,128)(2,1)S(1)} collective-permute-done((bf16[8,64,128]{2,1,0:T(8,128)(2,1)S(1)}, bf16[8,64,128]{2,1,0:T(8,128)(2,1)S(1)}, u32[]{:S(2)}, u32[]{:S(2)}) %collective-permute-start.17) | collective-permute-done | bytes 131104 | tf_op jit(solution)/shard_map/ppermute | solution.py:533
  91.4 2.8 %collective-permute-done.16.refs_3_ = bf16[16,64,128]{2,1,0:T(8,128)(2,1)S(1)} collective-permute-done((bf16[16,64,128]{2,1,0:T(8,128)(2,1)S(1)}, bf16[16,64,128]{2,1,0:T(8,128)(2,1)S(1)}, u32[]{:S(2)}, u32[]{:S(2)}) %collective-permute-start.16) | collective-permute-done | bytes 262176 | tf_op jit(solution)/shard_map/ppermute | solution.py:533
  94.2 1.8 %shard_map.103 = (bf16[128,4096]{1,0:T(8,128)(2,1)}, bf16[128,4096]{1,0:T(8,128)(2,1)}) custom-call(f32[12,128]{1,0:T(8,128)S(1)} %get-tuple-element.106.args_0_.info_ref, bf16[16,64,128]{2,1,0:T(8,128)(2,1)S(1)} %get-tuple-element.119.refs_0_, bf16[8,64,128]{2,1,0:T(8,128)(2,1)S(1)} %get-tuple-element.120.refs_1_, ...), custom_call_target="tpu_custom_call" | custom-call | tf_op jit(solution)/shard_map/pallas_call | solution.py:436
  (19 shorter events, 0.2 us)
Async XLA Ops:
  3.3 8.3 %collective-permute-start.8 = (bf16[16,4224]{1,0:T(8,128)(2,1)S(1)}, bf16[16,4224]{1,0:T(8,128)(2,1)S(1)}, u32[]{:S(2)}, u32[]{:S(2)}) collective-permute-start(bf16[16,4224]{1,0:T(8,128)(2,1)S(1)} %get-tuple-element.99), channel_id=1, source_target_pairs={{0,1},{1,0},{2,3},{3,2},{4,5},{5,4},{6,7},{7,6},{8,9},{9,8},{10,11... | collective-permute-start | bytes 405512 | tf_op jit(solution)/shard_map/ppermute | solution.py:448
  6.4 13.2 %collective-permute-start.9 = (bf16[16,4224]{1,0:T(8,128)(2,1)S(1)}, bf16[16,4224]{1,0:T(8,128)(2,1)S(1)}, u32[]{:S(2)}, u32[]{:S(2)}) collective-permute-start(bf16[16,4224]{1,0:T(8,128)(2,1)S(1)} %get-tuple-element.100), channel_id=1, source_target_pairs={{0,2},{1,3},{2,0},{3,1},{4,6},{5,7},{6,4},{7,5},{8,10},{9,11},{10,... | collective-permute-start | bytes 405512 | tf_op jit(solution)/shard_map/ppermute | solution.py:448
  9.0 10.6 %collective-permute-start.10 = (bf16[16,4224]{1,0:T(8,128)(2,1)S(1)}, bf16[16,4224]{1,0:T(8,128)(2,1)S(1)}, u32[]{:S(2)}, u32[]{:S(2)}) collective-permute-start(bf16[16,4224]{1,0:T(8,128)(2,1)S(1)} %get-tuple-element.101), channel_id=1, source_target_pairs={{0,3},{1,2},{2,1},{3,0},{4,7},{5,6},{6,5},{7,4},{8,11},{9,10},{10,... | collective-permute-start | bytes 405512 | tf_op jit(solution)/shard_map/ppermute | solution.py:448
  19.6 28.6 %collective-permute-start.11 = (bf16[128,4096]{1,0:T(8,128)(2,1)}, bf16[128,4096]{1,0:T(8,128)(2,1)}, u32[]{:S(2)}, u32[]{:S(2)}) collective-permute-start(bf16[128,4096]{1,0:T(8,128)(2,1)} %args_2_), channel_id=1, source_target_pairs={{0,1},{3,2},{4,5},{7,6},{8,9},{11,10},{12,13},{15,14},{16,17},{19,... | collective-permute-start | bytes 3145736 | tf_op jit(solution)/shard_map/ppermute | solution.py:503
  24.6 24.4 %collective-permute-start.12 = (bf16[128,4096]{1,0:T(8,128)(2,1)}, bf16[128,4096]{1,0:T(8,128)(2,1)}, u32[]{:S(2)}, u32[]{:S(2)}) collective-permute-start(bf16[128,4096]{1,0:T(8,128)(2,1)} %args_2_), channel_id=1, source_target_pairs={{1,2},{2,1},{5,6},{6,5},{9,10},{10,9},{13,14},{14,13},{17,18},{18,... | collective-permute-start | bytes 3145736 | tf_op jit(solution)/shard_map/ppermute | solution.py:504
  26.2 42.8 %collective-permute-start.14 = (bf16[128,4096]{1,0:T(8,128)(2,1)}, bf16[128,4096]{1,0:T(8,128)(2,1)S(1)}, u32[]{:S(2)}, u32[]{:S(2)}) collective-permute-start(bf16[128,4096]{1,0:T(8,128)(2,1)} %args_3_.5), channel_id=1, source_target_pairs={{0,1},{3,2},{4,5},{7,6},{8,9},{11,10},{12,13},{15,14},{16,17},{19,... | collective-permute-start | bytes 3145736 | tf_op jit(solution)/shard_map/ppermute | solution.py:505
  28.4 20.5 %copy-start = (bf16[128,4096]{1,0:T(8,128)(2,1)S(1)}, bf16[128,4096]{1,0:T(8,128)(2,1)}, u32[]{:S(2)}) copy-start(bf16[128,4096]{1,0:T(8,128)(2,1)} %args_3_.5) | copy-start | bytes 3145732
  28.9 5.0 %collective-permute-start.1 = (bf16[16,4096]{1,0:T(8,128)(2,1)S(1)}, bf16[16,4096]{1,0:T(8,128)(2,1)S(1)}, u32[]{:S(2)}, u32[]{:S(2)}) collective-permute-start(bf16[16,4096]{1,0:T(8,128)(2,1)S(1)} %get-tuple-element.43), channel_id=1, source_target_pairs={{0,16},{4,20},{8,24},{12,28},{16,0},{20,4},{24,8},{28,12},{1,17},{... | collective-permute-start | bytes 393224 | tf_op jit(solution)/shard_map/cond/branch_1_fun/ppermute | solution.py:448
  30.4 12.2 %collective-permute-start = (bf16[16,4096]{1,0:T(8,128)(2,1)S(1)}, bf16[16,4096]{1,0:T(8,128)(2,1)S(1)}, u32[]{:S(2)}, u32[]{:S(2)}) collective-permute-start(bf16[16,4096]{1,0:T(8,128)(2,1)S(1)} %get-tuple-element.43), channel_id=1, source_target_pairs={{0,8},{4,12},{8,0},{12,4},{16,24},{20,28},{24,16},{28,20},{1,9},{5... | collective-permute-start | bytes 393224 | tf_op jit(solution)/shard_map/cond/branch_1_fun/ppermute | solution.py:448
  33.9 8.8 %collective-permute-start.2 = (bf16[16,4096]{1,0:T(8,128)(2,1)S(1)}, bf16[16,4096]{1,0:T(8,128)(2,1)S(1)}, u32[]{:S(2)}, u32[]{:S(2)}) collective-permute-start(bf16[16,4096]{1,0:T(8,128)(2,1)S(1)} %collective-permute-done.1), channel_id=1, source_target_pairs={{0,8},{4,12},{8,0},{12,4},{16,24},{20,28},{24,16},{28,20},{1,9},{5... | collective-permute-start | bytes 393224 | tf_op jit(solution)/shard_map/cond/branch_1_fun/ppermute | solution.py:448
  42.8 2.0 %collective-permute-start.3 = (bf16[64,4096]{1,0:T(8,128)(2,1)S(1)}, bf16[64,4096]{1,0:T(8,128)(2,1)S(1)}, u32[]{:S(2)}, u32[]{:S(2)}) collective-permute-start(bf16[64,4096]{1,0:T(8,128)(2,1)S(1)} %constant_dynamic-update-slice_fusion.near_ref), channel_id=1, source_target_pairs={{0,4},{4,0},{8,12},{12,8},{16,20},{20,16},{24,28},{28,24},{1,5},{5... | collective-permute-start | bytes 1572872 | tf_op jit(solution)/shard_map/cond/branch_1_fun/ppermute | solution.py:448
  48.2 23.4 %collective-permute-start.15 = (bf16[128,4096]{1,0:T(8,128)(2,1)}, bf16[128,4096]{1,0:T(8,128)(2,1)S(1)}, u32[]{:S(2)}, u32[]{:S(2)}) collective-permute-start(bf16[128,4096]{1,0:T(8,128)(2,1)} %collective-permute-done.11.args_3_), channel_id=1, source_target_pairs={{1,2},{2,1},{5,6},{6,5},{9,10},{10,9},{13,14},{14,13},{17,18},{18,... | collective-permute-start | bytes 3145736 | tf_op jit(solution)/shard_map/ppermute | solution.py:508
  49.0 2.0 %collective-permute-start.4 = (bf16[64,4096]{1,0:T(8,128)(2,1)S(1)}, bf16[64,4096]{1,0:T(8,128)(2,1)S(1)}, u32[]{:S(2)}, u32[]{:S(2)}) collective-permute-start(bf16[64,4096]{1,0:T(8,128)(2,1)S(1)} %get-tuple-element.53), channel_id=1, source_target_pairs={{0,4},{4,0},{8,12},{12,8},{16,20},{20,16},{24,28},{28,24},{1,5},{5... | collective-permute-start | bytes 1572872 | tf_op jit(solution)/shard_map/cond/branch_1_fun/ppermute | solution.py:448
  51.1 7.3 %collective-permute-start.7 = (bf16[16,4096]{1,0:T(8,128)(2,1)S(1)}, bf16[16,4096]{1,0:T(8,128)(2,1)S(1)}, u32[]{:S(2)}, u32[]{:S(2)}) collective-permute-start(bf16[16,4096]{1,0:T(8,128)(2,1)S(1)} %get-tuple-element.133), channel_id=1, source_target_pairs={{0,24},{4,28},{8,16},{12,20},{16,8},{20,12},{24,0},{28,4},{1,25},{... | collective-permute-start | bytes 393224 | tf_op jit(solution)/shard_map/cond/branch_1_fun/ppermute | solution.py:448
  52.9 7.5 %collective-permute-start.6 = (bf16[16,4096]{1,0:T(8,128)(2,1)S(1)}, bf16[16,4096]{1,0:T(8,128)(2,1)S(1)}, u32[]{:S(2)}, u32[]{:S(2)}) collective-permute-start(bf16[16,4096]{1,0:T(8,128)(2,1)S(1)} %get-tuple-element.134), channel_id=1, source_target_pairs={{0,16},{4,20},{8,24},{12,28},{16,0},{20,4},{24,8},{28,12},{1,17},{... | collective-permute-start | bytes 393224 | tf_op jit(solution)/shard_map/cond/branch_1_fun/ppermute | solution.py:448
  53.4 7.1 %collective-permute-start.5 = (bf16[16,4096]{1,0:T(8,128)(2,1)S(1)}, bf16[16,4096]{1,0:T(8,128)(2,1)S(1)}, u32[]{:S(2)}, u32[]{:S(2)}) collective-permute-start(bf16[16,4096]{1,0:T(8,128)(2,1)S(1)} %get-tuple-element.135), channel_id=1, source_target_pairs={{0,8},{4,12},{8,0},{12,4},{16,24},{20,28},{24,16},{28,20},{1,9},{5... | collective-permute-start | bytes 393224 | tf_op jit(solution)/shard_map/cond/branch_1_fun/ppermute | solution.py:448
  60.6 16.5 %copy-start.1 = (bf16[64,4096]{1,0:T(8,128)(2,1)}, bf16[64,4096]{1,0:T(8,128)(2,1)S(1)}, u32[]{:S(2)}) copy-start(bf16[64,4096]{1,0:T(8,128)(2,1)S(1)} %get-tuple-element.113.args_1_) | copy-start | bytes 1572868
  60.6 11.0 %collective-permute-start.13 = (bf16[16,4096]{1,0:T(8,128)(2,1)S(1)}, bf16[16,4096]{1,0:T(8,128)(2,1)S(1)}, u32[]{:S(2)}, u32[]{:S(2)}) collective-permute-start(bf16[16,4096]{1,0:T(8,128)(2,1)S(1)} %get-tuple-element.125), channel_id=1, source_target_pairs={{0,1},{1,0},{2,3},{3,2},{4,5},{5,4},{6,7},{7,6},{8,9},{9,8},{10,11... | collective-permute-start | bytes 393224 | tf_op jit(solution)/shard_map/ppermute | solution.py:448
  71.6 14.2 %collective-permute-start.19 = (bf16[32,4096]{1,0:T(8,128)(2,1)S(1)}, bf16[32,4096]{1,0:T(8,128)(2,1)S(1)}, u32[]{:S(2)}, u32[]{:S(2)}) collective-permute-start(bf16[32,4096]{1,0:T(8,128)(2,1)S(1)} %pad_maximum_fusion.1), channel_id=1, source_target_pairs={{0,2},{1,3},{2,0},{3,1},{4,6},{5,7},{6,4},{7,5},{8,10},{9,11},{10,... | collective-permute-start | bytes 786440 | tf_op jit(solution)/shard_map/ppermute | solution.py:448
  77.0 1.9 %copy-start.2 = (bf16[64,4096]{1,0:T(8,128)(2,1)S(1)}, bf16[64,4096]{1,0:T(8,128)(2,1)}, u32[]{:S(2)}) copy-start(bf16[64,4096]{1,0:T(8,128)(2,1)} %copy-done.1) | copy-start | bytes 1572868
  79.2 9.5 %collective-permute-start.18 = (bf16[8,64,128]{2,1,0:T(8,128)(2,1)S(1)}, bf16[8,64,128]{2,1,0:T(8,128)(2,1)S(1)}, u32[]{:S(2)}, u32[]{:S(2)}) collective-permute-start(bf16[8,64,128]{2,1,0:T(8,128)(2,1)S(1)} %get-tuple-element.124), channel_id=1, source_target_pairs={{1,0},{2,3},{5,4},{6,7},{9,8},{10,11},{13,12},{14,15},{17,16},{18,... | collective-permute-start | bytes 393224 | tf_op jit(solution)/shard_map/ppermute | solution.py:533
  80.5 10.9 %collective-permute-start.17 = (bf16[8,64,128]{2,1,0:T(8,128)(2,1)S(1)}, bf16[8,64,128]{2,1,0:T(8,128)(2,1)S(1)}, u32[]{:S(2)}, u32[]{:S(2)}) collective-permute-start(bf16[8,64,128]{2,1,0:T(8,128)(2,1)S(1)} %get-tuple-element.123), channel_id=1, source_target_pairs={{1,0},{2,3},{5,4},{6,7},{9,8},{10,11},{13,12},{14,15},{17,16},{18,... | collective-permute-start | bytes 393224 | tf_op jit(solution)/shard_map/ppermute | solution.py:533
  81.8 12.4 %collective-permute-start.16 = (bf16[16,64,128]{2,1,0:T(8,128)(2,1)S(1)}, bf16[16,64,128]{2,1,0:T(8,128)(2,1)S(1)}, u32[]{:S(2)}, u32[]{:S(2)}) collective-permute-start(bf16[16,64,128]{2,1,0:T(8,128)(2,1)S(1)} %get-tuple-element.122), channel_id=1, source_target_pairs={{1,0},{2,3},{5,4},{6,7},{9,8},{10,11},{13,12},{14,15},{17,16},{18,... | collective-permute-start | bytes 786440 | tf_op jit(solution)/shard_map/ppermute | solution.py:533

commit v5 on v4

--- a/solution.py
+++ b/solution.py
@@ -83,7 +83,7 @@
 def route(n_type, types, mask_row, tokens):
     rows, width = tokens.shape
     wide = width + LANES
-    chunk, count = columns(width)
+    chunk, count = width // 2, 2
     return pl.pallas_call(
         functools.partial(route_kernel, n_type),
         grid=(count,),
@@ -311,7 +311,7 @@
             state_ref[head, 8:] = jnp.broadcast_to(top[:, mine], (8, tile))
 
 
-PER_STEP = 8
+PER_STEP = 16
 
 
 def weigh_begin(n_type, info, query, query_id, keys, tile_ids):
@@ -376,7 +376,7 @@
             out_refs[q][head] = weights[:, q * tile : (q + 1) * tile].astype(jnp.bfloat16)
 
 
-def weigh_end(n_type, info, kept, last_key, queries, states, tile_ids, first_head, heads):
+def weigh_end(n_type, info, kept, last_key, queries, states, tile_ids, first_head, heads, weight=0):
     tile = last_key.shape[0]
     n_query = len(queries)
     slots = n_type * EXP_CAP
@@ -394,7 +394,7 @@
         out_specs=[out_block] * n_query,
         scratch_shapes=[pltpu.VMEM((slots, n_query * tile), jnp.float32)],
         compiler_params=params(16, dimension_semantics=("arbitrary",)),
-        cost_estimate=cost(0, 0),
+        cost_estimate=cost(0, weight),
     )(info, kept, last_key, *queries, *states)
 
 
@@ -516,7 +516,7 @@
         twin, guest_state, far = tie((twin, guest_state, far))
         values = spread(jnp.concatenate([expert_rows, twin], axis=0), 2)
         own_weights, back_weights = [], []
-        ends = [0, heads // 2, heads - 8, heads]
+        ends = [0, heads // 2, heads]
         for first, last in zip(ends[:-1], ends[1:]):
             own, theirs = weigh_end(
                 n_type,
@@ -528,6 +528,7 @@
                 [0, 1, 3, 2],
                 first,
                 last - first,
+                (1 << 30) if first > 0 else 0,
             )
             own_weights.append(own)
             back_weights.append(lax.ppermute(theirs, "type", to_end))

time: 96.5 us -> 95.2 us (0.987)
  waiting for transfers between devices: 34.5 us -> 37.3 us
  Pallas kernels: 23 us -> 20.5 us
  starting transfers between devices: 37.4 us -> 36 us
    ppermute x13, waiting for transfers between devices: 22.2 us -> 25.1 us  [swap(): return lax.ppermute(x, axis, [(i, i ^ s) for i in range(size)])]
    pallas_call x2, Pallas kernels: 5.17 us -> 3.81 us  [weigh_begin(): pl.pallas_call(functools.partial(in_middle, weigh_begin_body, n_type, til...]
    ppermute x3 -> x2, starting transfers between devices: 3.88 us -> 2.57 us  [on_device(): back_weights.append(lax.ppermute(theirs, 'type', to_end))]
    pallas_call x1, Pallas kernels: 2.7 us -> 1.7 us  [route(): pl.pallas_call(functools.partial(route_kernel, n_type), grid=(count,), ou...]
    pallas_call x3 -> x2, Pallas kernels: 2.12 us -> 1.91 us  [weigh_end(): pl.pallas_call(functools.partial(in_middle, weigh_end_body, n_type, tile_...]
    ppermute x3 -> x2, waiting for transfers between devices: 8.38 us -> 8.28 us  [on_device(): back_weights.append(lax.ppermute(theirs, 'type', to_end))]
  transfers between devices with their start and end apart: 20 -> 19, of which waited for: 13 -> 12; matrix products, arithmetic and copies ran while one was open for 0% -> 0% of each run, Pallas kernels for 19% -> 18%
where the time goes in v5:
time: 95.2 us; the launch traced here: 94.9 us
  waiting for transfers between devices  37.3 us (39%)
  starting transfers between devices  36 us (38%)
  Pallas kernels  20.5 us (22%)
    ppermute x13, waiting for transfers between devices, swap(): return lax.ppermute(x, axis, [(i, i ^ s) for i in range(size)])  25.1 us
    ppermute x13, starting transfers between devices, swap(): return lax.ppermute(x, axis, [(i, i ^ s) for i in range(size)])  23.9 us
    ppermute x2, waiting for transfers between devices, on_device(): back_weights.append(lax.ppermute(theirs, 'type', to_end))  8.28 us
    pallas_call x1, Pallas kernels, fetch(): pl.pallas_call(functools.partial(fetch_kernel, count), out_shape=[pltpu.V...  7.28 us
    ppermute x1, starting transfers between devices, on_device(): near = lax.ppermute(keys, 'type', to_middle)  4.92 us
    ppermute x1, waiting for transfers between devices, on_device(): guest = lax.ppermute(queries, 'type', to_middle)  3.89 us
    pallas_call x2, Pallas kernels, weigh_begin(): pl.pallas_call(functools.partial(in_middle, weigh_begin_body, n_type, til...  3.81 us
    pallas_call x1, Pallas kernels, ffn(): pl.pallas_call(ffn_kernel, out_shape=[jax.ShapeDtypeStruct((half, width),...  3.58 us
  transfers between devices with their start and end apart: 19, of which 12 were waited for; matrix products, arithmetic and copies ran while one was open for 0% of the time, Pallas kernels for 18%

profile of v5, /device:TPU:0, one launch (start us, length us, event | category | flops | bytes accessed | tf_op | source)
XLA Modules:
  0.0 94.9 jit_solution(9914085419988034884)
XLA Ops:
  0.6 1.7 %shard_map.98 = (bf16[16,4224]{1,0:T(8,128)(2,1)S(1)}, bf16[16,4224]{1,0:T(8,128)(2,1)S(1)}, bf16[16,4224]{1,0:T(8,128)(2,1)S(1)}, bf16[16,4224]{1,0:T(8,128)(2,1)S(1)}) custom-call(s32[1,128]{1,0:T(1,128)} %bitcast.8, s32[1,4]{1,0:T(1,128)} %bitcast.9, bf16[128,4096]{1,0:T(8,128)(2,1)} %tokens_ref.1), custom_call_target="tpu_custom_call" | custom-call | tf_op jit(solution)/shard_map/pallas_call | solution.py:87
  2.3 3.1 %collective-permute-start.8 = (bf16[16,4224]{1,0:T(8,128)(2,1)S(1)}, bf16[16,4224]{1,0:T(8,128)(2,1)S(1)}, u32[]{:S(2)}, u32[]{:S(2)}) collective-permute-start(bf16[16,4224]{1,0:T(8,128)(2,1)S(1)} %get-tuple-element.97), channel_id=1, source_target_pairs={{0,1},{1,0},{2,3},{3,2},{4,5},{5,4},{6,7},{7,6},{8,9},{9,8},{10,11... | collective-permute-start | bytes 405512 | tf_op jit(solution)/shard_map/ppermute | solution.py:448
  5.4 2.6 %collective-permute-start.9 = (bf16[16,4224]{1,0:T(8,128)(2,1)S(1)}, bf16[16,4224]{1,0:T(8,128)(2,1)S(1)}, u32[]{:S(2)}, u32[]{:S(2)}) collective-permute-start(bf16[16,4224]{1,0:T(8,128)(2,1)S(1)} %get-tuple-element.98), channel_id=1, source_target_pairs={{0,2},{1,3},{2,0},{3,1},{4,6},{5,7},{6,4},{7,5},{8,10},{9,11},{10,... | collective-permute-start | bytes 405512 | tf_op jit(solution)/shard_map/ppermute | solution.py:448
  8.0 0.0 collective-permute-start.10
  8.0 2.6 %collective-permute-done.8 = bf16[16,4224]{1,0:T(8,128)(2,1)S(1)} collective-permute-done((bf16[16,4224]{1,0:T(8,128)(2,1)S(1)}, bf16[16,4224]{1,0:T(8,128)(2,1)S(1)}, u32[]{:S(2)}, u32[]{:S(2)}) %collective-permute-start.8) | collective-permute-done | bytes 135200 | tf_op jit(solution)/shard_map/ppermute | solution.py:448
  10.7 8.0 %collective-permute-done.9 = bf16[16,4224]{1,0:T(8,128)(2,1)S(1)} collective-permute-done((bf16[16,4224]{1,0:T(8,128)(2,1)S(1)}, bf16[16,4224]{1,0:T(8,128)(2,1)S(1)}, u32[]{:S(2)}, u32[]{:S(2)}) %collective-permute-start.9) | collective-permute-done | bytes 135200 | tf_op jit(solution)/shard_map/ppermute | solution.py:448
  18.6 0.0 collective-permute-done.10
  18.6 4.9 %collective-permute-start.11 = (bf16[128,4096]{1,0:T(8,128)(2,1)}, bf16[128,4096]{1,0:T(8,128)(2,1)}, u32[]{:S(2)}, u32[]{:S(2)}) collective-permute-start(bf16[128,4096]{1,0:T(8,128)(2,1)} %args_2_), channel_id=1, source_target_pairs={{0,1},{3,2},{4,5},{7,6},{8,9},{11,10},{12,13},{15,14},{16,17},{19,... | collective-permute-start | bytes 3145736 | tf_op jit(solution)/shard_map/ppermute | solution.py:503
  23.6 1.6 %collective-permute-start.12 = (bf16[128,4096]{1,0:T(8,128)(2,1)}, bf16[128,4096]{1,0:T(8,128)(2,1)}, u32[]{:S(2)}, u32[]{:S(2)}) collective-permute-start(bf16[128,4096]{1,0:T(8,128)(2,1)} %args_2_), channel_id=1, source_target_pairs={{1,2},{2,1},{5,6},{6,5},{9,10},{10,9},{13,14},{14,13},{17,18},{18,... | collective-permute-start | bytes 3145736 | tf_op jit(solution)/shard_map/ppermute | solution.py:504
  25.2 2.2 %collective-permute-start.14 = (bf16[128,4096]{1,0:T(8,128)(2,1)}, bf16[128,4096]{1,0:T(8,128)(2,1)S(1)}, u32[]{:S(2)}, u32[]{:S(2)}) collective-permute-start(bf16[128,4096]{1,0:T(8,128)(2,1)} %args_3_.4), channel_id=1, source_target_pairs={{0,1},{3,2},{4,5},{7,6},{8,9},{11,10},{12,13},{15,14},{16,17},{19,... | collective-permute-start | bytes 3145736 | tf_op jit(solution)/shard_map/ppermute | solution.py:505
  27.4 0.0 copy-start
  27.4 19.9 %conditional.2 = (f32[12,128]{1,0:T(8,128)S(1)}, f32[64,4096]{1,0:T(8,128)S(1)}, bf16[64,4096]{1,0:T(8,128)(2,1)S(1)}) conditional(s32[]{:T(128)} %convert_element_type.25, () %tuple.29, (bf16[16,4224]{1,0:T(8,128)(2,1)S(1)}, bf16[16,4224]{1,0:T(8,128)(2,1)S(1)}, bf16[16,4224]{1,0:T(8,128)(2,1)S(1)}, bf16[16,4224]{1,0:T(8,128)(2,1)S(1)}, ...), branch_computations={%region_0.0_spmd, %region_1.0_spmd} | conditional | bytes 48758968 | solution.py:454
  27.5 0.4 branch_1_fun.4
  27.9 1.6 %collective-permute-start.1 = (bf16[16,4096]{1,0:T(8,128)(2,1)S(1)}, bf16[16,4096]{1,0:T(8,128)(2,1)S(1)}, u32[]{:S(2)}, u32[]{:S(2)}) collective-permute-start(bf16[16,4096]{1,0:T(8,128)(2,1)S(1)} %get-tuple-element.43), channel_id=1, source_target_pairs={{0,16},{4,20},{8,24},{12,28},{16,0},{20,4},{24,8},{28,12},{1,17},{... | collective-permute-start | bytes 393224 | tf_op jit(solution)/shard_map/cond/branch_1_fun/ppermute | solution.py:448
  29.4 1.5 %collective-permute-start = (bf16[16,4096]{1,0:T(8,128)(2,1)S(1)}, bf16[16,4096]{1,0:T(8,128)(2,1)S(1)}, u32[]{:S(2)}, u32[]{:S(2)}) collective-permute-start(bf16[16,4096]{1,0:T(8,128)(2,1)S(1)} %get-tuple-element.43), channel_id=1, source_target_pairs={{0,8},{4,12},{8,0},{12,4},{16,24},{20,28},{24,16},{28,20},{1,9},{5... | collective-permute-start | bytes 393224 | tf_op jit(solution)/shard_map/cond/branch_1_fun/ppermute | solution.py:448
  30.9 2.0 %collective-permute-done.1 = bf16[16,4096]{1,0:T(8,128)(2,1)S(1)} collective-permute-done((bf16[16,4096]{1,0:T(8,128)(2,1)S(1)}, bf16[16,4096]{1,0:T(8,128)(2,1)S(1)}, u32[]{:S(2)}, u32[]{:S(2)}) %collective-permute-start.1) | collective-permute-done | bytes 131104 | tf_op jit(solution)/shard_map/cond/branch_1_fun/ppermute | solution.py:448
  32.9 1.5 %collective-permute-start.2 = (bf16[16,4096]{1,0:T(8,128)(2,1)S(1)}, bf16[16,4096]{1,0:T(8,128)(2,1)S(1)}, u32[]{:S(2)}, u32[]{:S(2)}) collective-permute-start(bf16[16,4096]{1,0:T(8,128)(2,1)S(1)} %collective-permute-done.1), channel_id=1, source_target_pairs={{0,8},{4,12},{8,0},{12,4},{16,24},{20,28},{24,16},{28,20},{1,9},{5... | collective-permute-start | bytes 393224 | tf_op jit(solution)/shard_map/cond/branch_1_fun/ppermute | solution.py:448
  34.4 7.3 %branch_1_fun.5 = (bf16[4096,896]{1,0:T(8,128)(2,1)S(1)}, bf16[4096,896]{1,0:T(8,128)(2,1)S(1)}, bf16[896,4096]{1,0:T(8,128)(2,1)S(1)}) custom-call(bf16[4096,896]{1,0:T(8,128)(2,1)} %bitcast.5, bf16[4096,896]{1,0:T(8,128)(2,1)} %bitcast.6, bf16[896,4096]{1,0:T(8,128)(2,1)} %bitcast.7), custom_call_target="tpu_custom_call" | custom-call | bytes 44040192 | tf_op jit(solution)/shard_map/cond/branch_1_fun/pallas_call | solution.py:114
  41.7 0.0 collective-permute-done
  41.8 0.1 collective-permute-start.3
  41.9 1.9 %collective-permute-done.3.far_ref = bf16[64,4096]{1,0:T(8,128)(2,1)S(1)} collective-permute-done((bf16[64,4096]{1,0:T(8,128)(2,1)S(1)}, bf16[64,4096]{1,0:T(8,128)(2,1)S(1)}, u32[]{:S(2)}, u32[]{:S(2)}) %collective-permute-start.3) | collective-permute-done | bytes 524320 | tf_op jit(solution)/shard_map/cond/branch_1_fun/ppermute | solution.py:448
  43.8 3.6 %branch_1_fun.6 = (f32[64,4096]{1,0:T(8,128)S(1)}, bf16[64,4096]{1,0:T(8,128)(2,1)S(1)}) custom-call(bf16[64,4096]{1,0:T(8,128)(2,1)S(1)} %constant_dynamic-update-slice_fusion.near_ref, bf16[64,4096]{1,0:T(8,128)(2,1)S(1)} %collective-permute-done.3.far_ref, bf16[4096,896]{1,0:T(8,128)(2,1)S(1)} %get-tuple-element.47.gate_ref, ...), custom_call_target="tpu_custom_call" | custom-call | tf_op jit(solution)/shard_map/cond/branch_1_fun/pallas_call | solution.py:216
  47.4 0.7 collective-permute-start.15
  48.1 11.6 %conditional.3 = (bf16[16,4096]{1,0:T(8,128)(2,1)S(1)}, f32[32,16,128]{2,1,0:T(8,128)S(1)}, bf16[64,4096]{1,0:T(8,128)(2,1)S(1)}) conditional(s32[]{:T(128)} %convert_element_type.25, () %tuple.32, (bf16[64,4096]{1,0:T(8,128)(2,1)S(1)}, f32[64,4096]{1,0:T(8,128)S(1)}, f32[12,128]{1,0:T(8,128)S(1)}, bf16[128,4096]{1,0:T(8,128)(2,1)S(1)}, ...), branch_computations={%region_2.0_spmd, %region_3.0_spmd} | conditional | flops 1310720 | bytes 15859896 | solution.py:454
  48.1 0.2 collective-permute-start.4
  48.3 1.8 %collective-permute-done.4 = bf16[64,4096]{1,0:T(8,128)(2,1)S(1)} collective-permute-done((bf16[64,4096]{1,0:T(8,128)(2,1)S(1)}, bf16[64,4096]{1,0:T(8,128)(2,1)S(1)}, u32[]{:S(2)}, u32[]{:S(2)}) %collective-permute-start.4) | collective-permute-done | bytes 524320 | tf_op jit(solution)/shard_map/cond/branch_1_fun/ppermute | solution.py:448
  50.1 0.1 add_convert_fusion
  50.2 1.6 %collective-permute-start.7 = (bf16[16,4096]{1,0:T(8,128)(2,1)S(1)}, bf16[16,4096]{1,0:T(8,128)(2,1)S(1)}, u32[]{:S(2)}, u32[]{:S(2)}) collective-permute-start(bf16[16,4096]{1,0:T(8,128)(2,1)S(1)} %get-tuple-element.129), channel_id=1, source_target_pairs={{0,24},{4,28},{8,16},{12,20},{16,8},{20,12},{24,0},{28,4},{1,25},{... | collective-permute-start | bytes 393224 | tf_op jit(solution)/shard_map/cond/branch_1_fun/ppermute | solution.py:448
  51.9 0.5 collective-permute-start.6
  52.4 1.4 %collective-permute-start.5 = (bf16[16,4096]{1,0:T(8,128)(2,1)S(1)}, bf16[16,4096]{1,0:T(8,128)(2,1)S(1)}, u32[]{:S(2)}, u32[]{:S(2)}) collective-permute-start(bf16[16,4096]{1,0:T(8,128)(2,1)S(1)} %get-tuple-element.131), channel_id=1, source_target_pairs={{0,8},{4,12},{8,0},{12,4},{16,24},{20,28},{24,16},{28,20},{1,9},{5... | collective-permute-start | bytes 393224 | tf_op jit(solution)/shard_map/cond/branch_1_fun/ppermute | solution.py:448
  53.8 1.9 %branch_1_fun.7 = (f32[32,16,128]{2,1,0:T(8,128)S(1)}, bf16[64,4096]{1,0:T(8,128)(2,1)S(1)}) custom-call(f32[12,128]{1,0:T(8,128)S(1)} %get-tuple-element.54.args_0_, bf16[128,4096]{1,0:T(8,128)(2,1)S(1)} %get-tuple-element.55.args_1_, bf16[128,4096]{1,0:T(8,128)(2,1)} %get-tuple-element.56.args_2_, bf16[128,4096]{1,0:T(8,128)(2,1)} %get-tuple-element.57.args_3_, ...), custom_call_target="tpu_custom_call" | custom-call | bytes 8388608 | tf_op jit(solution)/shard_map/cond/branch_1_fun/pallas_call | solution.py:322
  55.7 1.8 %collective-permute-done.7 = bf16[16,4096]{1,0:T(8,128)(2,1)S(1)} collective-permute-done((bf16[16,4096]{1,0:T(8,128)(2,1)S(1)}, bf16[16,4096]{1,0:T(8,128)(2,1)S(1)}, u32[]{:S(2)}, u32[]{:S(2)}) %collective-permute-start.7) | collective-permute-done | bytes 131104 | tf_op jit(solution)/shard_map/cond/branch_1_fun/ppermute | solution.py:448
  57.6 2.0 %collective-permute-done.6 = bf16[16,4096]{1,0:T(8,128)(2,1)S(1)} collective-permute-done((bf16[16,4096]{1,0:T(8,128)(2,1)S(1)}, bf16[16,4096]{1,0:T(8,128)(2,1)S(1)}, u32[]{:S(2)}, u32[]{:S(2)}) %collective-permute-start.6) | collective-permute-done | bytes 131104 | tf_op jit(solution)/shard_map/cond/branch_1_fun/ppermute | solution.py:448
  59.5 0.1 collective-permute-done.5
  59.7 0.1 add_convert_fusion.1
  59.7 0.0 copy-start.1
  59.7 4.4 %collective-permute-start.13 = (bf16[16,4096]{1,0:T(8,128)(2,1)S(1)}, bf16[16,4096]{1,0:T(8,128)(2,1)S(1)}, u32[]{:S(2)}, u32[]{:S(2)}) collective-permute-start(bf16[16,4096]{1,0:T(8,128)(2,1)S(1)} %get-tuple-element.121), channel_id=1, source_target_pairs={{0,1},{1,0},{2,3},{3,2},{4,5},{5,4},{6,7},{7,6},{8,9},{9,8},{10,11... | collective-permute-start | bytes 393224 | tf_op jit(solution)/shard_map/ppermute | solution.py:448
  64.1 3.9 %collective-permute-done.14.args_1_.args_4_ = bf16[128,4096]{1,0:T(8,128)(2,1)S(1)} collective-permute-done((bf16[128,4096]{1,0:T(8,128)(2,1)}, bf16[128,4096]{1,0:T(8,128)(2,1)S(1)}, u32[]{:S(2)}, u32[]{:S(2)}) %collective-permute-start.14) | collective-permute-done | bytes 1048608 | tf_op jit(solution)/shard_map/ppermute | solution.py:505
  68.0 1.9 %shard_map.99.args_6_ = f32[32,16,128]{2,1,0:T(8,128)S(1)} custom-call(f32[12,128]{1,0:T(8,128)S(1)} %get-tuple-element.104.args_0_.info_ref, bf16[128,4096]{1,0:T(8,128)(2,1)S(1)} %collective-permute-done.14.args_1_.args_4_, bf16[128,4096]{1,0:T(8,128)(2,1)} %args_2_, bf16[128,4096]{1,0:T(8,128)(2,1)} %collective-permute-done.11.args_3_, ...), custom_call_target="tpu_custom_call" | custom-call | bytes 8388608 | tf_op jit(solution)/shard_map/pallas_call | solution.py:322
  69.9 5.4 %collective-permute-start.18 = (bf16[32,4096]{1,0:T(8,128)(2,1)S(1)}, bf16[32,4096]{1,0:T(8,128)(2,1)S(1)}, u32[]{:S(2)}, u32[]{:S(2)}) collective-permute-start(bf16[32,4096]{1,0:T(8,128)(2,1)S(1)} %pad_maximum_fusion.1), channel_id=1, source_target_pairs={{0,2},{1,3},{2,0},{3,1},{4,6},{5,7},{6,4},{7,5},{8,10},{9,11},{10,... | collective-permute-start | bytes 786440 | tf_op jit(solution)/shard_map/ppermute | solution.py:448
  75.4 1.0 %shard_map.101 = (bf16[16,64,128]{2,1,0:T(8,128)(2,1)S(1)}, bf16[16,64,128]{2,1,0:T(8,128)(2,1)S(1)}) custom-call(f32[12,128]{1,0:T(8,128)S(1)} %get-tuple-element.104.args_0_.info_ref, bf16[64,4096]{1,0:T(8,128)(2,1)} %copy-done.1, bf16[128,4096]{1,0:T(8,128)(2,1)S(1)} %collective-permute-done.15.args_2_, bf16[128,4096]{1,0:T(8,128)(2,1)S(1)} %copy-done, ...), custom_call_target="tpu_custom_call" | custom-call | bytes 1073741824 | tf_op jit(solution)/shard_map/pallas_call | solution.py:387
  76.3 1.0 %shard_map.100 = (bf16[16,64,128]{2,1,0:T(8,128)(2,1)S(1)}, bf16[16,64,128]{2,1,0:T(8,128)(2,1)S(1)}) custom-call(f32[12,128]{1,0:T(8,128)S(1)} %get-tuple-element.104.args_0_.info_ref, bf16[64,4096]{1,0:T(8,128)(2,1)} %copy-done.1, bf16[128,4096]{1,0:T(8,128)(2,1)S(1)} %collective-permute-done.15.args_2_, bf16[128,4096]{1,0:T(8,128)(2,1)S(1)} %copy-done, ...), custom_call_target="tpu_custom_call" | custom-call | tf_op jit(solution)/shard_map/pallas_call | solution.py:387
  77.3 1.3 %collective-permute-start.17 = (bf16[16,64,128]{2,1,0:T(8,128)(2,1)S(1)}, bf16[16,64,128]{2,1,0:T(8,128)(2,1)S(1)}, u32[]{:S(2)}, u32[]{:S(2)}) collective-permute-start(bf16[16,64,128]{2,1,0:T(8,128)(2,1)S(1)} %get-tuple-element.120), channel_id=1, source_target_pairs={{1,0},{2,3},{5,4},{6,7},{9,8},{10,11},{13,12},{14,15},{17,16},{18,... | collective-permute-start | bytes 786440 | tf_op jit(solution)/shard_map/ppermute | solution.py:534
  78.6 1.3 %collective-permute-start.16 = (bf16[16,64,128]{2,1,0:T(8,128)(2,1)S(1)}, bf16[16,64,128]{2,1,0:T(8,128)(2,1)S(1)}, u32[]{:S(2)}, u32[]{:S(2)}) collective-permute-start(bf16[16,64,128]{2,1,0:T(8,128)(2,1)S(1)} %get-tuple-element.119), channel_id=1, source_target_pairs={{1,0},{2,3},{5,4},{6,7},{9,8},{10,11},{13,12},{14,15},{17,16},{18,... | collective-permute-start | bytes 786440 | tf_op jit(solution)/shard_map/ppermute | solution.py:534
  79.9 4.9 %collective-permute-done.18 = bf16[32,4096]{1,0:T(8,128)(2,1)S(1)} collective-permute-done((bf16[32,4096]{1,0:T(8,128)(2,1)S(1)}, bf16[32,4096]{1,0:T(8,128)(2,1)S(1)}, u32[]{:S(2)}, u32[]{:S(2)}) %collective-permute-start.18) | collective-permute-done | bytes 262176 | tf_op jit(solution)/shard_map/ppermute | solution.py:448
  84.8 5.5 %collective-permute-done.17.refs_3_ = bf16[16,64,128]{2,1,0:T(8,128)(2,1)S(1)} collective-permute-done((bf16[16,64,128]{2,1,0:T(8,128)(2,1)S(1)}, bf16[16,64,128]{2,1,0:T(8,128)(2,1)S(1)}, u32[]{:S(2)}, u32[]{:S(2)}) %collective-permute-start.17) | collective-permute-done | bytes 262176 | tf_op jit(solution)/shard_map/ppermute | solution.py:534
  90.3 2.8 %collective-permute-done.16.refs_2_ = bf16[16,64,128]{2,1,0:T(8,128)(2,1)S(1)} collective-permute-done((bf16[16,64,128]{2,1,0:T(8,128)(2,1)S(1)}, bf16[16,64,128]{2,1,0:T(8,128)(2,1)S(1)}, u32[]{:S(2)}, u32[]{:S(2)}) %collective-permute-start.16) | collective-permute-done | bytes 262176 | tf_op jit(solution)/shard_map/ppermute | solution.py:534
  93.1 1.8 %shard_map.102 = (bf16[128,4096]{1,0:T(8,128)(2,1)}, bf16[128,4096]{1,0:T(8,128)(2,1)}) custom-call(f32[12,128]{1,0:T(8,128)S(1)} %get-tuple-element.104.args_0_.info_ref, bf16[16,64,128]{2,1,0:T(8,128)(2,1)S(1)} %get-tuple-element.117.refs_0_, bf16[16,64,128]{2,1,0:T(8,128)(2,1)S(1)} %get-tuple-element.118.refs_1_, ...), custom_call_target="tpu_custom_call" | custom-call | tf_op jit(solution)/shard_map/pallas_call | solution.py:436
  (14 shorter events, 0.2 us)
Async XLA Ops:
  2.3 8.3 %collective-permute-start.8 = (bf16[16,4224]{1,0:T(8,128)(2,1)S(1)}, bf16[16,4224]{1,0:T(8,128)(2,1)S(1)}, u32[]{:S(2)}, u32[]{:S(2)}) collective-permute-start(bf16[16,4224]{1,0:T(8,128)(2,1)S(1)} %get-tuple-element.97), channel_id=1, source_target_pairs={{0,1},{1,0},{2,3},{3,2},{4,5},{5,4},{6,7},{7,6},{8,9},{9,8},{10,11... | collective-permute-start | bytes 405512 | tf_op jit(solution)/shard_map/ppermute | solution.py:448
  5.4 13.2 %collective-permute-start.9 = (bf16[16,4224]{1,0:T(8,128)(2,1)S(1)}, bf16[16,4224]{1,0:T(8,128)(2,1)S(1)}, u32[]{:S(2)}, u32[]{:S(2)}) collective-permute-start(bf16[16,4224]{1,0:T(8,128)(2,1)S(1)} %get-tuple-element.98), channel_id=1, source_target_pairs={{0,2},{1,3},{2,0},{3,1},{4,6},{5,7},{6,4},{7,5},{8,10},{9,11},{10,... | collective-permute-start | bytes 405512 | tf_op jit(solution)/shard_map/ppermute | solution.py:448
  8.0 10.6 %collective-permute-start.10 = (bf16[16,4224]{1,0:T(8,128)(2,1)S(1)}, bf16[16,4224]{1,0:T(8,128)(2,1)S(1)}, u32[]{:S(2)}, u32[]{:S(2)}) collective-permute-start(bf16[16,4224]{1,0:T(8,128)(2,1)S(1)} %get-tuple-element.99), channel_id=1, source_target_pairs={{0,3},{1,2},{2,1},{3,0},{4,7},{5,6},{6,5},{7,4},{8,11},{9,10},{10,... | collective-permute-start | bytes 405512 | tf_op jit(solution)/shard_map/ppermute | solution.py:448
  18.6 28.7 %collective-permute-start.11 = (bf16[128,4096]{1,0:T(8,128)(2,1)}, bf16[128,4096]{1,0:T(8,128)(2,1)}, u32[]{:S(2)}, u32[]{:S(2)}) collective-permute-start(bf16[128,4096]{1,0:T(8,128)(2,1)} %args_2_), channel_id=1, source_target_pairs={{0,1},{3,2},{4,5},{7,6},{8,9},{11,10},{12,13},{15,14},{16,17},{19,... | collective-permute-start | bytes 3145736 | tf_op jit(solution)/shard_map/ppermute | solution.py:503
  23.6 24.5 %collective-permute-start.12 = (bf16[128,4096]{1,0:T(8,128)(2,1)}, bf16[128,4096]{1,0:T(8,128)(2,1)}, u32[]{:S(2)}, u32[]{:S(2)}) collective-permute-start(bf16[128,4096]{1,0:T(8,128)(2,1)} %args_2_), channel_id=1, source_target_pairs={{1,2},{2,1},{5,6},{6,5},{9,10},{10,9},{13,14},{14,13},{17,18},{18,... | collective-permute-start | bytes 3145736 | tf_op jit(solution)/shard_map/ppermute | solution.py:504
  25.2 42.8 %collective-permute-start.14 = (bf16[128,4096]{1,0:T(8,128)(2,1)}, bf16[128,4096]{1,0:T(8,128)(2,1)S(1)}, u32[]{:S(2)}, u32[]{:S(2)}) collective-permute-start(bf16[128,4096]{1,0:T(8,128)(2,1)} %args_3_.4), channel_id=1, source_target_pairs={{0,1},{3,2},{4,5},{7,6},{8,9},{11,10},{12,13},{15,14},{16,17},{19,... | collective-permute-start | bytes 3145736 | tf_op jit(solution)/shard_map/ppermute | solution.py:505
  27.4 20.7 %copy-start = (bf16[128,4096]{1,0:T(8,128)(2,1)S(1)}, bf16[128,4096]{1,0:T(8,128)(2,1)}, u32[]{:S(2)}) copy-start(bf16[128,4096]{1,0:T(8,128)(2,1)} %args_3_.4) | copy-start | bytes 3145732
  27.9 5.0 %collective-permute-start.1 = (bf16[16,4096]{1,0:T(8,128)(2,1)S(1)}, bf16[16,4096]{1,0:T(8,128)(2,1)S(1)}, u32[]{:S(2)}, u32[]{:S(2)}) collective-permute-start(bf16[16,4096]{1,0:T(8,128)(2,1)S(1)} %get-tuple-element.43), channel_id=1, source_target_pairs={{0,16},{4,20},{8,24},{12,28},{16,0},{20,4},{24,8},{28,12},{1,17},{... | collective-permute-start | bytes 393224 | tf_op jit(solution)/shard_map/cond/branch_1_fun/ppermute | solution.py:448
  29.4 12.2 %collective-permute-start = (bf16[16,4096]{1,0:T(8,128)(2,1)S(1)}, bf16[16,4096]{1,0:T(8,128)(2,1)S(1)}, u32[]{:S(2)}, u32[]{:S(2)}) collective-permute-start(bf16[16,4096]{1,0:T(8,128)(2,1)S(1)} %get-tuple-element.43), channel_id=1, source_target_pairs={{0,8},{4,12},{8,0},{12,4},{16,24},{20,28},{24,16},{28,20},{1,9},{5... | collective-permute-start | bytes 393224 | tf_op jit(solution)/shard_map/cond/branch_1_fun/ppermute | solution.py:448
  32.9 8.8 %collective-permute-start.2 = (bf16[16,4096]{1,0:T(8,128)(2,1)S(1)}, bf16[16,4096]{1,0:T(8,128)(2,1)S(1)}, u32[]{:S(2)}, u32[]{:S(2)}) collective-permute-start(bf16[16,4096]{1,0:T(8,128)(2,1)S(1)} %collective-permute-done.1), channel_id=1, source_target_pairs={{0,8},{4,12},{8,0},{12,4},{16,24},{20,28},{24,16},{28,20},{1,9},{5... | collective-permute-start | bytes 393224 | tf_op jit(solution)/shard_map/cond/branch_1_fun/ppermute | solution.py:448
  41.8 2.0 %collective-permute-start.3 = (bf16[64,4096]{1,0:T(8,128)(2,1)S(1)}, bf16[64,4096]{1,0:T(8,128)(2,1)S(1)}, u32[]{:S(2)}, u32[]{:S(2)}) collective-permute-start(bf16[64,4096]{1,0:T(8,128)(2,1)S(1)} %constant_dynamic-update-slice_fusion.near_ref), channel_id=1, source_target_pairs={{0,4},{4,0},{8,12},{12,8},{16,20},{20,16},{24,28},{28,24},{1,5},{5... | collective-permute-start | bytes 1572872 | tf_op jit(solution)/shard_map/cond/branch_1_fun/ppermute | solution.py:448
  47.4 22.6 %collective-permute-start.15 = (bf16[128,4096]{1,0:T(8,128)(2,1)}, bf16[128,4096]{1,0:T(8,128)(2,1)S(1)}, u32[]{:S(2)}, u32[]{:S(2)}) collective-permute-start(bf16[128,4096]{1,0:T(8,128)(2,1)} %collective-permute-done.11.args_3_), channel_id=1, source_target_pairs={{1,2},{2,1},{5,6},{6,5},{9,10},{10,9},{13,14},{14,13},{17,18},{18,... | collective-permute-start | bytes 3145736 | tf_op jit(solution)/shard_map/ppermute | solution.py:508
  48.1 2.0 %collective-permute-start.4 = (bf16[64,4096]{1,0:T(8,128)(2,1)S(1)}, bf16[64,4096]{1,0:T(8,128)(2,1)S(1)}, u32[]{:S(2)}, u32[]{:S(2)}) collective-permute-start(bf16[64,4096]{1,0:T(8,128)(2,1)S(1)} %get-tuple-element.53), channel_id=1, source_target_pairs={{0,4},{4,0},{8,12},{12,8},{16,20},{20,16},{24,28},{28,24},{1,5},{5... | collective-permute-start | bytes 1572872 | tf_op jit(solution)/shard_map/cond/branch_1_fun/ppermute | solution.py:448
  50.2 7.3 %collective-permute-start.7 = (bf16[16,4096]{1,0:T(8,128)(2,1)S(1)}, bf16[16,4096]{1,0:T(8,128)(2,1)S(1)}, u32[]{:S(2)}, u32[]{:S(2)}) collective-permute-start(bf16[16,4096]{1,0:T(8,128)(2,1)S(1)} %get-tuple-element.129), channel_id=1, source_target_pairs={{0,24},{4,28},{8,16},{12,20},{16,8},{20,12},{24,0},{28,4},{1,25},{... | collective-permute-start | bytes 393224 | tf_op jit(solution)/shard_map/cond/branch_1_fun/ppermute | solution.py:448
  51.9 7.7 %collective-permute-start.6 = (bf16[16,4096]{1,0:T(8,128)(2,1)S(1)}, bf16[16,4096]{1,0:T(8,128)(2,1)S(1)}, u32[]{:S(2)}, u32[]{:S(2)}) collective-permute-start(bf16[16,4096]{1,0:T(8,128)(2,1)S(1)} %get-tuple-element.130), channel_id=1, source_target_pairs={{0,16},{4,20},{8,24},{12,28},{16,0},{20,4},{24,8},{28,12},{1,17},{... | collective-permute-start | bytes 393224 | tf_op jit(solution)/shard_map/cond/branch_1_fun/ppermute | solution.py:448
  52.4 7.3 %collective-permute-start.5 = (bf16[16,4096]{1,0:T(8,128)(2,1)S(1)}, bf16[16,4096]{1,0:T(8,128)(2,1)S(1)}, u32[]{:S(2)}, u32[]{:S(2)}) collective-permute-start(bf16[16,4096]{1,0:T(8,128)(2,1)S(1)} %get-tuple-element.131), channel_id=1, source_target_pairs={{0,8},{4,12},{8,0},{12,4},{16,24},{20,28},{24,16},{28,20},{1,9},{5... | collective-permute-start | bytes 393224 | tf_op jit(solution)/shard_map/cond/branch_1_fun/ppermute | solution.py:448
  59.7 15.6 %copy-start.1 = (bf16[64,4096]{1,0:T(8,128)(2,1)}, bf16[64,4096]{1,0:T(8,128)(2,1)S(1)}, u32[]{:S(2)}) copy-start(bf16[64,4096]{1,0:T(8,128)(2,1)S(1)} %get-tuple-element.111.args_1_) | copy-start | bytes 1572868
  59.7 10.2 %collective-permute-start.13 = (bf16[16,4096]{1,0:T(8,128)(2,1)S(1)}, bf16[16,4096]{1,0:T(8,128)(2,1)S(1)}, u32[]{:S(2)}, u32[]{:S(2)}) collective-permute-start(bf16[16,4096]{1,0:T(8,128)(2,1)S(1)} %get-tuple-element.121), channel_id=1, source_target_pairs={{0,1},{1,0},{2,3},{3,2},{4,5},{5,4},{6,7},{7,6},{8,9},{9,8},{10,11... | collective-permute-start | bytes 393224 | tf_op jit(solution)/shard_map/ppermute | solution.py:448
  69.9 14.8 %collective-permute-start.18 = (bf16[32,4096]{1,0:T(8,128)(2,1)S(1)}, bf16[32,4096]{1,0:T(8,128)(2,1)S(1)}, u32[]{:S(2)}, u32[]{:S(2)}) collective-permute-start(bf16[32,4096]{1,0:T(8,128)(2,1)S(1)} %pad_maximum_fusion.1), channel_id=1, source_target_pairs={{0,2},{1,3},{2,0},{3,1},{4,6},{5,7},{6,4},{7,5},{8,10},{9,11},{10,... | collective-permute-start | bytes 786440 | tf_op jit(solution)/shard_map/ppermute | solution.py:448
  77.3 13.0 %collective-permute-start.17 = (bf16[16,64,128]{2,1,0:T(8,128)(2,1)S(1)}, bf16[16,64,128]{2,1,0:T(8,128)(2,1)S(1)}, u32[]{:S(2)}, u32[]{:S(2)}) collective-permute-start(bf16[16,64,128]{2,1,0:T(8,128)(2,1)S(1)} %get-tuple-element.120), channel_id=1, source_target_pairs={{1,0},{2,3},{5,4},{6,7},{9,8},{10,11},{13,12},{14,15},{17,16},{18,... | collective-permute-start | bytes 786440 | tf_op jit(solution)/shard_map/ppermute | solution.py:534
  78.6 14.5 %collective-permute-start.16 = (bf16[16,64,128]{2,1,0:T(8,128)(2,1)S(1)}, bf16[16,64,128]{2,1,0:T(8,128)(2,1)S(1)}, u32[]{:S(2)}, u32[]{:S(2)}) collective-permute-start(bf16[16,64,128]{2,1,0:T(8,128)(2,1)S(1)} %get-tuple-element.119), channel_id=1, source_target_pairs={{1,0},{2,3},{5,4},{6,7},{9,8},{10,11},{13,12},{14,15},{17,16},{18,... | collective-permute-start | bytes 786440 | tf_op jit(solution)/shard_map/ppermute | solution.py:534

commit v6 on v5

--- a/solution.py
+++ b/solution.py
@@ -398,50 +398,84 @@
     )(info, kept, last_key, *queries, *states)
 
 
-def finish_kernel(n_type, n_part, info_ref, *refs):
-    own_refs, back_refs = refs[:n_part], refs[n_part : 2 * n_part]
-    values_ref, out_ref, attended_ref, value_ref = refs[2 * n_part :]
+def by_expert(n_type, values_ref, value_ref):
     me = lax.axis_index("type")
-    ends = (me == 0) | (me == n_type - 1)
-    tile = out_ref.shape[0]
-    width = out_ref.shape[1]
     for s in range(n_type):
         at = pl.multiple_of(jnp.bitwise_xor(me, s) * EXP_CAP, EXP_CAP)
         value_ref[pl.ds(at, EXP_CAP), :] = values_ref[s * EXP_CAP : (s + 1) * EXP_CAP]
-    row = lax.broadcasted_iota(jnp.int32, (n_type * EXP_CAP, tile), 0)
-    select = (row == info_ref[0:1, :].astype(jnp.int32)).astype(jnp.bfloat16)
+
+
+CONTRACT = (((0,), (0,)), ((), ()))
+
+
+def expert_out_kernel(n_type, info_ref, values_ref, out_ref, value_ref):
+    tile, width = out_ref.shape
+    by_expert(n_type, values_ref, value_ref)
+    select = slots_of(n_type * EXP_CAP, tile, 0, info_ref).astype(jnp.bfloat16)
     chunk, count = columns(width)
-    contract = (((0,), (0,)), ((), ()))
     for c in range(count):
         span = pl.ds(c * chunk, chunk)
         out_ref[:, span] = lax.dot_general(
-            select, value_ref[:, span], contract, preferred_element_type=jnp.float32
+            select, value_ref[:, span], CONTRACT, preferred_element_type=jnp.float32
         ).astype(jnp.bfloat16)
+
+
+def expert_output(n_type, info, values, tile):
+    slots, width = values.shape
+    return pl.pallas_call(
+        functools.partial(expert_out_kernel, n_type),
+        out_shape=jax.ShapeDtypeStruct((tile, width), jnp.bfloat16),
+        in_specs=[VMEM] * 2,
+        out_specs=VMEM,
+        scratch_shapes=[pltpu.VMEM((slots, width), jnp.bfloat16)],
+        compiler_params=params(8),
+        cost_estimate=cost(0, 0),
+    )(*held([info, values]))
+
+
+def attend_kernel(n_type, n_part, values_ref, *refs):
+    own_refs, back_refs = refs[:n_part], refs[n_part : 2 * n_part]
+    result_ref, value_ref, attended_ref, sems = refs[2 * n_part :]
+    me = lax.axis_index("type")
+    ends = (me == 0) | (me == n_type - 1)
+    by_expert(n_type, values_ref, value_ref)
     at = 0
+    copies = []
     for part in range(n_part):
         for h in range(own_refs[part].shape[0]):
             span = pl.ds(at * HEAD, HEAD)
-            weights = own_refs[part][h]
-            if back_refs:
-                weights = jnp.where(ends, back_refs[part][h], weights)
+            weights = jnp.where(ends, back_refs[part][h], own_refs[part][h])
             attended_ref[:, span] = lax.dot_general(
-                weights, value_ref[:, span], contract, preferred_element_type=jnp.float32
+                weights, value_ref[:, span], CONTRACT, preferred_element_type=jnp.float32
             ).astype(jnp.bfloat16)
             at += 1
-
-
-def finish(n_type, info, own, back, values, tile):
-    width = values.shape[1]
-    n_part = len(own)
-    return pl.pallas_call(
-        functools.partial(finish_kernel, n_type, n_part),
-        out_shape=[jax.ShapeDtypeStruct((tile, width), jnp.bfloat16)] * 2,
-        in_specs=[VMEM] * (2 + 2 * n_part),
-        out_specs=[VMEM] * 2,
-        scratch_shapes=[pltpu.VMEM((n_type * EXP_CAP, width), jnp.bfloat16)],
+            if at % 8 == 0:
+                done = pl.ds((at - 8) * HEAD, 8 * HEAD)
+                copies.append(
+                    pltpu.make_async_copy(
+                        attended_ref.at[:, done], result_ref.at[:, done], sems.at[at // 8 - 1]
+                    )
+                )
+                copies[-1].start()
+    for copy in copies:
+        copy.wait()
+
+
+def attend(n_type, own, back, values, tile):
+    slots, width = values.shape
+    return pl.pallas_call(
+        functools.partial(attend_kernel, n_type, len(own)),
+        out_shape=jax.ShapeDtypeStruct((tile, width), jnp.bfloat16),
+        in_specs=[VMEM] * (1 + 2 * len(own)),
+        out_specs=pl.BlockSpec(memory_space=pl.ANY),
+        scratch_shapes=[
+            pltpu.VMEM((slots, width), jnp.bfloat16),
+            pltpu.VMEM((tile, width), jnp.bfloat16),
+            pltpu.SemaphoreType.DMA((width // HEAD // 8,)),
+        ],
         compiler_params=params(8),
         cost_estimate=cost(0, 0),
-    )(*held([info, *own, *back, values]))
+    )(*held([values, *own, *back]))
 
 
 def swap(x, axis, size, s):
@@ -516,7 +550,7 @@
         twin, guest_state, far = tie((twin, guest_state, far))
         values = spread(jnp.concatenate([expert_rows, twin], axis=0), 2)
         own_weights, back_weights = [], []
-        ends = [0, heads // 2, heads]
+        ends = [0, heads]
         for first, last in zip(ends[:-1], ends[1:]):
             own, theirs = weigh_end(
                 n_type,
@@ -543,7 +577,9 @@
             weigh_end(n_type, info, kept, tiles[-1], [queries], [state], ids, 0, heads)
         )
         back_weights = own_weights
-    expert_out, attended = finish(n_type, info, own_weights, back_weights, values, tile)
+    expert_out = expert_output(n_type, info, values, tile)
+    values, expert_out = tie((values, expert_out))
+    attended = attend(n_type, own_weights, back_weights, values, tile)
     return (expert_out, attended)
 
 

time: 95.2 us -> 94.7 us (level)
  starting transfers between devices: 36 us -> 34.8 us
    ppermute x13, waiting for transfers between devices: 25.1 us -> 27 us  [swap(): return lax.ppermute(x, axis, [(i, i ^ s) for i in range(size)])]
    ppermute x2 -> x1, waiting for transfers between devices: 8.28 us -> 6.82 us  [on_device(): back_weights.append(lax.ppermute(theirs, 'type', to_end))]
    ppermute x2 -> x1, starting transfers between devices: 2.57 us -> 1.28 us  [on_device(): back_weights.append(lax.ppermute(theirs, 'type', to_end))]
    pallas_call x1 -> x2, Pallas kernels: 1.84 us -> 2.72 us  [the longest x1 1.43 us: expert_output(): pl.pallas_call(functools.partial(expert_out_kernel, n_type), out_shape=ja...]
    pallas_call x2 -> x1, Pallas kernels: 1.91 us -> 1.39 us  [weigh_end(): pl.pallas_call(functools.partial(in_middle, weigh_end_body, n_type, tile_...]
  transfers between devices with their start and end apart: 19 -> 18, of which waited for: 12 -> 11; matrix products, arithmetic and copies ran while one was open for 0% -> 0% of each run, Pallas kernels for 18% -> 19%
where the time goes in v6:
time: 94.7 us; the launch traced here: 94.4 us
  waiting for transfers between devices  37.8 us (40%)
  starting transfers between devices  34.8 us (37%)
  Pallas kernels  20.6 us (22%)
    ppermute x13, waiting for transfers between devices, swap(): return lax.ppermute(x, axis, [(i, i ^ s) for i in range(size)])  27 us
    ppermute x13, starting transfers between devices, swap(): return lax.ppermute(x, axis, [(i, i ^ s) for i in range(size)])  24.1 us
    pallas_call x1, Pallas kernels, fetch(): pl.pallas_call(functools.partial(fetch_kernel, count), out_shape=[pltpu.V...  7.28 us
    ppermute x1, waiting for transfers between devices, on_device(): back_weights.append(lax.ppermute(theirs, 'type', to_end))  6.82 us
    ppermute x1, starting transfers between devices, on_device(): near = lax.ppermute(keys, 'type', to_middle)  4.93 us
    ppermute x1, waiting for transfers between devices, on_device(): guest = lax.ppermute(queries, 'type', to_middle)  3.88 us
    pallas_call x1, Pallas kernels, ffn(): pl.pallas_call(ffn_kernel, out_shape=[jax.ShapeDtypeStruct((half, width),...  3.58 us
    pallas_call x2, Pallas kernels, weigh_begin(): pl.pallas_call(functools.partial(in_middle, weigh_begin_body, n_type, til...  3.51 us
  transfers between devices with their start and end apart: 18, of which 11 were waited for; matrix products, arithmetic and copies ran while one was open for 0% of the time, Pallas kernels for 19%

profile of v6, /device:TPU:0, one launch (start us, length us, event | category | flops | bytes accessed | tf_op | source)
XLA Modules:
  0.0 94.4 jit_solution(17855557173293951157)
XLA Ops:
  0.6 1.7 %shard_map.98 = (bf16[16,4224]{1,0:T(8,128)(2,1)S(1)}, bf16[16,4224]{1,0:T(8,128)(2,1)S(1)}, bf16[16,4224]{1,0:T(8,128)(2,1)S(1)}, bf16[16,4224]{1,0:T(8,128)(2,1)S(1)}) custom-call(s32[1,128]{1,0:T(1,128)} %bitcast.8, s32[1,4]{1,0:T(1,128)} %bitcast.9, bf16[128,4096]{1,0:T(8,128)(2,1)} %tokens_ref.1), custom_call_target="tpu_custom_call" | custom-call | tf_op jit(solution)/shard_map/pallas_call | solution.py:87
  2.3 3.1 %collective-permute-start.8 = (bf16[16,4224]{1,0:T(8,128)(2,1)S(1)}, bf16[16,4224]{1,0:T(8,128)(2,1)S(1)}, u32[]{:S(2)}, u32[]{:S(2)}) collective-permute-start(bf16[16,4224]{1,0:T(8,128)(2,1)S(1)} %get-tuple-element.97), channel_id=1, source_target_pairs={{0,1},{1,0},{2,3},{3,2},{4,5},{5,4},{6,7},{7,6},{8,9},{9,8},{10,11... | collective-permute-start | bytes 405512 | tf_op jit(solution)/shard_map/ppermute | solution.py:482
  5.4 2.6 %collective-permute-start.9 = (bf16[16,4224]{1,0:T(8,128)(2,1)S(1)}, bf16[16,4224]{1,0:T(8,128)(2,1)S(1)}, u32[]{:S(2)}, u32[]{:S(2)}) collective-permute-start(bf16[16,4224]{1,0:T(8,128)(2,1)S(1)} %get-tuple-element.98), channel_id=1, source_target_pairs={{0,2},{1,3},{2,0},{3,1},{4,6},{5,7},{6,4},{7,5},{8,10},{9,11},{10,... | collective-permute-start | bytes 405512 | tf_op jit(solution)/shard_map/ppermute | solution.py:482
  8.0 0.0 collective-permute-start.10
  8.0 2.6 %collective-permute-done.8 = bf16[16,4224]{1,0:T(8,128)(2,1)S(1)} collective-permute-done((bf16[16,4224]{1,0:T(8,128)(2,1)S(1)}, bf16[16,4224]{1,0:T(8,128)(2,1)S(1)}, u32[]{:S(2)}, u32[]{:S(2)}) %collective-permute-start.8) | collective-permute-done | bytes 135200 | tf_op jit(solution)/shard_map/ppermute | solution.py:482
  10.7 8.0 %collective-permute-done.9 = bf16[16,4224]{1,0:T(8,128)(2,1)S(1)} collective-permute-done((bf16[16,4224]{1,0:T(8,128)(2,1)S(1)}, bf16[16,4224]{1,0:T(8,128)(2,1)S(1)}, u32[]{:S(2)}, u32[]{:S(2)}) %collective-permute-start.9) | collective-permute-done | bytes 135200 | tf_op jit(solution)/shard_map/ppermute | solution.py:482
  18.6 0.0 collective-permute-done.10
  18.6 4.9 %collective-permute-start.11 = (bf16[128,4096]{1,0:T(8,128)(2,1)}, bf16[128,4096]{1,0:T(8,128)(2,1)}, u32[]{:S(2)}, u32[]{:S(2)}) collective-permute-start(bf16[128,4096]{1,0:T(8,128)(2,1)} %args_2_), channel_id=1, source_target_pairs={{0,1},{3,2},{4,5},{7,6},{8,9},{11,10},{12,13},{15,14},{16,17},{19,... | collective-permute-start | bytes 3145736 | tf_op jit(solution)/shard_map/ppermute | solution.py:537
  23.6 1.6 %collective-permute-start.12 = (bf16[128,4096]{1,0:T(8,128)(2,1)}, bf16[128,4096]{1,0:T(8,128)(2,1)}, u32[]{:S(2)}, u32[]{:S(2)}) collective-permute-start(bf16[128,4096]{1,0:T(8,128)(2,1)} %args_2_), channel_id=1, source_target_pairs={{1,2},{2,1},{5,6},{6,5},{9,10},{10,9},{13,14},{14,13},{17,18},{18,... | collective-permute-start | bytes 3145736 | tf_op jit(solution)/shard_map/ppermute | solution.py:538
  25.2 2.2 %collective-permute-start.13 = (bf16[128,4096]{1,0:T(8,128)(2,1)}, bf16[128,4096]{1,0:T(8,128)(2,1)S(1)}, u32[]{:S(2)}, u32[]{:S(2)}) collective-permute-start(bf16[128,4096]{1,0:T(8,128)(2,1)} %args_3_), channel_id=1, source_target_pairs={{0,1},{3,2},{4,5},{7,6},{8,9},{11,10},{12,13},{15,14},{16,17},{19,... | collective-permute-start | bytes 3145736 | tf_op jit(solution)/shard_map/ppermute | solution.py:539
  27.4 0.0 copy-start
  27.4 19.9 %conditional.2 = (f32[12,128]{1,0:T(8,128)S(1)}, f32[64,4096]{1,0:T(8,128)S(1)}, bf16[64,4096]{1,0:T(8,128)(2,1)S(1)}) conditional(s32[]{:T(128)} %convert_element_type.25, () %tuple.32, (bf16[16,4224]{1,0:T(8,128)(2,1)S(1)}, bf16[16,4224]{1,0:T(8,128)(2,1)S(1)}, bf16[16,4224]{1,0:T(8,128)(2,1)S(1)}, bf16[16,4224]{1,0:T(8,128)(2,1)S(1)}, ...), branch_computations={%region_0.0_spmd, %region_1.0_spmd} | conditional | bytes 48758968 | solution.py:488
  27.5 0.4 branch_1_fun.4
  27.9 1.6 %collective-permute-start.1 = (bf16[16,4096]{1,0:T(8,128)(2,1)S(1)}, bf16[16,4096]{1,0:T(8,128)(2,1)S(1)}, u32[]{:S(2)}, u32[]{:S(2)}) collective-permute-start(bf16[16,4096]{1,0:T(8,128)(2,1)S(1)} %get-tuple-element.43), channel_id=1, source_target_pairs={{0,16},{4,20},{8,24},{12,28},{16,0},{20,4},{24,8},{28,12},{1,17},{... | collective-permute-start | bytes 393224 | tf_op jit(solution)/shard_map/cond/branch_1_fun/ppermute | solution.py:482
  29.4 1.5 %collective-permute-start = (bf16[16,4096]{1,0:T(8,128)(2,1)S(1)}, bf16[16,4096]{1,0:T(8,128)(2,1)S(1)}, u32[]{:S(2)}, u32[]{:S(2)}) collective-permute-start(bf16[16,4096]{1,0:T(8,128)(2,1)S(1)} %get-tuple-element.43), channel_id=1, source_target_pairs={{0,8},{4,12},{8,0},{12,4},{16,24},{20,28},{24,16},{28,20},{1,9},{5... | collective-permute-start | bytes 393224 | tf_op jit(solution)/shard_map/cond/branch_1_fun/ppermute | solution.py:482
  30.9 2.0 %collective-permute-done.1 = bf16[16,4096]{1,0:T(8,128)(2,1)S(1)} collective-permute-done((bf16[16,4096]{1,0:T(8,128)(2,1)S(1)}, bf16[16,4096]{1,0:T(8,128)(2,1)S(1)}, u32[]{:S(2)}, u32[]{:S(2)}) %collective-permute-start.1) | collective-permute-done | bytes 131104 | tf_op jit(solution)/shard_map/cond/branch_1_fun/ppermute | solution.py:482
  32.9 1.5 %collective-permute-start.2 = (bf16[16,4096]{1,0:T(8,128)(2,1)S(1)}, bf16[16,4096]{1,0:T(8,128)(2,1)S(1)}, u32[]{:S(2)}, u32[]{:S(2)}) collective-permute-start(bf16[16,4096]{1,0:T(8,128)(2,1)S(1)} %collective-permute-done.1), channel_id=1, source_target_pairs={{0,8},{4,12},{8,0},{12,4},{16,24},{20,28},{24,16},{28,20},{1,9},{5... | collective-permute-start | bytes 393224 | tf_op jit(solution)/shard_map/cond/branch_1_fun/ppermute | solution.py:482
  34.4 7.3 %branch_1_fun.5 = (bf16[4096,896]{1,0:T(8,128)(2,1)S(1)}, bf16[4096,896]{1,0:T(8,128)(2,1)S(1)}, bf16[896,4096]{1,0:T(8,128)(2,1)S(1)}) custom-call(bf16[4096,896]{1,0:T(8,128)(2,1)} %bitcast.5, bf16[4096,896]{1,0:T(8,128)(2,1)} %bitcast.6, bf16[896,4096]{1,0:T(8,128)(2,1)} %bitcast.7), custom_call_target="tpu_custom_call" | custom-call | bytes 44040192 | tf_op jit(solution)/shard_map/cond/branch_1_fun/pallas_call | solution.py:114
  41.7 0.0 collective-permute-done
  41.7 0.0 collective-permute-done.2
  41.8 0.1 collective-permute-start.3
  41.9 1.9 %collective-permute-done.3.far_ref = bf16[64,4096]{1,0:T(8,128)(2,1)S(1)} collective-permute-done((bf16[64,4096]{1,0:T(8,128)(2,1)S(1)}, bf16[64,4096]{1,0:T(8,128)(2,1)S(1)}, u32[]{:S(2)}, u32[]{:S(2)}) %collective-permute-start.3) | collective-permute-done | bytes 524320 | tf_op jit(solution)/shard_map/cond/branch_1_fun/ppermute | solution.py:482
  43.8 3.6 %branch_1_fun.6 = (f32[64,4096]{1,0:T(8,128)S(1)}, bf16[64,4096]{1,0:T(8,128)(2,1)S(1)}) custom-call(bf16[64,4096]{1,0:T(8,128)(2,1)S(1)} %constant_dynamic-update-slice_fusion.near_ref, bf16[64,4096]{1,0:T(8,128)(2,1)S(1)} %collective-permute-done.3.far_ref, bf16[4096,896]{1,0:T(8,128)(2,1)S(1)} %get-tuple-element.47.gate_ref, ...), custom_call_target="tpu_custom_call" | custom-call | tf_op jit(solution)/shard_map/cond/branch_1_fun/pallas_call | solution.py:216
  47.4 0.7 collective-permute-start.15
  48.1 11.6 %conditional.3 = (bf16[16,4096]{1,0:T(8,128)(2,1)S(1)}, f32[32,16,128]{2,1,0:T(8,128)S(1)}, bf16[64,4096]{1,0:T(8,128)(2,1)S(1)}) conditional(s32[]{:T(128)} %convert_element_type.25, () %tuple.31, (bf16[64,4096]{1,0:T(8,128)(2,1)S(1)}, f32[64,4096]{1,0:T(8,128)S(1)}, f32[12,128]{1,0:T(8,128)S(1)}, bf16[128,4096]{1,0:T(8,128)(2,1)}, ...), branch_computations={%region_2.0_spmd, %region_3.0_spmd} | conditional | flops 1310720 | bytes 15859896 | solution.py:488
  48.1 0.2 collective-permute-start.4
  48.3 1.8 %collective-permute-done.4 = bf16[64,4096]{1,0:T(8,128)(2,1)S(1)} collective-permute-done((bf16[64,4096]{1,0:T(8,128)(2,1)S(1)}, bf16[64,4096]{1,0:T(8,128)(2,1)S(1)}, u32[]{:S(2)}, u32[]{:S(2)}) %collective-permute-start.4) | collective-permute-done | bytes 524320 | tf_op jit(solution)/shard_map/cond/branch_1_fun/ppermute | solution.py:482
  50.1 0.1 add_convert_fusion
  50.2 1.6 %collective-permute-start.7 = (bf16[16,4096]{1,0:T(8,128)(2,1)S(1)}, bf16[16,4096]{1,0:T(8,128)(2,1)S(1)}, u32[]{:S(2)}, u32[]{:S(2)}) collective-permute-start(bf16[16,4096]{1,0:T(8,128)(2,1)S(1)} %get-tuple-element.129), channel_id=1, source_target_pairs={{0,24},{4,28},{8,16},{12,20},{16,8},{20,12},{24,0},{28,4},{1,25},{... | collective-permute-start | bytes 393224 | tf_op jit(solution)/shard_map/cond/branch_1_fun/ppermute | solution.py:482
  51.9 0.5 collective-permute-start.6
  52.4 1.4 %collective-permute-start.5 = (bf16[16,4096]{1,0:T(8,128)(2,1)S(1)}, bf16[16,4096]{1,0:T(8,128)(2,1)S(1)}, u32[]{:S(2)}, u32[]{:S(2)}) collective-permute-start(bf16[16,4096]{1,0:T(8,128)(2,1)S(1)} %get-tuple-element.131), channel_id=1, source_target_pairs={{0,8},{4,12},{8,0},{12,4},{16,24},{20,28},{24,16},{28,20},{1,9},{5... | collective-permute-start | bytes 393224 | tf_op jit(solution)/shard_map/cond/branch_1_fun/ppermute | solution.py:482
  53.8 1.9 %branch_1_fun.7 = (f32[32,16,128]{2,1,0:T(8,128)S(1)}, bf16[64,4096]{1,0:T(8,128)(2,1)S(1)}) custom-call(f32[12,128]{1,0:T(8,128)S(1)} %get-tuple-element.54.args_0_, bf16[128,4096]{1,0:T(8,128)(2,1)} %get-tuple-element.55.args_1_, bf16[128,4096]{1,0:T(8,128)(2,1)S(1)} %get-tuple-element.56.args_2_, bf16[128,4096]{1,0:T(8,128)(2,1)} %get-tuple-element.57.args_3_, ...), custom_call_target="tpu_custom_call" | custom-call | bytes 8388608 | tf_op jit(solution)/shard_map/cond/branch_1_fun/pallas_call | solution.py:322
  55.7 1.9 %collective-permute-done.7 = bf16[16,4096]{1,0:T(8,128)(2,1)S(1)} collective-permute-done((bf16[16,4096]{1,0:T(8,128)(2,1)S(1)}, bf16[16,4096]{1,0:T(8,128)(2,1)S(1)}, u32[]{:S(2)}, u32[]{:S(2)}) %collective-permute-start.7) | collective-permute-done | bytes 131104 | tf_op jit(solution)/shard_map/cond/branch_1_fun/ppermute | solution.py:482
  57.6 2.0 %collective-permute-done.6 = bf16[16,4096]{1,0:T(8,128)(2,1)S(1)} collective-permute-done((bf16[16,4096]{1,0:T(8,128)(2,1)S(1)}, bf16[16,4096]{1,0:T(8,128)(2,1)S(1)}, u32[]{:S(2)}, u32[]{:S(2)}) %collective-permute-start.6) | collective-permute-done | bytes 131104 | tf_op jit(solution)/shard_map/cond/branch_1_fun/ppermute | solution.py:482
  59.5 0.1 collective-permute-done.5
  59.7 0.1 add_convert_fusion.1
  59.7 0.0 copy-start.1
  59.7 4.4 %collective-permute-start.14 = (bf16[16,4096]{1,0:T(8,128)(2,1)S(1)}, bf16[16,4096]{1,0:T(8,128)(2,1)S(1)}, u32[]{:S(2)}, u32[]{:S(2)}) collective-permute-start(bf16[16,4096]{1,0:T(8,128)(2,1)S(1)} %get-tuple-element.112), channel_id=1, source_target_pairs={{0,1},{1,0},{2,3},{3,2},{4,5},{5,4},{6,7},{7,6},{8,9},{9,8},{10,11... | collective-permute-start | bytes 393224 | tf_op jit(solution)/shard_map/ppermute | solution.py:482
  64.1 3.9 %collective-permute-done.13.args_1_.args_4_ = bf16[128,4096]{1,0:T(8,128)(2,1)S(1)} collective-permute-done((bf16[128,4096]{1,0:T(8,128)(2,1)}, bf16[128,4096]{1,0:T(8,128)(2,1)S(1)}, u32[]{:S(2)}, u32[]{:S(2)}) %collective-permute-start.13) | collective-permute-done | bytes 1048608 | tf_op jit(solution)/shard_map/ppermute | solution.py:539
  68.0 1.6 %shard_map.99.args_6_ = f32[32,16,128]{2,1,0:T(8,128)S(1)} custom-call(f32[12,128]{1,0:T(8,128)S(1)} %get-tuple-element.108.args_0_.info_ref, bf16[128,4096]{1,0:T(8,128)(2,1)S(1)} %collective-permute-done.13.args_1_.args_4_, bf16[128,4096]{1,0:T(8,128)(2,1)S(1)} %copy-done, bf16[128,4096]{1,0:T(8,128)(2,1)} %collective-permute-done.11.args_3_, ...), custom_call_target="tpu_custom_call" | custom-call | bytes 8388608 | tf_op jit(solution)/shard_map/pallas_call | solution.py:322
  69.7 0.0 collective-permute-done.14
  69.7 5.6 %collective-permute-start.16 = (bf16[32,4096]{1,0:T(8,128)(2,1)S(1)}, bf16[32,4096]{1,0:T(8,128)(2,1)S(1)}, u32[]{:S(2)}, u32[]{:S(2)}) collective-permute-start(bf16[32,4096]{1,0:T(8,128)(2,1)S(1)} %pad_maximum_fusion), channel_id=1, source_target_pairs={{0,2},{1,3},{2,0},{3,1},{4,6},{5,7},{6,4},{7,5},{8,10},{9,11},{10,... | collective-permute-start | bytes 786440 | tf_op jit(solution)/shard_map/ppermute | solution.py:482
  75.3 1.4 %shard_map.101 = (bf16[32,64,128]{2,1,0:T(8,128)(2,1)S(1)}, bf16[32,64,128]{2,1,0:T(8,128)(2,1)S(1)}) custom-call(f32[12,128]{1,0:T(8,128)S(1)} %get-tuple-element.108.args_0_.info_ref, bf16[64,4096]{1,0:T(8,128)(2,1)} %copy-done.1, bf16[128,4096]{1,0:T(8,128)(2,1)S(1)} %collective-permute-done.15.args_2_, bf16[128,4096]{1,0:T(8,128)(2,1)} %args_3_, ...), custom_call_target="tpu_custom_call" | custom-call | tf_op jit(solution)/shard_map/pallas_call | solution.py:387
  76.7 1.3 %collective-permute-start.17 = (bf16[32,64,128]{2,1,0:T(8,128)(2,1)S(1)}, bf16[32,64,128]{2,1,0:T(8,128)(2,1)S(1)}, u32[]{:S(2)}, u32[]{:S(2)}) collective-permute-start(bf16[32,64,128]{2,1,0:T(8,128)(2,1)S(1)} %get-tuple-element.122), channel_id=1, source_target_pairs={{1,0},{2,3},{5,4},{6,7},{9,8},{10,11},{13,12},{14,15},{17,16},{18,... | collective-permute-start | bytes 1572872 | tf_op jit(solution)/shard_map/ppermute | solution.py:568
  78.0 6.8 %collective-permute-done.16 = bf16[32,4096]{1,0:T(8,128)(2,1)S(1)} collective-permute-done((bf16[32,4096]{1,0:T(8,128)(2,1)S(1)}, bf16[32,4096]{1,0:T(8,128)(2,1)S(1)}, u32[]{:S(2)}, u32[]{:S(2)}) %collective-permute-start.16) | collective-permute-done | bytes 262176 | tf_op jit(solution)/shard_map/ppermute | solution.py:482
  84.8 1.4 %shard_map.100 = bf16[128,4096]{1,0:T(8,128)(2,1)} custom-call(f32[12,128]{1,0:T(8,128)S(1)} %get-tuple-element.108.args_0_.info_ref, bf16[64,4096]{1,0:T(8,128)(2,1)S(1)} %constant_dynamic-update-slice_fusion.4.values_ref), custom_call_target="tpu_custom_call" | custom-call | tf_op jit(solution)/shard_map/pallas_call | solution.py:425
  86.3 6.8 %collective-permute-done.17.refs_1_ = bf16[32,64,128]{2,1,0:T(8,128)(2,1)S(1)} collective-permute-done((bf16[32,64,128]{2,1,0:T(8,128)(2,1)S(1)}, bf16[32,64,128]{2,1,0:T(8,128)(2,1)S(1)}, u32[]{:S(2)}, u32[]{:S(2)}) %collective-permute-start.17) | collective-permute-done | bytes 524320 | tf_op jit(solution)/shard_map/ppermute | solution.py:568
  93.1 1.3 %shard_map.102 = bf16[128,4096]{1,0:T(8,128)(2,1)} custom-call(bf16[64,4096]{1,0:T(8,128)(2,1)S(1)} %constant_dynamic-update-slice_fusion.4.values_ref, bf16[32,64,128]{2,1,0:T(8,128)(2,1)S(1)} %get-tuple-element.121.refs_0_, bf16[32,64,128]{2,1,0:T(8,128)(2,1)S(1)} %collective-permute-done.17.refs_1_), custom_call_target="tpu_custom_call" | custom-call | tf_op jit(solution)/shard_map/pallas_call | solution.py:466
  (14 shorter events, 0.1 us)
Async XLA Ops:
  2.3 8.3 %collective-permute-start.8 = (bf16[16,4224]{1,0:T(8,128)(2,1)S(1)}, bf16[16,4224]{1,0:T(8,128)(2,1)S(1)}, u32[]{:S(2)}, u32[]{:S(2)}) collective-permute-start(bf16[16,4224]{1,0:T(8,128)(2,1)S(1)} %get-tuple-element.97), channel_id=1, source_target_pairs={{0,1},{1,0},{2,3},{3,2},{4,5},{5,4},{6,7},{7,6},{8,9},{9,8},{10,11... | collective-permute-start | bytes 405512 | tf_op jit(solution)/shard_map/ppermute | solution.py:482
  5.4 13.2 %collective-permute-start.9 = (bf16[16,4224]{1,0:T(8,128)(2,1)S(1)}, bf16[16,4224]{1,0:T(8,128)(2,1)S(1)}, u32[]{:S(2)}, u32[]{:S(2)}) collective-permute-start(bf16[16,4224]{1,0:T(8,128)(2,1)S(1)} %get-tuple-element.98), channel_id=1, source_target_pairs={{0,2},{1,3},{2,0},{3,1},{4,6},{5,7},{6,4},{7,5},{8,10},{9,11},{10,... | collective-permute-start | bytes 405512 | tf_op jit(solution)/shard_map/ppermute | solution.py:482
  8.0 10.6 %collective-permute-start.10 = (bf16[16,4224]{1,0:T(8,128)(2,1)S(1)}, bf16[16,4224]{1,0:T(8,128)(2,1)S(1)}, u32[]{:S(2)}, u32[]{:S(2)}) collective-permute-start(bf16[16,4224]{1,0:T(8,128)(2,1)S(1)} %get-tuple-element.99), channel_id=1, source_target_pairs={{0,3},{1,2},{2,1},{3,0},{4,7},{5,6},{6,5},{7,4},{8,11},{9,10},{10,... | collective-permute-start | bytes 405512 | tf_op jit(solution)/shard_map/ppermute | solution.py:482
  18.6 28.7 %collective-permute-start.11 = (bf16[128,4096]{1,0:T(8,128)(2,1)}, bf16[128,4096]{1,0:T(8,128)(2,1)}, u32[]{:S(2)}, u32[]{:S(2)}) collective-permute-start(bf16[128,4096]{1,0:T(8,128)(2,1)} %args_2_), channel_id=1, source_target_pairs={{0,1},{3,2},{4,5},{7,6},{8,9},{11,10},{12,13},{15,14},{16,17},{19,... | collective-permute-start | bytes 3145736 | tf_op jit(solution)/shard_map/ppermute | solution.py:537
  23.6 24.5 %collective-permute-start.12 = (bf16[128,4096]{1,0:T(8,128)(2,1)}, bf16[128,4096]{1,0:T(8,128)(2,1)}, u32[]{:S(2)}, u32[]{:S(2)}) collective-permute-start(bf16[128,4096]{1,0:T(8,128)(2,1)} %args_2_), channel_id=1, source_target_pairs={{1,2},{2,1},{5,6},{6,5},{9,10},{10,9},{13,14},{14,13},{17,18},{18,... | collective-permute-start | bytes 3145736 | tf_op jit(solution)/shard_map/ppermute | solution.py:538
  25.2 42.8 %collective-permute-start.13 = (bf16[128,4096]{1,0:T(8,128)(2,1)}, bf16[128,4096]{1,0:T(8,128)(2,1)S(1)}, u32[]{:S(2)}, u32[]{:S(2)}) collective-permute-start(bf16[128,4096]{1,0:T(8,128)(2,1)} %args_3_), channel_id=1, source_target_pairs={{0,1},{3,2},{4,5},{7,6},{8,9},{11,10},{12,13},{15,14},{16,17},{19,... | collective-permute-start | bytes 3145736 | tf_op jit(solution)/shard_map/ppermute | solution.py:539
  27.4 20.7 %copy-start = (bf16[128,4096]{1,0:T(8,128)(2,1)S(1)}, bf16[128,4096]{1,0:T(8,128)(2,1)}, u32[]{:S(2)}) copy-start(bf16[128,4096]{1,0:T(8,128)(2,1)} %args_2_) | copy-start | bytes 3145732
  27.9 5.0 %collective-permute-start.1 = (bf16[16,4096]{1,0:T(8,128)(2,1)S(1)}, bf16[16,4096]{1,0:T(8,128)(2,1)S(1)}, u32[]{:S(2)}, u32[]{:S(2)}) collective-permute-start(bf16[16,4096]{1,0:T(8,128)(2,1)S(1)} %get-tuple-element.43), channel_id=1, source_target_pairs={{0,16},{4,20},{8,24},{12,28},{16,0},{20,4},{24,8},{28,12},{1,17},{... | collective-permute-start | bytes 393224 | tf_op jit(solution)/shard_map/cond/branch_1_fun/ppermute | solution.py:482
  29.4 12.2 %collective-permute-start = (bf16[16,4096]{1,0:T(8,128)(2,1)S(1)}, bf16[16,4096]{1,0:T(8,128)(2,1)S(1)}, u32[]{:S(2)}, u32[]{:S(2)}) collective-permute-start(bf16[16,4096]{1,0:T(8,128)(2,1)S(1)} %get-tuple-element.43), channel_id=1, source_target_pairs={{0,8},{4,12},{8,0},{12,4},{16,24},{20,28},{24,16},{28,20},{1,9},{5... | collective-permute-start | bytes 393224 | tf_op jit(solution)/shard_map/cond/branch_1_fun/ppermute | solution.py:482
  32.9 8.8 %collective-permute-start.2 = (bf16[16,4096]{1,0:T(8,128)(2,1)S(1)}, bf16[16,4096]{1,0:T(8,128)(2,1)S(1)}, u32[]{:S(2)}, u32[]{:S(2)}) collective-permute-start(bf16[16,4096]{1,0:T(8,128)(2,1)S(1)} %collective-permute-done.1), channel_id=1, source_target_pairs={{0,8},{4,12},{8,0},{12,4},{16,24},{20,28},{24,16},{28,20},{1,9},{5... | collective-permute-start | bytes 393224 | tf_op jit(solution)/shard_map/cond/branch_1_fun/ppermute | solution.py:482
  41.8 2.0 %collective-permute-start.3 = (bf16[64,4096]{1,0:T(8,128)(2,1)S(1)}, bf16[64,4096]{1,0:T(8,128)(2,1)S(1)}, u32[]{:S(2)}, u32[]{:S(2)}) collective-permute-start(bf16[64,4096]{1,0:T(8,128)(2,1)S(1)} %constant_dynamic-update-slice_fusion.near_ref), channel_id=1, source_target_pairs={{0,4},{4,0},{8,12},{12,8},{16,20},{20,16},{24,28},{28,24},{1,5},{5... | collective-permute-start | bytes 1572872 | tf_op jit(solution)/shard_map/cond/branch_1_fun/ppermute | solution.py:482
  47.4 22.3 %collective-permute-start.15 = (bf16[128,4096]{1,0:T(8,128)(2,1)}, bf16[128,4096]{1,0:T(8,128)(2,1)S(1)}, u32[]{:S(2)}, u32[]{:S(2)}) collective-permute-start(bf16[128,4096]{1,0:T(8,128)(2,1)} %collective-permute-done.11.args_3_), channel_id=1, source_target_pairs={{1,2},{2,1},{5,6},{6,5},{9,10},{10,9},{13,14},{14,13},{17,18},{18,... | collective-permute-start | bytes 3145736 | tf_op jit(solution)/shard_map/ppermute | solution.py:542
  48.1 2.0 %collective-permute-start.4 = (bf16[64,4096]{1,0:T(8,128)(2,1)S(1)}, bf16[64,4096]{1,0:T(8,128)(2,1)S(1)}, u32[]{:S(2)}, u32[]{:S(2)}) collective-permute-start(bf16[64,4096]{1,0:T(8,128)(2,1)S(1)} %get-tuple-element.53), channel_id=1, source_target_pairs={{0,4},{4,0},{8,12},{12,8},{16,20},{20,16},{24,28},{28,24},{1,5},{5... | collective-permute-start | bytes 1572872 | tf_op jit(solution)/shard_map/cond/branch_1_fun/ppermute | solution.py:482
  50.2 7.3 %collective-permute-start.7 = (bf16[16,4096]{1,0:T(8,128)(2,1)S(1)}, bf16[16,4096]{1,0:T(8,128)(2,1)S(1)}, u32[]{:S(2)}, u32[]{:S(2)}) collective-permute-start(bf16[16,4096]{1,0:T(8,128)(2,1)S(1)} %get-tuple-element.129), channel_id=1, source_target_pairs={{0,24},{4,28},{8,16},{12,20},{16,8},{20,12},{24,0},{28,4},{1,25},{... | collective-permute-start | bytes 393224 | tf_op jit(solution)/shard_map/cond/branch_1_fun/ppermute | solution.py:482
  51.9 7.7 %collective-permute-start.6 = (bf16[16,4096]{1,0:T(8,128)(2,1)S(1)}, bf16[16,4096]{1,0:T(8,128)(2,1)S(1)}, u32[]{:S(2)}, u32[]{:S(2)}) collective-permute-start(bf16[16,4096]{1,0:T(8,128)(2,1)S(1)} %get-tuple-element.130), channel_id=1, source_target_pairs={{0,16},{4,20},{8,24},{12,28},{16,0},{20,4},{24,8},{28,12},{1,17},{... | collective-permute-start | bytes 393224 | tf_op jit(solution)/shard_map/cond/branch_1_fun/ppermute | solution.py:482
  52.4 7.3 %collective-permute-start.5 = (bf16[16,4096]{1,0:T(8,128)(2,1)S(1)}, bf16[16,4096]{1,0:T(8,128)(2,1)S(1)}, u32[]{:S(2)}, u32[]{:S(2)}) collective-permute-start(bf16[16,4096]{1,0:T(8,128)(2,1)S(1)} %get-tuple-element.131), channel_id=1, source_target_pairs={{0,8},{4,12},{8,0},{12,4},{16,24},{20,28},{24,16},{28,20},{1,9},{5... | collective-permute-start | bytes 393224 | tf_op jit(solution)/shard_map/cond/branch_1_fun/ppermute | solution.py:482
  59.7 4.4 %copy-start.1 = (bf16[64,4096]{1,0:T(8,128)(2,1)}, bf16[64,4096]{1,0:T(8,128)(2,1)S(1)}, u32[]{:S(2)}) copy-start(bf16[64,4096]{1,0:T(8,128)(2,1)S(1)} %get-tuple-element.117.args_1_) | copy-start | bytes 1572868
  59.7 9.9 %collective-permute-start.14 = (bf16[16,4096]{1,0:T(8,128)(2,1)S(1)}, bf16[16,4096]{1,0:T(8,128)(2,1)S(1)}, u32[]{:S(2)}, u32[]{:S(2)}) collective-permute-start(bf16[16,4096]{1,0:T(8,128)(2,1)S(1)} %get-tuple-element.112), channel_id=1, source_target_pairs={{0,1},{1,0},{2,3},{3,2},{4,5},{5,4},{6,7},{7,6},{8,9},{9,8},{10,11... | collective-permute-start | bytes 393224 | tf_op jit(solution)/shard_map/ppermute | solution.py:482
  69.7 15.1 %collective-permute-start.16 = (bf16[32,4096]{1,0:T(8,128)(2,1)S(1)}, bf16[32,4096]{1,0:T(8,128)(2,1)S(1)}, u32[]{:S(2)}, u32[]{:S(2)}) collective-permute-start(bf16[32,4096]{1,0:T(8,128)(2,1)S(1)} %pad_maximum_fusion), channel_id=1, source_target_pairs={{0,2},{1,3},{2,0},{3,1},{4,6},{5,7},{6,4},{7,5},{8,10},{9,11},{10,... | collective-permute-start | bytes 786440 | tf_op jit(solution)/shard_map/ppermute | solution.py:482
  76.7 16.4 %collective-permute-start.17 = (bf16[32,64,128]{2,1,0:T(8,128)(2,1)S(1)}, bf16[32,64,128]{2,1,0:T(8,128)(2,1)S(1)}, u32[]{:S(2)}, u32[]{:S(2)}) collective-permute-start(bf16[32,64,128]{2,1,0:T(8,128)(2,1)S(1)} %get-tuple-element.122), channel_id=1, source_target_pairs={{1,0},{2,3},{5,4},{6,7},{9,8},{10,11},{13,12},{14,15},{17,16},{18,... | collective-permute-start | bytes 1572872 | tf_op jit(solution)/shard_map/ppermute | solution.py:568

commit v7 on v6

--- a/solution.py
+++ b/solution.py
@@ -449,11 +449,11 @@
                 weights, value_ref[:, span], CONTRACT, preferred_element_type=jnp.float32
             ).astype(jnp.bfloat16)
             at += 1
-            if at % 8 == 0:
-                done = pl.ds((at - 8) * HEAD, 8 * HEAD)
+            if at % 4 == 0:
+                done = pl.ds((at - 4) * HEAD, 4 * HEAD)
                 copies.append(
                     pltpu.make_async_copy(
-                        attended_ref.at[:, done], result_ref.at[:, done], sems.at[at // 8 - 1]
+                        attended_ref.at[:, done], result_ref.at[:, done], sems.at[at // 4 - 1]
                     )
                 )
                 copies[-1].start()
@@ -471,7 +471,7 @@
         scratch_shapes=[
             pltpu.VMEM((slots, width), jnp.bfloat16),
             pltpu.VMEM((tile, width), jnp.bfloat16),
-            pltpu.SemaphoreType.DMA((width // HEAD // 8,)),
+            pltpu.SemaphoreType.DMA((width // HEAD // 4,)),
         ],
         compiler_params=params(8),
         cost_estimate=cost(0, 0),

time: 94.7 us -> 94.6 us (level)
  no operation moved by 1% of the time
where the time goes in v7:
time: 94.6 us; the launch traced here: 94.4 us
  waiting for transfers between devices  37.8 us (40%)
  starting transfers between devices  34.8 us (37%)
  Pallas kernels  20.6 us (22%)
    ppermute x13, waiting for transfers between devices, swap(): return lax.ppermute(x, axis, [(i, i ^ s) for i in range(size)])  27 us
    ppermute x13, starting transfers between devices, swap(): return lax.ppermute(x, axis, [(i, i ^ s) for i in range(size)])  24.1 us
    pallas_call x1, Pallas kernels, fetch(): pl.pallas_call(functools.partial(fetch_kernel, count), out_shape=[pltpu.V...  7.28 us
    ppermute x1, waiting for transfers between devices, on_device(): back_weights.append(lax.ppermute(theirs, 'type', to_end))  6.82 us
    ppermute x1, starting transfers between devices, on_device(): near = lax.ppermute(keys, 'type', to_middle)  4.93 us
    ppermute x1, waiting for transfers between devices, on_device(): guest = lax.ppermute(queries, 'type', to_middle)  3.88 us
    pallas_call x1, Pallas kernels, ffn(): pl.pallas_call(ffn_kernel, out_shape=[jax.ShapeDtypeStruct((half, width),...  3.58 us
    pallas_call x2, Pallas kernels, weigh_begin(): pl.pallas_call(functools.partial(in_middle, weigh_begin_body, n_type, til...  3.51 us
  transfers between devices with their start and end apart: 18, of which 11 were waited for; matrix products, arithmetic and copies ran while one was open for 0% of the time, Pallas kernels for 19%

profile of v7, /device:TPU:0, one launch (start us, length us, event | category | flops | bytes accessed | tf_op | source)
XLA Modules:
  0.0 94.4 jit_solution(8794479062885813764)
XLA Ops:
  0.6 1.7 %shard_map.98 = (bf16[16,4224]{1,0:T(8,128)(2,1)S(1)}, bf16[16,4224]{1,0:T(8,128)(2,1)S(1)}, bf16[16,4224]{1,0:T(8,128)(2,1)S(1)}, bf16[16,4224]{1,0:T(8,128)(2,1)S(1)}) custom-call(s32[1,128]{1,0:T(1,128)} %bitcast.8, s32[1,4]{1,0:T(1,128)} %bitcast.9, bf16[128,4096]{1,0:T(8,128)(2,1)} %tokens_ref.1), custom_call_target="tpu_custom_call" | custom-call | tf_op jit(solution)/shard_map/pallas_call | solution.py:87
  2.3 3.1 %collective-permute-start.8 = (bf16[16,4224]{1,0:T(8,128)(2,1)S(1)}, bf16[16,4224]{1,0:T(8,128)(2,1)S(1)}, u32[]{:S(2)}, u32[]{:S(2)}) collective-permute-start(bf16[16,4224]{1,0:T(8,128)(2,1)S(1)} %get-tuple-element.97), channel_id=1, source_target_pairs={{0,1},{1,0},{2,3},{3,2},{4,5},{5,4},{6,7},{7,6},{8,9},{9,8},{10,11... | collective-permute-start | bytes 405512 | tf_op jit(solution)/shard_map/ppermute | solution.py:482
  5.4 2.6 %collective-permute-start.9 = (bf16[16,4224]{1,0:T(8,128)(2,1)S(1)}, bf16[16,4224]{1,0:T(8,128)(2,1)S(1)}, u32[]{:S(2)}, u32[]{:S(2)}) collective-permute-start(bf16[16,4224]{1,0:T(8,128)(2,1)S(1)} %get-tuple-element.98), channel_id=1, source_target_pairs={{0,2},{1,3},{2,0},{3,1},{4,6},{5,7},{6,4},{7,5},{8,10},{9,11},{10,... | collective-permute-start | bytes 405512 | tf_op jit(solution)/shard_map/ppermute | solution.py:482
  8.0 0.0 collective-permute-start.10
  8.0 2.6 %collective-permute-done.8 = bf16[16,4224]{1,0:T(8,128)(2,1)S(1)} collective-permute-done((bf16[16,4224]{1,0:T(8,128)(2,1)S(1)}, bf16[16,4224]{1,0:T(8,128)(2,1)S(1)}, u32[]{:S(2)}, u32[]{:S(2)}) %collective-permute-start.8) | collective-permute-done | bytes 135200 | tf_op jit(solution)/shard_map/ppermute | solution.py:482
  10.7 8.0 %collective-permute-done.9 = bf16[16,4224]{1,0:T(8,128)(2,1)S(1)} collective-permute-done((bf16[16,4224]{1,0:T(8,128)(2,1)S(1)}, bf16[16,4224]{1,0:T(8,128)(2,1)S(1)}, u32[]{:S(2)}, u32[]{:S(2)}) %collective-permute-start.9) | collective-permute-done | bytes 135200 | tf_op jit(solution)/shard_map/ppermute | solution.py:482
  18.6 0.0 collective-permute-done.10
  18.6 4.9 %collective-permute-start.11 = (bf16[128,4096]{1,0:T(8,128)(2,1)}, bf16[128,4096]{1,0:T(8,128)(2,1)}, u32[]{:S(2)}, u32[]{:S(2)}) collective-permute-start(bf16[128,4096]{1,0:T(8,128)(2,1)} %args_2_), channel_id=1, source_target_pairs={{0,1},{3,2},{4,5},{7,6},{8,9},{11,10},{12,13},{15,14},{16,17},{19,... | collective-permute-start | bytes 3145736 | tf_op jit(solution)/shard_map/ppermute | solution.py:537
  23.6 1.6 %collective-permute-start.12 = (bf16[128,4096]{1,0:T(8,128)(2,1)}, bf16[128,4096]{1,0:T(8,128)(2,1)}, u32[]{:S(2)}, u32[]{:S(2)}) collective-permute-start(bf16[128,4096]{1,0:T(8,128)(2,1)} %args_2_), channel_id=1, source_target_pairs={{1,2},{2,1},{5,6},{6,5},{9,10},{10,9},{13,14},{14,13},{17,18},{18,... | collective-permute-start | bytes 3145736 | tf_op jit(solution)/shard_map/ppermute | solution.py:538
  25.2 2.2 %collective-permute-start.13 = (bf16[128,4096]{1,0:T(8,128)(2,1)}, bf16[128,4096]{1,0:T(8,128)(2,1)S(1)}, u32[]{:S(2)}, u32[]{:S(2)}) collective-permute-start(bf16[128,4096]{1,0:T(8,128)(2,1)} %args_3_), channel_id=1, source_target_pairs={{0,1},{3,2},{4,5},{7,6},{8,9},{11,10},{12,13},{15,14},{16,17},{19,... | collective-permute-start | bytes 3145736 | tf_op jit(solution)/shard_map/ppermute | solution.py:539
  27.4 0.0 copy-start
  27.4 19.9 %conditional.2 = (f32[12,128]{1,0:T(8,128)S(1)}, f32[64,4096]{1,0:T(8,128)S(1)}, bf16[64,4096]{1,0:T(8,128)(2,1)S(1)}) conditional(s32[]{:T(128)} %convert_element_type.25, () %tuple.32, (bf16[16,4224]{1,0:T(8,128)(2,1)S(1)}, bf16[16,4224]{1,0:T(8,128)(2,1)S(1)}, bf16[16,4224]{1,0:T(8,128)(2,1)S(1)}, bf16[16,4224]{1,0:T(8,128)(2,1)S(1)}, ...), branch_computations={%region_0.0_spmd, %region_1.0_spmd} | conditional | bytes 48758968 | solution.py:488
  27.5 0.4 branch_1_fun.4
  27.9 1.6 %collective-permute-start.1 = (bf16[16,4096]{1,0:T(8,128)(2,1)S(1)}, bf16[16,4096]{1,0:T(8,128)(2,1)S(1)}, u32[]{:S(2)}, u32[]{:S(2)}) collective-permute-start(bf16[16,4096]{1,0:T(8,128)(2,1)S(1)} %get-tuple-element.43), channel_id=1, source_target_pairs={{0,16},{4,20},{8,24},{12,28},{16,0},{20,4},{24,8},{28,12},{1,17},{... | collective-permute-start | bytes 393224 | tf_op jit(solution)/shard_map/cond/branch_1_fun/ppermute | solution.py:482
  29.4 1.5 %collective-permute-start = (bf16[16,4096]{1,0:T(8,128)(2,1)S(1)}, bf16[16,4096]{1,0:T(8,128)(2,1)S(1)}, u32[]{:S(2)}, u32[]{:S(2)}) collective-permute-start(bf16[16,4096]{1,0:T(8,128)(2,1)S(1)} %get-tuple-element.43), channel_id=1, source_target_pairs={{0,8},{4,12},{8,0},{12,4},{16,24},{20,28},{24,16},{28,20},{1,9},{5... | collective-permute-start | bytes 393224 | tf_op jit(solution)/shard_map/cond/branch_1_fun/ppermute | solution.py:482
  30.9 2.0 %collective-permute-done.1 = bf16[16,4096]{1,0:T(8,128)(2,1)S(1)} collective-permute-done((bf16[16,4096]{1,0:T(8,128)(2,1)S(1)}, bf16[16,4096]{1,0:T(8,128)(2,1)S(1)}, u32[]{:S(2)}, u32[]{:S(2)}) %collective-permute-start.1) | collective-permute-done | bytes 131104 | tf_op jit(solution)/shard_map/cond/branch_1_fun/ppermute | solution.py:482
  32.9 1.5 %collective-permute-start.2 = (bf16[16,4096]{1,0:T(8,128)(2,1)S(1)}, bf16[16,4096]{1,0:T(8,128)(2,1)S(1)}, u32[]{:S(2)}, u32[]{:S(2)}) collective-permute-start(bf16[16,4096]{1,0:T(8,128)(2,1)S(1)} %collective-permute-done.1), channel_id=1, source_target_pairs={{0,8},{4,12},{8,0},{12,4},{16,24},{20,28},{24,16},{28,20},{1,9},{5... | collective-permute-start | bytes 393224 | tf_op jit(solution)/shard_map/cond/branch_1_fun/ppermute | solution.py:482
  34.4 7.3 %branch_1_fun.5 = (bf16[4096,896]{1,0:T(8,128)(2,1)S(1)}, bf16[4096,896]{1,0:T(8,128)(2,1)S(1)}, bf16[896,4096]{1,0:T(8,128)(2,1)S(1)}) custom-call(bf16[4096,896]{1,0:T(8,128)(2,1)} %bitcast.5, bf16[4096,896]{1,0:T(8,128)(2,1)} %bitcast.6, bf16[896,4096]{1,0:T(8,128)(2,1)} %bitcast.7), custom_call_target="tpu_custom_call" | custom-call | bytes 44040192 | tf_op jit(solution)/shard_map/cond/branch_1_fun/pallas_call | solution.py:114
  41.7 0.0 collective-permute-done
  41.7 0.0 collective-permute-done.2
  41.8 0.1 collective-permute-start.3
  41.9 1.9 %collective-permute-done.3.far_ref = bf16[64,4096]{1,0:T(8,128)(2,1)S(1)} collective-permute-done((bf16[64,4096]{1,0:T(8,128)(2,1)S(1)}, bf16[64,4096]{1,0:T(8,128)(2,1)S(1)}, u32[]{:S(2)}, u32[]{:S(2)}) %collective-permute-start.3) | collective-permute-done | bytes 524320 | tf_op jit(solution)/shard_map/cond/branch_1_fun/ppermute | solution.py:482
  43.8 3.6 %branch_1_fun.6 = (f32[64,4096]{1,0:T(8,128)S(1)}, bf16[64,4096]{1,0:T(8,128)(2,1)S(1)}) custom-call(bf16[64,4096]{1,0:T(8,128)(2,1)S(1)} %constant_dynamic-update-slice_fusion.near_ref, bf16[64,4096]{1,0:T(8,128)(2,1)S(1)} %collective-permute-done.3.far_ref, bf16[4096,896]{1,0:T(8,128)(2,1)S(1)} %get-tuple-element.47.gate_ref, ...), custom_call_target="tpu_custom_call" | custom-call | tf_op jit(solution)/shard_map/cond/branch_1_fun/pallas_call | solution.py:216
  47.4 0.7 collective-permute-start.15
  48.1 11.6 %conditional.3 = (bf16[16,4096]{1,0:T(8,128)(2,1)S(1)}, f32[32,16,128]{2,1,0:T(8,128)S(1)}, bf16[64,4096]{1,0:T(8,128)(2,1)S(1)}) conditional(s32[]{:T(128)} %convert_element_type.25, () %tuple.31, (bf16[64,4096]{1,0:T(8,128)(2,1)S(1)}, f32[64,4096]{1,0:T(8,128)S(1)}, f32[12,128]{1,0:T(8,128)S(1)}, bf16[128,4096]{1,0:T(8,128)(2,1)}, ...), branch_computations={%region_2.0_spmd, %region_3.0_spmd} | conditional | flops 1310720 | bytes 15859896 | solution.py:488
  48.1 0.2 collective-permute-start.4
  48.3 1.8 %collective-permute-done.4 = bf16[64,4096]{1,0:T(8,128)(2,1)S(1)} collective-permute-done((bf16[64,4096]{1,0:T(8,128)(2,1)S(1)}, bf16[64,4096]{1,0:T(8,128)(2,1)S(1)}, u32[]{:S(2)}, u32[]{:S(2)}) %collective-permute-start.4) | collective-permute-done | bytes 524320 | tf_op jit(solution)/shard_map/cond/branch_1_fun/ppermute | solution.py:482
  50.1 0.1 add_convert_fusion
  50.2 1.6 %collective-permute-start.7 = (bf16[16,4096]{1,0:T(8,128)(2,1)S(1)}, bf16[16,4096]{1,0:T(8,128)(2,1)S(1)}, u32[]{:S(2)}, u32[]{:S(2)}) collective-permute-start(bf16[16,4096]{1,0:T(8,128)(2,1)S(1)} %get-tuple-element.129), channel_id=1, source_target_pairs={{0,24},{4,28},{8,16},{12,20},{16,8},{20,12},{24,0},{28,4},{1,25},{... | collective-permute-start | bytes 393224 | tf_op jit(solution)/shard_map/cond/branch_1_fun/ppermute | solution.py:482
  51.9 0.5 collective-permute-start.6
  52.4 1.4 %collective-permute-start.5 = (bf16[16,4096]{1,0:T(8,128)(2,1)S(1)}, bf16[16,4096]{1,0:T(8,128)(2,1)S(1)}, u32[]{:S(2)}, u32[]{:S(2)}) collective-permute-start(bf16[16,4096]{1,0:T(8,128)(2,1)S(1)} %get-tuple-element.131), channel_id=1, source_target_pairs={{0,8},{4,12},{8,0},{12,4},{16,24},{20,28},{24,16},{28,20},{1,9},{5... | collective-permute-start | bytes 393224 | tf_op jit(solution)/shard_map/cond/branch_1_fun/ppermute | solution.py:482
  53.8 1.9 %branch_1_fun.7 = (f32[32,16,128]{2,1,0:T(8,128)S(1)}, bf16[64,4096]{1,0:T(8,128)(2,1)S(1)}) custom-call(f32[12,128]{1,0:T(8,128)S(1)} %get-tuple-element.54.args_0_, bf16[128,4096]{1,0:T(8,128)(2,1)} %get-tuple-element.55.args_1_, bf16[128,4096]{1,0:T(8,128)(2,1)S(1)} %get-tuple-element.56.args_2_, bf16[128,4096]{1,0:T(8,128)(2,1)} %get-tuple-element.57.args_3_, ...), custom_call_target="tpu_custom_call" | custom-call | bytes 8388608 | tf_op jit(solution)/shard_map/cond/branch_1_fun/pallas_call | solution.py:322
  55.7 1.9 %collective-permute-done.7 = bf16[16,4096]{1,0:T(8,128)(2,1)S(1)} collective-permute-done((bf16[16,4096]{1,0:T(8,128)(2,1)S(1)}, bf16[16,4096]{1,0:T(8,128)(2,1)S(1)}, u32[]{:S(2)}, u32[]{:S(2)}) %collective-permute-start.7) | collective-permute-done | bytes 131104 | tf_op jit(solution)/shard_map/cond/branch_1_fun/ppermute | solution.py:482
  57.6 2.0 %collective-permute-done.6 = bf16[16,4096]{1,0:T(8,128)(2,1)S(1)} collective-permute-done((bf16[16,4096]{1,0:T(8,128)(2,1)S(1)}, bf16[16,4096]{1,0:T(8,128)(2,1)S(1)}, u32[]{:S(2)}, u32[]{:S(2)}) %collective-permute-start.6) | collective-permute-done | bytes 131104 | tf_op jit(solution)/shard_map/cond/branch_1_fun/ppermute | solution.py:482
  59.5 0.1 collective-permute-done.5
  59.7 0.1 add_convert_fusion.1
  59.7 0.0 copy-start.1
  59.7 4.4 %collective-permute-start.14 = (bf16[16,4096]{1,0:T(8,128)(2,1)S(1)}, bf16[16,4096]{1,0:T(8,128)(2,1)S(1)}, u32[]{:S(2)}, u32[]{:S(2)}) collective-permute-start(bf16[16,4096]{1,0:T(8,128)(2,1)S(1)} %get-tuple-element.112), channel_id=1, source_target_pairs={{0,1},{1,0},{2,3},{3,2},{4,5},{5,4},{6,7},{7,6},{8,9},{9,8},{10,11... | collective-permute-start | bytes 393224 | tf_op jit(solution)/shard_map/ppermute | solution.py:482
  64.1 3.9 %collective-permute-done.13.args_1_.args_4_ = bf16[128,4096]{1,0:T(8,128)(2,1)S(1)} collective-permute-done((bf16[128,4096]{1,0:T(8,128)(2,1)}, bf16[128,4096]{1,0:T(8,128)(2,1)S(1)}, u32[]{:S(2)}, u32[]{:S(2)}) %collective-permute-start.13) | collective-permute-done | bytes 1048608 | tf_op jit(solution)/shard_map/ppermute | solution.py:539
  68.0 1.6 %shard_map.99.args_6_ = f32[32,16,128]{2,1,0:T(8,128)S(1)} custom-call(f32[12,128]{1,0:T(8,128)S(1)} %get-tuple-element.108.args_0_.info_ref, bf16[128,4096]{1,0:T(8,128)(2,1)S(1)} %collective-permute-done.13.args_1_.args_4_, bf16[128,4096]{1,0:T(8,128)(2,1)S(1)} %copy-done, bf16[128,4096]{1,0:T(8,128)(2,1)} %collective-permute-done.11.args_3_, ...), custom_call_target="tpu_custom_call" | custom-call | bytes 8388608 | tf_op jit(solution)/shard_map/pallas_call | solution.py:322
  69.7 0.0 collective-permute-done.14
  69.7 5.6 %collective-permute-start.16 = (bf16[32,4096]{1,0:T(8,128)(2,1)S(1)}, bf16[32,4096]{1,0:T(8,128)(2,1)S(1)}, u32[]{:S(2)}, u32[]{:S(2)}) collective-permute-start(bf16[32,4096]{1,0:T(8,128)(2,1)S(1)} %pad_maximum_fusion), channel_id=1, source_target_pairs={{0,2},{1,3},{2,0},{3,1},{4,6},{5,7},{6,4},{7,5},{8,10},{9,11},{10,... | collective-permute-start | bytes 786440 | tf_op jit(solution)/shard_map/ppermute | solution.py:482
  75.3 1.4 %shard_map.101 = (bf16[32,64,128]{2,1,0:T(8,128)(2,1)S(1)}, bf16[32,64,128]{2,1,0:T(8,128)(2,1)S(1)}) custom-call(f32[12,128]{1,0:T(8,128)S(1)} %get-tuple-element.108.args_0_.info_ref, bf16[64,4096]{1,0:T(8,128)(2,1)} %copy-done.1, bf16[128,4096]{1,0:T(8,128)(2,1)S(1)} %collective-permute-done.15.args_2_, bf16[128,4096]{1,0:T(8,128)(2,1)} %args_3_, ...), custom_call_target="tpu_custom_call" | custom-call | tf_op jit(solution)/shard_map/pallas_call | solution.py:387
  76.7 1.3 %collective-permute-start.17 = (bf16[32,64,128]{2,1,0:T(8,128)(2,1)S(1)}, bf16[32,64,128]{2,1,0:T(8,128)(2,1)S(1)}, u32[]{:S(2)}, u32[]{:S(2)}) collective-permute-start(bf16[32,64,128]{2,1,0:T(8,128)(2,1)S(1)} %get-tuple-element.122), channel_id=1, source_target_pairs={{1,0},{2,3},{5,4},{6,7},{9,8},{10,11},{13,12},{14,15},{17,16},{18,... | collective-permute-start | bytes 1572872 | tf_op jit(solution)/shard_map/ppermute | solution.py:568
  78.0 6.8 %collective-permute-done.16 = bf16[32,4096]{1,0:T(8,128)(2,1)S(1)} collective-permute-done((bf16[32,4096]{1,0:T(8,128)(2,1)S(1)}, bf16[32,4096]{1,0:T(8,128)(2,1)S(1)}, u32[]{:S(2)}, u32[]{:S(2)}) %collective-permute-start.16) | collective-permute-done | bytes 262176 | tf_op jit(solution)/shard_map/ppermute | solution.py:482
  84.8 1.4 %shard_map.100 = bf16[128,4096]{1,0:T(8,128)(2,1)} custom-call(f32[12,128]{1,0:T(8,128)S(1)} %get-tuple-element.108.args_0_.info_ref, bf16[64,4096]{1,0:T(8,128)(2,1)S(1)} %constant_dynamic-update-slice_fusion.4.values_ref), custom_call_target="tpu_custom_call" | custom-call | tf_op jit(solution)/shard_map/pallas_call | solution.py:425
  86.3 6.8 %collective-permute-done.17.refs_1_ = bf16[32,64,128]{2,1,0:T(8,128)(2,1)S(1)} collective-permute-done((bf16[32,64,128]{2,1,0:T(8,128)(2,1)S(1)}, bf16[32,64,128]{2,1,0:T(8,128)(2,1)S(1)}, u32[]{:S(2)}, u32[]{:S(2)}) %collective-permute-start.17) | collective-permute-done | bytes 524320 | tf_op jit(solution)/shard_map/ppermute | solution.py:568
  93.1 1.3 %shard_map.102 = bf16[128,4096]{1,0:T(8,128)(2,1)} custom-call(bf16[64,4096]{1,0:T(8,128)(2,1)S(1)} %constant_dynamic-update-slice_fusion.4.values_ref, bf16[32,64,128]{2,1,0:T(8,128)(2,1)S(1)} %get-tuple-element.121.refs_0_, bf16[32,64,128]{2,1,0:T(8,128)(2,1)S(1)} %collective-permute-done.17.refs_1_), custom_call_target="tpu_custom_call" | custom-call | tf_op jit(solution)/shard_map/pallas_call | solution.py:466
  (14 shorter events, 0.1 us)
Async XLA Ops:
  2.3 8.3 %collective-permute-start.8 = (bf16[16,4224]{1,0:T(8,128)(2,1)S(1)}, bf16[16,4224]{1,0:T(8,128)(2,1)S(1)}, u32[]{:S(2)}, u32[]{:S(2)}) collective-permute-start(bf16[16,4224]{1,0:T(8,128)(2,1)S(1)} %get-tuple-element.97), channel_id=1, source_target_pairs={{0,1},{1,0},{2,3},{3,2},{4,5},{5,4},{6,7},{7,6},{8,9},{9,8},{10,11... | collective-permute-start | bytes 405512 | tf_op jit(solution)/shard_map/ppermute | solution.py:482
  5.4 13.2 %collective-permute-start.9 = (bf16[16,4224]{1,0:T(8,128)(2,1)S(1)}, bf16[16,4224]{1,0:T(8,128)(2,1)S(1)}, u32[]{:S(2)}, u32[]{:S(2)}) collective-permute-start(bf16[16,4224]{1,0:T(8,128)(2,1)S(1)} %get-tuple-element.98), channel_id=1, source_target_pairs={{0,2},{1,3},{2,0},{3,1},{4,6},{5,7},{6,4},{7,5},{8,10},{9,11},{10,... | collective-permute-start | bytes 405512 | tf_op jit(solution)/shard_map/ppermute | solution.py:482
  8.0 10.6 %collective-permute-start.10 = (bf16[16,4224]{1,0:T(8,128)(2,1)S(1)}, bf16[16,4224]{1,0:T(8,128)(2,1)S(1)}, u32[]{:S(2)}, u32[]{:S(2)}) collective-permute-start(bf16[16,4224]{1,0:T(8,128)(2,1)S(1)} %get-tuple-element.99), channel_id=1, source_target_pairs={{0,3},{1,2},{2,1},{3,0},{4,7},{5,6},{6,5},{7,4},{8,11},{9,10},{10,... | collective-permute-start | bytes 405512 | tf_op jit(solution)/shard_map/ppermute | solution.py:482
  18.6 28.7 %collective-permute-start.11 = (bf16[128,4096]{1,0:T(8,128)(2,1)}, bf16[128,4096]{1,0:T(8,128)(2,1)}, u32[]{:S(2)}, u32[]{:S(2)}) collective-permute-start(bf16[128,4096]{1,0:T(8,128)(2,1)} %args_2_), channel_id=1, source_target_pairs={{0,1},{3,2},{4,5},{7,6},{8,9},{11,10},{12,13},{15,14},{16,17},{19,... | collective-permute-start | bytes 3145736 | tf_op jit(solution)/shard_map/ppermute | solution.py:537
  23.6 24.5 %collective-permute-start.12 = (bf16[128,4096]{1,0:T(8,128)(2,1)}, bf16[128,4096]{1,0:T(8,128)(2,1)}, u32[]{:S(2)}, u32[]{:S(2)}) collective-permute-start(bf16[128,4096]{1,0:T(8,128)(2,1)} %args_2_), channel_id=1, source_target_pairs={{1,2},{2,1},{5,6},{6,5},{9,10},{10,9},{13,14},{14,13},{17,18},{18,... | collective-permute-start | bytes 3145736 | tf_op jit(solution)/shard_map/ppermute | solution.py:538
  25.2 42.8 %collective-permute-start.13 = (bf16[128,4096]{1,0:T(8,128)(2,1)}, bf16[128,4096]{1,0:T(8,128)(2,1)S(1)}, u32[]{:S(2)}, u32[]{:S(2)}) collective-permute-start(bf16[128,4096]{1,0:T(8,128)(2,1)} %args_3_), channel_id=1, source_target_pairs={{0,1},{3,2},{4,5},{7,6},{8,9},{11,10},{12,13},{15,14},{16,17},{19,... | collective-permute-start | bytes 3145736 | tf_op jit(solution)/shard_map/ppermute | solution.py:539
  27.4 20.7 %copy-start = (bf16[128,4096]{1,0:T(8,128)(2,1)S(1)}, bf16[128,4096]{1,0:T(8,128)(2,1)}, u32[]{:S(2)}) copy-start(bf16[128,4096]{1,0:T(8,128)(2,1)} %args_2_) | copy-start | bytes 3145732
  27.9 5.0 %collective-permute-start.1 = (bf16[16,4096]{1,0:T(8,128)(2,1)S(1)}, bf16[16,4096]{1,0:T(8,128)(2,1)S(1)}, u32[]{:S(2)}, u32[]{:S(2)}) collective-permute-start(bf16[16,4096]{1,0:T(8,128)(2,1)S(1)} %get-tuple-element.43), channel_id=1, source_target_pairs={{0,16},{4,20},{8,24},{12,28},{16,0},{20,4},{24,8},{28,12},{1,17},{... | collective-permute-start | bytes 393224 | tf_op jit(solution)/shard_map/cond/branch_1_fun/ppermute | solution.py:482
  29.4 12.2 %collective-permute-start = (bf16[16,4096]{1,0:T(8,128)(2,1)S(1)}, bf16[16,4096]{1,0:T(8,128)(2,1)S(1)}, u32[]{:S(2)}, u32[]{:S(2)}) collective-permute-start(bf16[16,4096]{1,0:T(8,128)(2,1)S(1)} %get-tuple-element.43), channel_id=1, source_target_pairs={{0,8},{4,12},{8,0},{12,4},{16,24},{20,28},{24,16},{28,20},{1,9},{5... | collective-permute-start | bytes 393224 | tf_op jit(solution)/shard_map/cond/branch_1_fun/ppermute | solution.py:482
  32.9 8.8 %collective-permute-start.2 = (bf16[16,4096]{1,0:T(8,128)(2,1)S(1)}, bf16[16,4096]{1,0:T(8,128)(2,1)S(1)}, u32[]{:S(2)}, u32[]{:S(2)}) collective-permute-start(bf16[16,4096]{1,0:T(8,128)(2,1)S(1)} %collective-permute-done.1), channel_id=1, source_target_pairs={{0,8},{4,12},{8,0},{12,4},{16,24},{20,28},{24,16},{28,20},{1,9},{5... | collective-permute-start | bytes 393224 | tf_op jit(solution)/shard_map/cond/branch_1_fun/ppermute | solution.py:482
  41.8 2.0 %collective-permute-start.3 = (bf16[64,4096]{1,0:T(8,128)(2,1)S(1)}, bf16[64,4096]{1,0:T(8,128)(2,1)S(1)}, u32[]{:S(2)}, u32[]{:S(2)}) collective-permute-start(bf16[64,4096]{1,0:T(8,128)(2,1)S(1)} %constant_dynamic-update-slice_fusion.near_ref), channel_id=1, source_target_pairs={{0,4},{4,0},{8,12},{12,8},{16,20},{20,16},{24,28},{28,24},{1,5},{5... | collective-permute-start | bytes 1572872 | tf_op jit(solution)/shard_map/cond/branch_1_fun/ppermute | solution.py:482
  47.4 22.3 %collective-permute-start.15 = (bf16[128,4096]{1,0:T(8,128)(2,1)}, bf16[128,4096]{1,0:T(8,128)(2,1)S(1)}, u32[]{:S(2)}, u32[]{:S(2)}) collective-permute-start(bf16[128,4096]{1,0:T(8,128)(2,1)} %collective-permute-done.11.args_3_), channel_id=1, source_target_pairs={{1,2},{2,1},{5,6},{6,5},{9,10},{10,9},{13,14},{14,13},{17,18},{18,... | collective-permute-start | bytes 3145736 | tf_op jit(solution)/shard_map/ppermute | solution.py:542
  48.1 2.0 %collective-permute-start.4 = (bf16[64,4096]{1,0:T(8,128)(2,1)S(1)}, bf16[64,4096]{1,0:T(8,128)(2,1)S(1)}, u32[]{:S(2)}, u32[]{:S(2)}) collective-permute-start(bf16[64,4096]{1,0:T(8,128)(2,1)S(1)} %get-tuple-element.53), channel_id=1, source_target_pairs={{0,4},{4,0},{8,12},{12,8},{16,20},{20,16},{24,28},{28,24},{1,5},{5... | collective-permute-start | bytes 1572872 | tf_op jit(solution)/shard_map/cond/branch_1_fun/ppermute | solution.py:482
  50.2 7.3 %collective-permute-start.7 = (bf16[16,4096]{1,0:T(8,128)(2,1)S(1)}, bf16[16,4096]{1,0:T(8,128)(2,1)S(1)}, u32[]{:S(2)}, u32[]{:S(2)}) collective-permute-start(bf16[16,4096]{1,0:T(8,128)(2,1)S(1)} %get-tuple-element.129), channel_id=1, source_target_pairs={{0,24},{4,28},{8,16},{12,20},{16,8},{20,12},{24,0},{28,4},{1,25},{... | collective-permute-start | bytes 393224 | tf_op jit(solution)/shard_map/cond/branch_1_fun/ppermute | solution.py:482
  51.9 7.7 %collective-permute-start.6 = (bf16[16,4096]{1,0:T(8,128)(2,1)S(1)}, bf16[16,4096]{1,0:T(8,128)(2,1)S(1)}, u32[]{:S(2)}, u32[]{:S(2)}) collective-permute-start(bf16[16,4096]{1,0:T(8,128)(2,1)S(1)} %get-tuple-element.130), channel_id=1, source_target_pairs={{0,16},{4,20},{8,24},{12,28},{16,0},{20,4},{24,8},{28,12},{1,17},{... | collective-permute-start | bytes 393224 | tf_op jit(solution)/shard_map/cond/branch_1_fun/ppermute | solution.py:482
  52.4 7.3 %collective-permute-start.5 = (bf16[16,4096]{1,0:T(8,128)(2,1)S(1)}, bf16[16,4096]{1,0:T(8,128)(2,1)S(1)}, u32[]{:S(2)}, u32[]{:S(2)}) collective-permute-start(bf16[16,4096]{1,0:T(8,128)(2,1)S(1)} %get-tuple-element.131), channel_id=1, source_target_pairs={{0,8},{4,12},{8,0},{12,4},{16,24},{20,28},{24,16},{28,20},{1,9},{5... | collective-permute-start | bytes 393224 | tf_op jit(solution)/shard_map/cond/branch_1_fun/ppermute | solution.py:482
  59.7 4.4 %copy-start.1 = (bf16[64,4096]{1,0:T(8,128)(2,1)}, bf16[64,4096]{1,0:T(8,128)(2,1)S(1)}, u32[]{:S(2)}) copy-start(bf16[64,4096]{1,0:T(8,128)(2,1)S(1)} %get-tuple-element.117.args_1_) | copy-start | bytes 1572868
  59.7 9.9 %collective-permute-start.14 = (bf16[16,4096]{1,0:T(8,128)(2,1)S(1)}, bf16[16,4096]{1,0:T(8,128)(2,1)S(1)}, u32[]{:S(2)}, u32[]{:S(2)}) collective-permute-start(bf16[16,4096]{1,0:T(8,128)(2,1)S(1)} %get-tuple-element.112), channel_id=1, source_target_pairs={{0,1},{1,0},{2,3},{3,2},{4,5},{5,4},{6,7},{7,6},{8,9},{9,8},{10,11... | collective-permute-start | bytes 393224 | tf_op jit(solution)/shard_map/ppermute | solution.py:482
  69.7 15.1 %collective-permute-start.16 = (bf16[32,4096]{1,0:T(8,128)(2,1)S(1)}, bf16[32,4096]{1,0:T(8,128)(2,1)S(1)}, u32[]{:S(2)}, u32[]{:S(2)}) collective-permute-start(bf16[32,4096]{1,0:T(8,128)(2,1)S(1)} %pad_maximum_fusion), channel_id=1, source_target_pairs={{0,2},{1,3},{2,0},{3,1},{4,6},{5,7},{6,4},{7,5},{8,10},{9,11},{10,... | collective-permute-start | bytes 786440 | tf_op jit(solution)/shard_map/ppermute | solution.py:482
  76.7 16.4 %collective-permute-start.17 = (bf16[32,64,128]{2,1,0:T(8,128)(2,1)S(1)}, bf16[32,64,128]{2,1,0:T(8,128)(2,1)S(1)}, u32[]{:S(2)}, u32[]{:S(2)}) collective-permute-start(bf16[32,64,128]{2,1,0:T(8,128)(2,1)S(1)} %get-tuple-element.122), channel_id=1, source_target_pairs={{1,0},{2,3},{5,4},{6,7},{9,8},{10,11},{13,12},{14,15},{17,16},{18,... | collective-permute-start | bytes 1572872 | tf_op jit(solution)/shard_map/ppermute | solution.py:568
